TPU v7x, 128 devices: a whole 4x4x4 slice. The times are simulated.
128 devices in a mesh: dp: 4 (over y_hi, core), sp: 32 (over z, x, y_lo).
Axes of the slice: x: 4, y: 4 (y_hi: 2, y_lo: 2; y = y_hi * 2 + y_lo), z: 4, core: 2. Of those that a mesh axis runs over, the one named last changes fastest.
Arguments:
- x_long: bfloat16 [16384, 1024], P(('dp', 'sp')), may hold values from -24 to 24
- x_short: bfloat16 [131072, 1024], P(('dp', 'sp')), may hold values from -24 to 24
- long_blocks: int32 [4], replicated, may hold values from 4 to 8, as said below
- short_user: int32 [128, 2], P(('dp', 'sp')), may hold values from 0 to 1, as said below
- proj_in: bfloat16 [1024, 1536], replicated, may hold values from -0.1875 to 0.1875
- proj_out: bfloat16 [512, 1024], replicated, may hold values from -0.25 to 0.25
- cot_long: bfloat16 [16384, 1024], P(('dp', 'sp')), may hold values from -24 to 24
- cot_short: bfloat16 [131072, 1024], P(('dp', 'sp')), may hold values from -24 to 24
Outputs:
- out_long: bfloat16 [16384, 1024], P(('dp', 'sp'))
- out_short: bfloat16 [131072, 1024], P(('dp', 'sp'))
- back_long: bfloat16 [16384, 1024], P(('dp', 'sp'))
- back_short: bfloat16 [131072, 1024], P(('dp', 'sp'))
- grad_in: float32 [1024, 1536], P(('dp', 'sp'))
- grad_out_t: float32 [1024, 512], P(('dp', 'sp'))
Inputs may be any that keep to these rules, and one draw needn't show every extreme that they name: Rows past long_blocks[g] * 512 of a long history are padding; some group's history fills all its blocks. `short_user`: along a device's blocks the user numbers start at 0 and never fall; each user covers one or two whole blocks, and the blocks of one user lie in one aligned pair (blocks 2p and 2p + 1); on some device every user covers one block, and on some device a user covers two.
All inputs are finite; a program needn't handle non-finite values.
Results may differ from a plain program's by a relative error of at most 0.013.
Values may be sent and summed in bfloat16 or wider, within the bound.
No kernel may reach another device: no remote copies, remote signals or barrier semaphores. Data moves between devices by JAX's collectives and lax.ppermute only.
A program may use at most 192 MiB of HBM per device.

v0:
```python
import jax
import jax.numpy as jnp
from jax import lax
from jax.sharding import PartitionSpec as P

H = 4
BLOCK = 512


EPS = 1e-05


def silu_slope(inputs):
    sigma = jax.nn.sigmoid(inputs)
    return sigma * (1.0 + inputs * (1.0 - sigma))


def norm_rows(inputs):
    center = inputs - jnp.mean(inputs, axis=-1, keepdims=True)
    inv_root = lax.rsqrt(jnp.mean(center * center, axis=-1, keepdims=True) + EPS)
    return (center * inv_root, inv_root)


def norm_back(upstream, normed, inv_root):
    return inv_root * (
        upstream
        - jnp.mean(upstream, axis=-1, keepdims=True)
        - normed * jnp.mean(upstream * normed, axis=-1, keepdims=True)
    )


def contract(first_op, second_op, contract_dims):
    return lax.dot_general(
        first_op, second_op, (contract_dims, ((), ())), preferred_element_type=jnp.float32
    )


def attend(queries, keys_vals, coeffs):
    key_width = queries.shape[1] // H
    val_width = (keys_vals.shape[1] - queries.shape[1]) // H
    keys_end = queries.shape[1]
    pieces = []
    for which_head in range(H):
        head_q = queries[:, which_head * key_width : (which_head + 1) * key_width]
        head_k = keys_vals[:, which_head * key_width : (which_head + 1) * key_width]
        head_v = keys_vals[
            :, keys_end + which_head * val_width : keys_end + (which_head + 1) * val_width
        ]
        scores = contract(head_q, head_k, ((1,), (1,))) * key_width ** (-0.5)
        weights = (jax.nn.silu(scores) * coeffs).astype(jnp.bfloat16)
        pieces.append(contract(weights, head_v, ((1,), (0,))))
    return jnp.concatenate(pieces, axis=1)


def attend_back(queries, keys_vals, grad_mixed, coeffs, want_query, want_keys):
    key_width = queries.shape[1] // H
    val_width = (keys_vals.shape[1] - queries.shape[1]) // H
    keys_end = queries.shape[1]
    root_scale = key_width ** (-0.5)
    query_parts = []
    key_parts = []
    value_parts = []
    for which_head in range(H):
        head_q = queries[:, which_head * key_width : (which_head + 1) * key_width]
        head_k = keys_vals[:, which_head * key_width : (which_head + 1) * key_width]
        head_v = keys_vals[
            :, keys_end + which_head * val_width : keys_end + (which_head + 1) * val_width
        ]
        head_g = grad_mixed[:, which_head * val_width : (which_head + 1) * val_width]
        scores = contract(head_q, head_k, ((1,), (1,))) * root_scale
        grad_w = contract(head_g, head_v, ((1,), (1,)))
        slopes = (grad_w * coeffs * silu_slope(scores)).astype(jnp.bfloat16)
        if want_query:
            query_parts.append(contract(slopes, head_k, ((1,), (0,))) * root_scale)
        if want_keys:
            weights = (jax.nn.silu(scores) * coeffs).astype(jnp.bfloat16)
            key_parts.append(contract(slopes, head_q, ((0,), (0,))) * root_scale)
            value_parts.append(contract(weights, head_g, ((0,), (0,))))
    grad_q = jnp.concatenate(query_parts, axis=1) if want_query else None
    grad_kv = jnp.concatenate(key_parts + value_parts, axis=1) if want_keys else None
    return (grad_q, grad_kv)


def head_out(x_rows, cotangent, proj_out, gate_u, mixed_out):
    mixed_n, inv_mix = norm_rows(mixed_out)
    gate_f = gate_u.astype(jnp.float32)
    gated_bf = (mixed_n * gate_f).astype(jnp.bfloat16)
    output = (x_rows.astype(jnp.float32) + contract(gated_bf, proj_out, ((1,), (0,)))).astype(
        jnp.bfloat16
    )
    grad_g = contract(cotangent, proj_out, ((1,), (1,)))
    grad_mixed = norm_back(grad_g * gate_f, mixed_n, inv_mix).astype(jnp.bfloat16)
    return (output, gated_bf, grad_g * mixed_n, grad_mixed)


def input_back(cotangent, proj_in, normed, inv_std, pre_act, grad_act):
    grad_pre = (grad_act * silu_slope(pre_act)).astype(jnp.bfloat16)
    grad_norm = contract(grad_pre, proj_in, ((1,), (1,)))
    back_rows = (cotangent.astype(jnp.float32) + norm_back(grad_norm, normed, inv_std)).astype(
        jnp.bfloat16
    )
    return (grad_pre, back_rows)


def long_coeffs(query_pos, key_pos, valid_rows):
    inside = (key_pos[None, :] <= query_pos[:, None]) & (query_pos[:, None] < valid_rows)
    return inside.astype(jnp.float32) / valid_rows.astype(jnp.float32)


def short_coeffs(user_ids):
    block_count = jnp.sum((user_ids[:, None] == user_ids[None, :]).astype(jnp.int32), axis=1)
    row_user = jnp.repeat(user_ids, BLOCK)
    row_len = jnp.repeat(block_count * BLOCK, BLOCK)
    row_ids = jnp.arange(row_user.shape[0], dtype=jnp.int32)
    inside = (row_user[:, None] == row_user[None, :]) & (row_ids[None, :] <= row_ids[:, None])
    return inside.astype(jnp.float32) / row_len[:, None].astype(jnp.float32)


def project_rows(x_rows, proj_in, value_cols, query_cols):
    normed, inv_std = norm_rows(x_rows.astype(jnp.float32))
    x_bf = normed.astype(jnp.bfloat16)
    pre_act = contract(x_bf, proj_in, ((1,), (0,)))
    activated = jax.nn.silu(pre_act).astype(jnp.bfloat16)
    gate_u = activated[:, :value_cols]
    queries = activated[:, value_cols : value_cols + query_cols]
    keys_vals = activated[:, value_cols + query_cols :]
    return (normed, inv_std, x_bf, pre_act, gate_u, queries, keys_vals)


def body(x_long, x_short, long_blocks, short_user, proj_in, proj_out, cot_long, cot_short):
    sp_size = lax.axis_size("sp")
    sp_index = lax.axis_index("sp")
    group_idx = lax.axis_index("dp")
    long_rows = x_long.shape[0]
    value_cols = proj_out.shape[0]
    query_cols = (proj_in.shape[1] - 2 * value_cols) // 2
    short_parts = project_rows(x_short, proj_in, value_cols, query_cols)
    short_normed, short_inv, short_bf, short_pre, short_gate, short_q, short_kv = short_parts
    packed_coeffs = short_coeffs(short_user[0])
    short_mixed = attend(short_q, short_kv, packed_coeffs)
    out_short, gated_short, short_grad_gate, short_grad_mixed = head_out(
        x_short, cot_short, proj_out, short_gate, short_mixed
    )
    short_grad_q, short_grad_kv = attend_back(
        short_q, short_kv, short_grad_mixed, packed_coeffs, True, True
    )
    grad_pre_short, back_short = input_back(
        cot_short,
        proj_in,
        short_normed,
        short_inv,
        short_pre,
        jnp.concatenate([short_grad_gate, short_grad_q, short_grad_kv], axis=1),
    )
    valid_rows = long_blocks[group_idx] * BLOCK
    normed, inv_std, x_bf, pre_act, gate_u, queries, keys_vals = project_rows(
        x_long, proj_in, value_cols, query_cols
    )
    offsets = jnp.arange(long_rows, dtype=jnp.int32)
    own_pos = sp_index * long_rows + offsets
    received = lax.all_gather(keys_vals, "sp", axis=0, tiled=True)
    key_pos = jnp.arange(received.shape[0], dtype=jnp.int32)
    mixed_out = attend(queries, received, long_coeffs(own_pos, key_pos, valid_rows))
    out_long, gated_long, grad_gate, grad_mixed = head_out(
        x_long, cot_long, proj_out, gate_u, mixed_out
    )
    received = lax.all_gather(keys_vals, "sp", axis=0, tiled=True)
    key_pos = jnp.arange(received.shape[0], dtype=jnp.int32)
    add_q, unused_kv = attend_back(
        queries, received, grad_mixed, long_coeffs(own_pos, key_pos, valid_rows), True, False
    )
    query_grads = jnp.concatenate([queries, grad_mixed], axis=1)
    received = lax.all_gather(query_grads, "sp", axis=0, tiled=True)
    query_pos = jnp.arange(received.shape[0], dtype=jnp.int32)
    unused_q, add_kv = attend_back(
        received[:, :query_cols],
        keys_vals,
        received[:, query_cols:],
        long_coeffs(query_pos, own_pos, valid_rows),
        False,
        True,
    )
    grad_pre_long, back_long = input_back(
        cot_long,
        proj_in,
        normed,
        inv_std,
        pre_act,
        jnp.concatenate([grad_gate, add_q, add_kv], axis=1),
    )
    total_rows = lax.axis_size("dp") * sp_size * (long_rows + x_short.shape[0])
    factor = float(total_rows) ** (-0.5)
    long_part = contract(x_bf, grad_pre_long, ((0,), (0,)))
    sum_in = lax.psum_scatter(
        long_part + contract(short_bf, grad_pre_short, ((0,), (0,))),
        ("dp", "sp"),
        scatter_dimension=0,
        tiled=True,
    )
    long_part = contract(cot_long, gated_long, ((0,), (0,)))
    sum_out = lax.psum_scatter(
        long_part + contract(cot_short, gated_short, ((0,), (0,))),
        ("dp", "sp"),
        scatter_dimension=0,
        tiled=True,
    )
    return (out_long, out_short, back_long, back_short, sum_in * factor, sum_out * factor)


def solution(mesh):
    return jax.shard_map(
        body,
        mesh=mesh,
        in_specs=(
            P(("dp", "sp"), None),
            P(("dp", "sp"), None),
            P(),
            P(("dp", "sp"), None),
            P(),
            P(),
            P(("dp", "sp"), None),
            P(("dp", "sp"), None),
        ),
        out_specs=(
            P(("dp", "sp"), None),
            P(("dp", "sp"), None),
            P(("dp", "sp"), None),
            P(("dp", "sp"), None),
            P(("dp", "sp"), None),
            P(("dp", "sp"), None),
        ),
        check_vma=False,
    )
```

profile of v0, /device:TPU:0, one launch (start us, length us, event | category | flops | bytes accessed | tf_op | source)
XLA Modules:
  0.0 1679.2 jit_solution(11346485338654008116)
XLA Ops:
  16.7 6.2 multiply_convert_fusion.1
  27.3 8.0 multiply_convert_fusion.8
  58.4 4.5 fusion.158
  75.0 106.3 %all-gather.3.cloned.1.call-done = bf16[4096,768]{1,0:T(8,128)(2,1)} async-done(((bf16[128,768]{1,0:T(8,128)(2,1)}), bf16[4096,768]{1,0:T(8,128)(2,1)}) %all-gather.3.cloned.1.call-update) | async-done | bytes 6291472 | tf_op jit(solution)/shard_map/all_gather | solution.py:161
  183.0 4.4 fusion.280
  190.7 4.4 fusion.281
  198.4 4.4 fusion.279
  206.1 4.3 fusion.278
  218.5 4.7 multiply_convert_fusion.3
  227.0 4.7 multiply_convert_fusion.4
  235.7 4.7 multiply_convert_fusion.5
  266.1 8.4 concatenate.19
  274.5 4.5 fusion.287
  279.0 6.0 multiply_convert_fusion
  286.7 5.6 fusion.271
  292.3 4.0 fusion.56
  301.5 4.0 fusion.54
  306.2 4.4 fusion.53
  319.1 64.1 %all-gather.5.cloned.1.call-done = bf16[4096,768]{1,0:T(8,128)(2,1)} async-done(((bf16[128,768]{1,0:T(8,128)(2,1)}), bf16[4096,768]{1,0:T(8,128)(2,1)}) %all-gather.5.cloned.1.call-update) | async-done | bytes 6291472 | tf_op jit(solution)/shard_map/all_gather | solution.py:173
  392.3 4.9 fusion.52
  397.2 4.4 fusion.51
  401.6 4.9 fusion.50
  413.9 4.4 fusion.49
  423.5 4.0 fusion.107
  427.5 4.0 fusion.109
  431.5 3.9 fusion.111
  440.0 6.5 convolution_add_fusion
  446.5 6.9 fusion.286
  453.4 5.3 copy.159
  458.7 3.9 fusion.21
  471.2 553.9 %reduce-scatter.7.cloned.1.call-done = f32[8,512]{1,0:T(8,128)} async-done(((f32[1024,512]{1,0:T(8,128)}), f32[8,512]{1,0:T(8,128)}) %reduce-scatter.7.cloned.1.call-update) | async-done | bytes 16400
  1033.3 637.5 %reduce-scatter.5.cloned.1.call-done = f32[8,1536]{1,0:T(8,128)} async-done(((f32[1024,1536]{1,0:T(8,128)}), f32[8,1536]{1,0:T(8,128)}) %reduce-scatter.5.cloned.1.call-update) | async-done | bytes 49168 | tf_op jit(solution)/shard_map/reduce_scatter | solution.py:194
  (254 shorter events, 161.6 us)
Async XLA Ops:
  7.2 174.1 %all-gather.3.cloned.1.call-start = ((), (), s32[]{:S(2)}) async-start(), calls=%async_computation.2 | async-start | bytes 6488064 | tf_op jit(solution)/shard_map/all_gather | solution.py:161
  9.7 4.0 copy-start.63
  12.2 4.5 copy-start.38
  13.0 370.2 %all-gather.5.cloned.1.call-start = ((), (), s32[]{:S(2)}) async-start(), calls=%async_computation.3 | async-start | bytes 6488064 | tf_op jit(solution)/shard_map/all_gather | solution.py:173
  14.0 51.2 %copy-start.59 = (s32[1,4,2,128]{3,1,2,0:T(4,128)}, s32[1,4,2,128]{3,1,2,0:T(4,128)S(1)}, u32[]{:S(2)}) copy-start(s32[1,4,2,128]{3,1,2,0:T(4,128)S(1)} %copy.173) | copy-start | bytes 12292
  22.9 12.3 copy-start.13
  25.2 10.1 copy-start.25
  58.4 4.6 copy-start.14
  58.4 4.6 copy-start.18
  58.4 4.6 copy-start.19
  58.4 4.6 copy-start.20
  58.4 4.6 copy-start.21
  65.2 4.9 copy-start.23
  74.4 131.7 %copy-start.66 = (pred[128]{0:T(512)(128)(4,1)}, pred[128]{0:T(512)(128)(4,1)S(1)}, u32[]{:S(2)}) copy-start(pred[128]{0:T(512)(128)(4,1)S(1)} %broadcast_compare_fusion) | copy-start | bytes 388
  183.0 4.4 copy-start.31
  183.0 6.0 copy-start.39
  190.7 4.4 copy-start.32
  198.4 4.4 copy-start.33
  206.1 4.3 copy-start.34
  212.0 5.3 copy-start.54
  218.0 807.1 %reduce-scatter.7.cloned.1.call-start = ((), (), s32[]{:S(2)}) async-start(), calls=%async_computation.5 | async-start | bytes 2113536
  279.0 7.7 copy-start.3
  286.7 5.6 copy-start.51
  286.7 5.6 copy-start.67
  286.7 5.6 copy-start.69
  306.2 5.9 copy-start.40
  318.8 1352.0 %reduce-scatter.5.cloned.1.call-start = ((), (), s32[]{:S(2)}) async-start(), calls=%async_computation.4 | async-start | bytes 6340608 | tf_op jit(solution)/shard_map/reduce_scatter | solution.py:194
  423.5 4.0 copy-start.35
  435.4 4.6 copy-start.17
  435.4 4.6 copy-start.56
  458.7 4.1 copy-start.64
  469.3 560.7 %copy-start.58 = (f32[128]{0:T(128)S(1)}, f32[128]{0:T(128)}, u32[]{:S(2)}) copy-start(f32[128]{0:T(128)} %copy-done.57) | copy-start | bytes 1540
  (43 other events, 115.5 us)
Sparse Core Ops, SparseCore 0:
  13.1 168.1 all-gather.2
  218.1 164.9 all-gather.4
  385.5 639.5 reduce-scatter.6
  1027.4 643.3 reduce-scatter.4
where the time goes:
time: 1690 us; the launch traced here: 1680 us
  waiting for transfers between devices  1360 us (80%)
  matrix products  198 us (12%)
  local copies, waits for them, and re-layouts  71.1 us (4%)
  other arithmetic  31.9 us (2%)
    reduce_scatter x1, waiting for transfers between devices, body(): lax.psum_scatter(long_part + contract(short_bf, grad_pre_short, ((0,), (0...  638 us
    unnamed x5, waiting for transfers between devices  554 us
    dot_general x60, matrix products, contract(): lax.dot_general(first_op, second_op, (contract_dims, ((), ())), preferred...  198 us
    all_gather x1, waiting for transfers between devices, body(): received = lax.all_gather(keys_vals, 'sp', axis=0, tiled=True)  106 us
    all_gather x1, waiting for transfers between devices, body(): received = lax.all_gather(query_grads, 'sp', axis=0, tiled=True)  64.1 us
  transfers between devices with their start and end apart: 4, of which 4 were waited for; matrix products, arithmetic and copies ran while one was open for 14% of the time, Pallas kernels for 0%

commit v1 on v0

v1 whole, which is shorter than its diff:
```python
import functools

import jax
import jax.numpy as jnp
from jax import lax
from jax.experimental import pallas as pl
from jax.experimental.pallas import tpu as pltpu
from jax.sharding import PartitionSpec as P

H = 4
BLOCK = 512
KW = 64
VW = 128
HW = 2 * KW + VW
EPS = 1e-05
HALF_SCALE = 0.5 * KW**-0.5
F32 = jnp.float32
BF16 = jnp.bfloat16
MIB = 1024 * 1024


def dot(first, second, first_dim, second_dim):
    return lax.dot_general(
        first, second, (((first_dim,), (second_dim,)), ((), ())), preferred_element_type=F32
    )


def norm_rows(rows):
    center = rows - jnp.mean(rows, axis=-1, keepdims=True)
    inv_root = lax.rsqrt(jnp.mean(center * center, axis=-1, keepdims=True) + EPS)
    return center * inv_root, inv_root


def norm_back(upstream, normed, inv_root):
    return inv_root * (
        upstream
        - jnp.mean(upstream, axis=-1, keepdims=True)
        - normed * jnp.mean(upstream * normed, axis=-1, keepdims=True)
    )


def silu_half(half):
    return half * (1.0 + jnp.tanh(half))


def silu_both(half):
    curve = jnp.tanh(half)
    above = 1.0 + curve
    act = half * above
    return act, above + act * (1.0 - curve)


def low_lanes(shape):
    return lax.broadcasted_iota(jnp.int32, shape, 1) < KW


def turned(pair):
    return pltpu.roll(pair.astype(F32), KW, 1)


def score_side(qk):
    return jnp.where(low_lanes(qk.shape), 0.0, turned(qk) * HALF_SCALE).astype(BF16)


def causal(keys_first, keys, queries, key_start=0, query_start=0):
    shape = (keys, queries) if keys_first else (queries, keys)
    key_pos = key_start + lax.broadcasted_iota(jnp.int32, shape, 0 if keys_first else 1)
    query_pos = query_start + lax.broadcasted_iota(jnp.int32, shape, 1 if keys_first else 0)
    return key_pos <= query_pos


def project(x_bf, proj):
    act, slope = silu_both(0.5 * dot(x_bf, proj, 1, 0))
    return act.astype(BF16), 0.5 * slope


def head_out(x_rows, cot, proj_out, gate_u, slope_gate, mixed):
    mixed_n, inv_mix = norm_rows(mixed)
    gate_f = gate_u.astype(F32)
    gated = (mixed_n * gate_f).astype(BF16)
    out = (x_rows.astype(F32) + dot(gated, proj_out, 1, 0)).astype(BF16)
    grad_g = dot(cot, proj_out, 1, 1)
    grad_mixed = norm_back(grad_g * gate_f, mixed_n, inv_mix)
    grad_gate = (grad_g * mixed_n * slope_gate).astype(BF16)
    return out, gated, grad_gate, grad_mixed


def run_place():
    index = lax.axis_index("sp")
    return lax.rem(index, H), lax.div(index, H), lax.axis_index("dp")


def split_rows(part, start):
    for block in range(2):
        yield block, pl.ds(pl.multiple_of(start + 2 * part * block, part), part)


def long_project_kernel(
    x_ref,
    cot_ref,
    pin_gate_ref,
    pin_q_ref,
    pin_k_ref,
    pin_v_ref,
    proj_ref,
    send_ref,
    inv_ref,
    gate_ref,
    slope_ref,
    half_ref,
    *refs,
):
    pack_refs, (xbf_ref, rest_ref) = refs[:H], refs[H:]
    step = pl.program_id(0)
    width = x_ref.shape[1]

    @pl.when(step == 0)
    def _():
        normed, inv_std = norm_rows(x_ref[...].astype(F32))
        xbf_ref[...] = normed.astype(BF16)
        inv_ref[...] = inv_std

    x_bf = xbf_ref[...]
    act, slope = project(x_bf, pin_gate_ref[...])
    gate_ref[...] = act
    slope_ref[...] = slope.astype(BF16)
    q_pair, k_pair = pin_q_ref[...], pin_k_ref[...]
    low = low_lanes(q_pair.shape)
    even = jnp.where(low, q_pair.astype(F32), turned(k_pair)).astype(BF16)
    odd = jnp.where(low, turned(q_pair), k_pair.astype(F32)).astype(BF16)
    proj = jnp.concatenate([even, pin_v_ref[:, :VW], odd, pin_v_ref[:, VW:]], axis=1)
    proj_ref[...] = proj
    act, slope = project(x_bf, proj)
    rest_ref[step] = slope.astype(BF16)
    for copy in range(send_ref.shape[0]):
        for which in range(2):
            send_ref[copy, which] = act[:, HW * which : HW * (which + 1)]

    @pl.when(step == 1)
    def _():
        mine, _, group = run_place()
        part = width // 4
        for block, features in split_rows(part, (1 - lax.rem(group, 2)) * part):
            half_ref[:, block * part : (block + 1) * part] = cot_ref[:, features]
            half_ref[:, (block + 2) * part : (block + 3) * part] = xbf_ref[:, features]
        for bits in range(H):
            head = mine ^ bits
            start = pl.multiple_of(lax.rem(head, 2) * HW, HW)
            pack_refs[bits][:, :width] = xbf_ref[...]
            pack_refs[bits][:, width:] = rest_ref[lax.div(head, 2), :, pl.ds(start, HW)]


def short_forward_kernel(
    user_ref,
    x_ref,
    cot_ref,
    pin_ref,
    proj_ref,
    pout_ref,
    out_ref,
    qkv_ref,
    g_ref,
    grad_gate_ref,
    slope_ref,
    xbf_ref,
    inv_ref,
    mine_ref,
    other_ref,
    sum_ref,
    seen_ref,
    mixed_ref,
    side_ref,
):
    step = pl.program_id(0)
    joined = user_ref[0, 0] == user_ref[0, 1]
    share = jnp.where(joined, 0.5 / BLOCK, 1.0 / BLOCK)
    normed, inv_std = norm_rows(x_ref[...].astype(F32))
    x_bf = normed.astype(BF16)
    xbf_ref[...] = x_bf
    inv_ref[...] = inv_std
    act, slope = project(x_bf, proj_ref[...])
    slope_ref[...] = slope.astype(BF16)
    qkv_ref[...] = act
    gate_u, slope_gate = project(x_bf, pin_ref[...])
    half = BLOCK // 2
    for which in range(H):
        qk = act[:, HW * which : HW * which + 2 * KW]
        values = act[:, HW * which + 2 * KW : HW * (which + 1)]
        side = score_side(qk)
        scores = dot(side, qk[:half], 1, 1)
        weights = jnp.where(causal(False, half, BLOCK), silu_half(scores), 0.0).astype(BF16)
        mixed = dot(weights, values[:half], 1, 0)
        scores = dot(side[half:], qk[half:], 1, 1)
        weights = jnp.where(causal(False, half, half), silu_half(scores), 0.0).astype(BF16)
        lower = mixed[half:] + dot(weights, values[half:], 1, 0)
        mixed_ref[:half, VW * which : VW * (which + 1)] = mixed[:half]
        mixed_ref[half:, VW * which : VW * (which + 1)] = lower

        side_ref[:, 2 * KW * which : 2 * KW * (which + 1)] = side

    @pl.when(jnp.logical_and(step == 1, joined))
    def _():
        for which in range(H):
            first = HW * which
            side = side_ref[:, 2 * KW * which : 2 * KW * (which + 1)]
            scores = dot(side, seen_ref[:, first : first + 2 * KW], 1, 1)
            mixed_ref[:, VW * which : VW * (which + 1)] += dot(
                silu_half(scores).astype(BF16), seen_ref[:, first + 2 * KW : first + HW], 1, 0
            )

    @pl.when(step == 0)
    def _():
        seen_ref[...] = act

    out, gated, grad_gate, grad_mixed = head_out(
        x_ref[...],
        cot_ref[...],
        pout_ref[...],
        gate_u,
        slope_gate,
        mixed_ref[...] * share,
    )
    out_ref[...] = out
    grad_gate_ref[...] = grad_gate
    g_ref[...] = (grad_mixed.astype(BF16).astype(F32) * share).astype(BF16)
    gates = gated.shape[1]

    @pl.when(step == 0)
    def _():
        sum_ref[:, :gates] = dot(cot_ref[...], gated, 0, 0)
        sum_ref[:, gates:] = dot(xbf_ref[...], grad_gate_ref[...], 0, 0)

    @pl.when(step == 1)
    def _():
        part = mine_ref.shape[0] // 2
        core = lax.rem(lax.axis_index("dp"), 2)
        for target, side in ((mine_ref, core), (other_ref, 1 - core)):
            for block, features in split_rows(part, side * part):
                here = slice(block * part, (block + 1) * part)
                total = sum_ref[features, :gates] + dot(cot_ref[:, features], gated, 0, 0)
                target[here, :gates] = total.astype(BF16)
                total = dot(xbf_ref[:, features], grad_gate_ref[...], 0, 0)
                target[here, gates:] = (sum_ref[features, gates:] + total).astype(BF16)


def back_block(query_side, query_qk, key_qk, values, g_rows, mask):
    act, slope = silu_both(dot(key_qk, query_side, 1, 1))
    slopes = dot(values, g_rows, 1, 1) * slope
    if mask is not None:
        act = jnp.where(mask, act, 0.0)
        slopes = jnp.where(mask, slopes, 0.0)
    slopes = slopes.astype(BF16)
    grad_q = dot(slopes, key_qk, 0, 0)
    grad_k = dot(slopes, query_qk, 1, 0)
    grad_v = dot(act.astype(BF16), g_rows, 1, 0)
    return grad_q, grad_k, grad_v


def short_back_kernel(
    user_ref, qkv_ref, g_ref, slope_ref, xbf_ref, grad_ref, mine_ref, other_ref, acc_ref, side_ref
):
    joined = user_ref[0, 0] == user_ref[0, 1]
    half = BLOCK // 2
    heads = range(qkv_ref.shape[1] // HW)
    for which in heads:
        first = HW * which
        qk = qkv_ref[:, first : first + 2 * KW]
        side = score_side(qk)
        values = qkv_ref[:, first + 2 * KW : first + HW]
        g_rows = g_ref[:, VW * which : VW * (which + 1)]
        lanes = low_lanes((half, 2 * KW))
        for block in range(qkv_ref.shape[0] // BLOCK):
            top = slice(block * BLOCK, block * BLOCK + half)
            end = slice(block * BLOCK + half, (block + 1) * BLOCK)
            both = slice(block * BLOCK, (block + 1) * BLOCK)
            dq_one, dk_one, dv_one = back_block(
                side[both], qk[both], qk[top], values[top], g_rows[both], causal(True, half, BLOCK)
            )
            dq_two, dk_two, dv_two = back_block(
                side[end], qk[end], qk[end], values[end], g_rows[end], causal(True, half, half)
            )
            acc_ref[top, first : first + 2 * KW] = jnp.where(lanes, dk_one, dq_one[:half])
            acc_ref[end, first : first + 2 * KW] = jnp.where(lanes, dk_two, dq_one[half:] + dq_two)
            acc_ref[top, first + 2 * KW : first + HW] = dv_one
            acc_ref[end, first + 2 * KW : first + HW] = dv_two
        side_ref[:, 2 * KW * which : 2 * KW * (which + 1)] = side[BLOCK:]

    @pl.when(joined)
    def _():
        one, two = slice(0, BLOCK), slice(BLOCK, 2 * BLOCK)
        for which in heads:
            first = HW * which
            pair = slice(first, first + 2 * KW)
            grad_q, grad_k, grad_v = back_block(
                side_ref[:, 2 * KW * which : 2 * KW * (which + 1)],
                qkv_ref[two, pair],
                qkv_ref[one, pair],
                qkv_ref[one, first + 2 * KW : first + HW],
                g_ref[two, VW * which : VW * (which + 1)],
                None,
            )
            lanes = low_lanes((BLOCK, 2 * KW))
            acc_ref[one, pair] += jnp.where(lanes, grad_k, 0.0)
            acc_ref[two, pair] += jnp.where(lanes, 0.0, grad_q)
            acc_ref[one, first + 2 * KW : first + HW] += grad_v

    for which in heads:
        first = HW * which
        pair, rest = slice(first, first + 2 * KW), slice(first + 2 * KW, first + HW)
        grads = turned(acc_ref[:, pair]) * HALF_SCALE
        grad_ref[:, pair] = (grads * slope_ref[:, pair].astype(F32)).astype(BF16)
        grad_ref[:, rest] = (acc_ref[:, rest] * slope_ref[:, rest].astype(F32)).astype(BF16)
    grad_pre = grad_ref[...]
    part = mine_ref.shape[0] // 2
    core = lax.rem(lax.axis_index("dp"), 2)
    for target, side in ((mine_ref, core), (other_ref, 1 - core)):
        for block, features in split_rows(part, side * part):
            total = dot(xbf_ref[:, features], grad_pre, 0, 0)
            target[block * part : (block + 1) * part] = total.astype(BF16)


def rows_at(index):
    return pl.ds(pl.multiple_of(index * BLOCK, BLOCK), BLOCK)


def long_attend_kernel(blocks_smem, all_ref, *refs):
    mixed_refs, acc_ref = refs[:H], refs[H]
    mine, chunk, group = run_place()
    valid = blocks_smem[group]
    acc_ref[...] = jnp.zeros_like(acc_ref)

    @pl.when(chunk < valid)
    def _():
        side = score_side(all_ref[rows_at(chunk), : 2 * KW])

        @pl.loop(0, chunk)
        def _(index):
            scores = dot(side, all_ref[rows_at(index), : 2 * KW], 1, 1)
            acc_ref[...] += dot(
                silu_half(scores).astype(BF16), all_ref[rows_at(index), 2 * KW :], 1, 0
            )

        weights = silu_half(dot(side, all_ref[rows_at(chunk), : 2 * KW], 1, 1))
        weights = jnp.where(causal(False, BLOCK, BLOCK), weights, 0.0).astype(BF16)
        acc_ref[...] += dot(weights, all_ref[rows_at(chunk), 2 * KW :], 1, 0)

    coeff = 1.0 / (valid * BLOCK).astype(F32)
    rows = mixed_refs[0].shape[0]
    for bits in range(H):
        start = pl.multiple_of((mine ^ bits) * rows, rows)
        mixed_refs[bits][...] = (acc_ref[pl.ds(start, rows), :] * coeff).astype(BF16)


def long_back_kernel(blocks_smem, all_ref, g_ref, *refs):
    pack_refs, sum_refs, grad_refs = refs[:H], refs[H : H + 2], refs[H + 2 : 2 * H + 2]
    dq_ref, dk_ref, dv_ref, x_ref, pre_ref = refs[2 * H + 2 :]
    mine, chunk, group = run_place()
    valid = blocks_smem[group]
    dq_ref[...] = jnp.zeros_like(dq_ref)
    dk_ref[...] = jnp.zeros_like(dk_ref)
    dv_ref[...] = jnp.zeros_like(dv_ref)

    @pl.when(chunk < valid)
    def _():
        own = rows_at(chunk)
        qk = all_ref[own, : 2 * KW]
        side = score_side(qk)
        values = all_ref[own, 2 * KW :]
        g_own = g_ref[own, :]
        grad_q, grad_k, grad_v = back_block(
            side, qk, qk, values, g_own, causal(True, BLOCK, BLOCK)
        )
        dq_ref[...] = grad_q
        dk_ref[...] = grad_k
        dv_ref[...] = grad_v

        @pl.loop(0, chunk)
        def _(index):
            keys = all_ref[rows_at(index), : 2 * KW]
            act, slope = silu_both(dot(side, keys, 1, 1))
            slopes = dot(g_own, all_ref[rows_at(index), 2 * KW :], 1, 1) * slope
            dq_ref[...] += dot(slopes.astype(BF16), keys, 1, 0)

        @pl.loop(chunk + 1, valid)
        def _(index):
            g_rows = g_ref[rows_at(index), :]
            queries = all_ref[rows_at(index), : 2 * KW]
            act, slope = silu_both(dot(qk, score_side(queries), 1, 1))
            slopes = (dot(values, g_rows, 1, 1) * slope).astype(BF16)
            dk_ref[...] += dot(slopes, queries, 1, 0)
            dv_ref[...] += dot(act.astype(BF16), g_rows, 1, 0)

    coeff = 1.0 / (valid * BLOCK).astype(F32)
    rows = grad_refs[0].shape[0]
    width = x_ref.shape[1]
    lanes = low_lanes((rows, 2 * KW))
    for bits in range(H):
        part = pl.ds(pl.multiple_of((mine ^ bits) * rows, rows), rows)
        pair = turned(jnp.where(lanes, dk_ref[part, :], dq_ref[part, :])) * HALF_SCALE
        slope = pack_refs[bits][:, width:].astype(F32)
        here = slice(bits * rows, (bits + 1) * rows)
        pre_ref[here, : 2 * KW] = (pair * coeff * slope[:, : 2 * KW]).astype(BF16)
        pre_ref[here, 2 * KW :] = (dv_ref[part, :] * coeff * slope[:, 2 * KW :]).astype(BF16)
        grad_refs[bits][...] = pre_ref[here, :]
        x_ref[here, :] = pack_refs[bits][:, :width]
    part = sum_refs[0].shape[0] // 2
    core = lax.rem(group, 2)
    for target, side in zip(sum_refs, (core, 1 - core)):
        for block, features in split_rows(part, side * part):
            total = dot(x_ref[:, features], pre_ref[...], 0, 0)
            target[block * part : (block + 1) * part] = total.astype(BF16)


def long_head_kernel(
    got_0,
    got_1,
    got_2,
    got_3,
    x_ref,
    cot_ref,
    pout_ref,
    gate_ref,
    slope_ref,
    out_ref,
    send_ref,
    mid_ref,
    mixed_ref,
):
    mine, _, _ = run_place()
    for bits, got in enumerate((got_0, got_1, got_2, got_3)):
        start = pl.multiple_of((mine ^ bits) * VW, VW)
        mixed_ref[:, pl.ds(start, VW)] = got[...].astype(F32)
    out, gated, grad_gate, grad_mixed = head_out(
        x_ref[...],
        cot_ref[...],
        pout_ref[...],
        gate_ref[...],
        slope_ref[...].astype(F32),
        mixed_ref[...],
    )
    out_ref[...] = out
    cols = gated.shape[1]
    mid_ref[:, :cols] = gated
    mid_ref[:, cols:] = grad_gate
    grad_mixed = grad_mixed.astype(BF16)
    for copy in range(send_ref.shape[0]):
        for which in range(H):
            send_ref[copy, which] = grad_mixed[:, VW * which : VW * (which + 1)]


def early_sums_kernel(
    pack_ref, cot_ref, mid_ref, half_ref, mid_got, mine_ref, got_ref, sum_ref
):
    cols = mid_ref.shape[1] // 2
    part = sum_ref.shape[0] // 2
    core = lax.rem(lax.axis_index("dp"), 2)
    mid = jnp.concatenate([mid_ref[...], mid_got[...]], axis=0)
    for block, features in split_rows(part, core * part):
        here = slice(block * part, (block + 1) * part)
        for place, own in ((0, cot_ref), (1, pack_ref)):
            start = (2 * place + block) * part
            rows = jnp.concatenate([own[:, features], half_ref[:, start : start + part]], axis=0)
            there = slice(place * cols, (place + 1) * cols)
            total = mine_ref[here, there].astype(F32) + got_ref[here, there].astype(F32)
            sum_ref[here, there] = (total + dot(rows, mid[:, there], 0, 0)).astype(BF16)


def late_pair_sum_kernel(short_mine, short_got, long_mine, long_got, sum_ref):
    mine, _, _ = run_place()
    total = short_mine[...].astype(F32) + short_got[...].astype(F32)
    sum_ref[...] = total.astype(BF16)
    head = pl.ds(pl.multiple_of(mine * HW, HW), HW)
    total = short_mine[:, head].astype(F32) + short_got[:, head].astype(F32)
    total += long_mine[...].astype(F32) + long_got[...].astype(F32)
    sum_ref[:, head] = total.astype(BF16)


def final_sums_kernel(factor, early_ref, late_ref, in_ref, out_ref):
    gates = out_ref.shape[1]
    out_ref[...] = early_ref[:, :gates] * factor
    in_ref[:, :gates] = early_ref[:, gates:] * factor
    late = late_ref[0].astype(F32)
    for step in range(1, late_ref.shape[0]):
        late += late_ref[step].astype(F32)
    late = late * factor
    low = low_lanes((late.shape[0], 2 * KW))
    for pair in range(H // 2):
        first = 2 * HW * pair
        even, odd = late[:, first : first + 2 * KW], late[:, first + HW : first + HW + 2 * KW]
        first_q = gates + 2 * KW * pair
        first_k = first_q + H * KW
        first_v = gates + 2 * H * KW + 2 * VW * pair
        in_ref[:, first_q : first_q + 2 * KW] = jnp.where(low, even, turned(odd))
        in_ref[:, first_k : first_k + 2 * KW] = jnp.where(low, turned(even), odd)
        in_ref[:, first_v : first_v + VW] = late[:, first + 2 * KW : first + HW]
        in_ref[:, first_v + VW : first_v + 2 * VW] = late[:, first + HW + 2 * KW : first + 2 * HW]


def input_back_kernel(
    grad_gate_ref,
    grad_ref,
    cot_ref,
    xbf_ref,
    inv_ref,
    pin_ref,
    proj_ref,
    got_0,
    got_1,
    got_2,
    got_3,
    long_gate_ref,
    long_cot_ref,
    pack_ref,
    long_inv_ref,
    back_ref,
    long_back_ref,
    long_grad_ref,
):
    step = pl.program_id(0)
    width = cot_ref.shape[1]

    def finish(gate, grad, cot, normed, inv, target):
        grad_norm = dot(gate[...], pin_ref[...], 1, 1) + dot(grad[...], proj_ref[...], 1, 1)
        back = norm_back(grad_norm, normed.astype(F32), inv[...])
        target[...] = (cot[...].astype(F32) + back).astype(BF16)

    @pl.when(step < 2)
    def _():
        finish(grad_gate_ref, grad_ref, cot_ref, xbf_ref[...], inv_ref, back_ref)

    @pl.when(step == 2)
    def _():
        mine, _, _ = run_place()
        for bits, got in enumerate((got_0, got_1, got_2, got_3)):
            start = pl.multiple_of((mine ^ bits) * HW, HW)
            long_grad_ref[:, pl.ds(start, HW)] = got[...]
        finish(
            long_gate_ref,
            long_grad_ref,
            long_cot_ref,
            pack_ref[:, :width],
            long_inv_ref,
            long_back_ref,
        )


def shaped(shape, dtype=BF16):
    return jax.ShapeDtypeStruct(shape, dtype)


def in_hbm(shape, dtype=BF16):
    return pltpu.HBM(shape, dtype)


def call(kernel, out_shape, flops, moved, name, vmem=24, **kwargs):
    return pl.pallas_call(
        kernel,
        out_shape=out_shape,
        cost_estimate=pl.CostEstimate(flops=flops, bytes_accessed=moved, transcendentals=0),
        compiler_params=pltpu.CompilerParams(vmem_limit_bytes=vmem * MIB),
        name=name,
        **kwargs,
    )


SMEM = pl.BlockSpec(memory_space=pltpu.SMEM)
WHOLE = pl.BlockSpec(memory_space=pltpu.VMEM)


def rows_spec(rows, cols):
    return pl.BlockSpec((rows, cols), lambda step: (step, 0))


def cols_spec(rows, cols):
    return pl.BlockSpec((rows, cols), lambda step: (0, step))


def fixed_spec(rows, cols):
    return pl.BlockSpec((rows, cols), lambda step: (0, 0))


def swap_heads(pieces):
    size = lax.axis_size("sp")
    return [pieces[0]] + [
        lax.ppermute(pieces[bits], "sp", [(src, src ^ bits) for src in range(size)])
        for bits in range(1, H)
    ]


def spread_heads(sent):
    chunks, heads, rows, cols = sent.shape
    got = lax.all_to_all(sent.reshape(chunks * heads, rows, cols), "sp", 0, 0, tiled=True)
    return got.reshape(chunks * heads * rows, cols)


def swap_cores(half):
    size = lax.axis_size("dp")
    return lax.ppermute(half, "dp", [(src, src ^ 1) for src in range(size)])


def scatter_pairs(partial):
    runs, size = lax.axis_size("dp"), lax.axis_size("sp")
    groups = [
        [run * size + place for run in range(core, runs, 2) for place in range(size)]
        for core in range(2)
    ]
    count = len(groups[0])
    sent = partial.reshape(count, partial.shape[0] // count, partial.shape[1])
    return lax.all_to_all(sent, ("dp", "sp"), 0, 0, tiled=True, axis_index_groups=groups)


def body(x_long, x_short, long_blocks, short_user, proj_in, proj_out, cot_long, cot_short):
    sp_size = lax.axis_size("sp")
    long_rows, width = x_long.shape
    short_rows = x_short.shape[0]
    gates = proj_out.shape[0]
    cols = proj_in.shape[1]
    rest = cols - gates
    half = width // 2
    chunks = sp_size // H

    proj, sent, inv_long, gate_long, slope_long, half_other, *packs = call(
        long_project_kernel,
        (
            in_hbm((width, rest)),
            in_hbm((chunks, H, long_rows, HW)),
            in_hbm((long_rows, 1), F32),
            in_hbm((long_rows, gates)),
            in_hbm((long_rows, gates)),
            in_hbm((long_rows, width)),
        )
        + (in_hbm((long_rows, width + HW)),) * H,
        2 * long_rows * width * cols,
        10 * 2**20,
        "long_project",
        vmem=60,
        grid=(2,),
        in_specs=[
            fixed_spec(long_rows, width),
            fixed_spec(long_rows, width),
            cols_spec(width, gates // 2),
            pl.BlockSpec((width, 2 * KW), lambda step: (0, step + gates // (2 * KW))),
            pl.BlockSpec((width, 2 * KW), lambda step: (0, step + (gates + H * KW) // (2 * KW))),
            pl.BlockSpec((width, 2 * VW), lambda step: (0, step + (gates + 2 * H * KW) // (2 * VW))),
        ],
        out_specs=[
            cols_spec(width, rest // 2),
            pl.BlockSpec((chunks, 2, long_rows, HW), lambda step: (0, step, 0, 0)),
            fixed_spec(long_rows, 1),
            cols_spec(long_rows, gates // 2),
            cols_spec(long_rows, gates // 2),
            fixed_spec(long_rows, width),
        ]
        + [fixed_spec(long_rows, width + HW)] * H,
        scratch_shapes=[
            pltpu.VMEM((long_rows, width), BF16),
            pltpu.VMEM((2, long_rows, rest // 2), BF16),
        ],
    )(x_long, cot_long, proj_in, proj_in, proj_in, proj_in)
    whole = spread_heads(sent)

    short_out = call(
        short_forward_kernel,
        (
            in_hbm((short_rows, width)),
            in_hbm((short_rows, rest)),
            in_hbm((short_rows, gates)),
            in_hbm((short_rows, gates)),
            in_hbm((short_rows, rest)),
            in_hbm((short_rows, width)),
            in_hbm((short_rows, 1), F32),
            in_hbm((half, 2 * gates)),
            in_hbm((half, 2 * gates)),
        ),
        20 * 10**9,
        24 * 2**20,
        "short_forward",
        vmem=56,
        grid=(short_rows // BLOCK,),
        in_specs=[
            SMEM,
            rows_spec(BLOCK, width),
            rows_spec(BLOCK, width),
            fixed_spec(width, gates),
            fixed_spec(width, rest),
            fixed_spec(gates, width),
        ],
        out_specs=[
            rows_spec(BLOCK, width),
            rows_spec(BLOCK, rest),
            rows_spec(BLOCK, gates),
            rows_spec(BLOCK, gates),
            rows_spec(BLOCK, rest),
            rows_spec(BLOCK, width),
            rows_spec(BLOCK, 1),
            fixed_spec(half, 2 * gates),
            fixed_spec(half, 2 * gates),
        ],
        scratch_shapes=[
            pltpu.VMEM((width, 2 * gates), F32),
            pltpu.VMEM((BLOCK, rest), BF16),
            pltpu.VMEM((BLOCK, gates), F32),
            pltpu.VMEM((BLOCK, 2 * KW * H), BF16),
        ],
    )(short_user, x_short, cot_short, proj_in, proj, proj_out)
    out_short, qkv_short, g_short, gate_short, slope_short, xbf_short, inv_short = short_out[:7]
    early_mine, early_other = short_out[7:]
    early_got = swap_cores(early_other)

    whole, early_got, out_short = lax.optimization_barrier((whole, early_got, out_short))
    mixed = call(
        long_attend_kernel,
        (shaped((long_rows, VW)),) * H,
        2 * 10**9,
        2 * 2**20,
        "long_attend",
        in_specs=[SMEM, WHOLE],
        scratch_shapes=[
            pltpu.VMEM((BLOCK, VW), F32),
        ],
    )(long_blocks, whole)
    out_long, sent, mid = call(
        long_head_kernel,
        (
            shaped((long_rows, width)),
            in_hbm((chunks, H, long_rows, VW)),
            in_hbm((long_rows, 2 * gates)),
        ),
        4 * long_rows * width * gates,
        3 * 2**20,
        "long_head",
        in_specs=[WHOLE] * 9,
        scratch_shapes=[pltpu.VMEM((long_rows, gates), F32)],
    )(*swap_heads(mixed), x_long, cot_long, proj_out, gate_long, slope_long)
    sent, qkv_short, mid, packs, half_other = lax.optimization_barrier(
        (sent, qkv_short, mid, packs, half_other)
    )
    all_g = spread_heads(sent)
    packs = swap_heads(packs)
    half_got = swap_cores(half_other)
    mid_got = swap_cores(mid)
    grad_short, short_mine, short_other = call(
        short_back_kernel,
        (in_hbm((short_rows, rest)), in_hbm((half, rest)), in_hbm((half, rest))),
        16 * 10**9,
        13 * 2**20,
        "short_back",
        vmem=56,
        grid=(2,),
        in_specs=[
            SMEM,
            cols_spec(short_rows, rest // 2),
            cols_spec(short_rows, gates // 2),
            cols_spec(short_rows, rest // 2),
            fixed_spec(short_rows, width),
        ],
        out_specs=[
            cols_spec(short_rows, rest // 2),
            cols_spec(half, rest // 2),
            cols_spec(half, rest // 2),
        ],
        scratch_shapes=[
            pltpu.VMEM((short_rows, rest // 2), F32),
            pltpu.VMEM((BLOCK, rest // 4), BF16),
        ],
    )(short_user, qkv_short, g_short, slope_short, xbf_short)
    mid_got, half_got, packs, grad_short = lax.optimization_barrier(
        (mid_got, half_got, packs, grad_short)
    )
    short_got = swap_cores(short_other)
    early = call(
        early_sums_kernel,
        in_hbm((half, 2 * gates)),
        8 * long_rows * half * gates,
        5 * 2**20,
        "early_sums",
    )(packs[0], cot_long, mid, half_got, mid_got, early_mine, early_got)
    all_g, early = lax.optimization_barrier((all_g, early))
    early = scatter_pairs(early)

    long_mine, long_other, *grads = call(
        long_back_kernel,
        (in_hbm((half, HW)),) * 2 + (shaped((long_rows, HW)),) * H,
        7 * 10**9,
        6 * 2**20,
        "long_back",
        in_specs=[SMEM] + [WHOLE] * (2 + H),
        scratch_shapes=[
            pltpu.VMEM((BLOCK, 2 * KW), F32),
            pltpu.VMEM((BLOCK, 2 * KW), F32),
            pltpu.VMEM((BLOCK, VW), F32),
            pltpu.VMEM((BLOCK, width), BF16),
            pltpu.VMEM((BLOCK, HW), BF16),
        ],
    )(long_blocks, whole, all_g, *packs)
    grads = swap_heads(grads)
    late = call(
        late_pair_sum_kernel,
        in_hbm((half, rest)),
        half * rest,
        4 * 2**20,
        "late_pair_sum",
        vmem=60,
        grid=(2,),
        in_specs=[rows_spec(half // 2, rest)] * 2 + [rows_spec(half // 2, HW)] * 2,
        out_specs=rows_spec(half // 2, rest),
    )(short_mine, short_got, long_mine, swap_cores(long_other))
    late, grads, gate_short = lax.optimization_barrier((late, grads, gate_short))
    late = scatter_pairs(late)

    def short_rows_spec(cols):
        return pl.BlockSpec((BLOCK, cols), lambda step: (jnp.minimum(step, 1), 0))

    back_short, back_long = call(
        input_back_kernel,
        (in_hbm((short_rows, width)), in_hbm((long_rows, width))),
        2 * (short_rows + long_rows) * width * cols,
        14 * 2**20,
        "input_back",
        vmem=60,
        grid=(short_rows // BLOCK + 1,),
        in_specs=[
            short_rows_spec(gates),
            short_rows_spec(rest),
            short_rows_spec(width),
            short_rows_spec(width),
            short_rows_spec(1),
            fixed_spec(width, gates),
            fixed_spec(width, rest),
        ]
        + [fixed_spec(long_rows, HW)] * H
        + [
            pl.BlockSpec((long_rows, gates), lambda step: (0, 1)),
            fixed_spec(long_rows, width),
            fixed_spec(long_rows, width + HW),
            fixed_spec(long_rows, 1),
        ],
        out_specs=[short_rows_spec(width), fixed_spec(long_rows, width)],
        scratch_shapes=[pltpu.VMEM((long_rows, rest), BF16)],
    )(
        gate_short,
        grad_short,
        cot_short,
        xbf_short,
        inv_short,
        proj_in,
        proj,
        *grads,
        mid,
        cot_long,
        packs[0],
        inv_long,
    )
    total_rows = lax.axis_size("dp") * sp_size * (long_rows + short_rows)
    early = jnp.sum(early.astype(F32), axis=0)
    sum_in, sum_out = call(
        functools.partial(final_sums_kernel, float(total_rows) ** (-0.5)),
        (shaped((early.shape[0], cols), F32), shaped((early.shape[0], gates), F32)),
        128 * 2**10,
        2**20,
        "final_sums",
    )(early, late)
    return (out_long, out_short, back_long, back_short, sum_in, sum_out)


def solution(mesh):
    rows = P(("dp", "sp"), None)
    return jax.shard_map(
        body,
        mesh=mesh,
        in_specs=(rows, rows, P(), rows, P(), P(), rows, rows),
        out_specs=(rows,) * 6,
        check_vma=False,
    )
```

time: 1690 us -> 147 us (0.09)
  waiting for transfers between devices: 1360 us -> 24.7 us
  matrix products: 198 us -> 0 us
  Pallas kernels: 0 us -> 68.8 us
  local copies, waits for them, and re-layouts: 71.1 us -> 5.76 us
  starting transfers between devices: 0.78 us -> 44.7 us
  other arithmetic: 31.9 us -> 1.4 us
    reduce_scatter x1 -> x0, waiting for transfers between devices: 638 us -> none  [body(): lax.psum_scatter(long_part + contract(short_bf, grad_pre_short, ((0,), (0...]
    unnamed x5 -> x0, waiting for transfers between devices: 554 us -> none
    dot_general x60 -> x0, matrix products: 198 us -> none  [contract(): lax.dot_general(first_op, second_op, (contract_dims, ((), ())), preferred...]
    all_gather x2 -> x0, waiting for transfers between devices: 170 us -> none  [the longest x1 106 us: body(): received = lax.all_gather(keys_vals, 'sp', axis=0, tiled=True)]
    pallas_call x0 -> x10, Pallas kernels: none -> 68.8 us  [the longest x1 20.1 us: body(): call(short_forward_kernel, (in_hbm((short_rows, width)), in_hbm((short_ro...]
    all_to_all x0 -> x4, starting transfers between devices: none -> 33.4 us  [the longest x2 16.9 us: spread_heads(): lax.all_to_all(sent.reshape(chunks * heads, rows, cols), 'sp', 0, 0, tile...]
    dot_general x9 -> x0, local copies, waits for them, and re-layouts: 19.8 us -> none  [contract(): lax.dot_general(first_op, second_op, (contract_dims, ((), ())), preferred...]
    mul x16 -> x0, local copies, waits for them, and re-layouts: 17.7 us -> none  [the longest x8 10 us: attend_back(): key_parts.append(contract(slopes, head_q, ((0,), (0,))) * root_scale)]
  transfers between devices with their start and end apart: 4 -> 18, of which waited for: 4 -> 10; matrix products, arithmetic and copies ran while one was open for 14% -> 1% of each run, Pallas kernels for 0% -> 41%
where the time goes in v1:
time: 147 us; the launch traced here: 146 us
  Pallas kernels  68.8 us (47%)
  starting transfers between devices  44.7 us (30%)
  waiting for transfers between devices  24.7 us (17%)
  local copies, waits for them, and re-layouts  5.76 us (4%)
    pallas_call x1, Pallas kernels, body(): call(short_forward_kernel, (in_hbm((short_rows, width)), in_hbm((short_ro...  20.1 us
    all_to_all x2, starting transfers between devices, spread_heads(): lax.all_to_all(sent.reshape(chunks * heads, rows, cols), 'sp', 0, 0, tile...  16.9 us
    all_to_all x2, starting transfers between devices, scatter_pairs(): lax.all_to_all(sent, ('dp', 'sp'), 0, 0, tiled=True, axis_index_groups=gr...  16.5 us
    pallas_call x1, Pallas kernels, body(): call(short_back_kernel, (in_hbm((short_rows, rest)), in_hbm((half, rest))...  13.6 us
    pallas_call x1, Pallas kernels, body(): call(input_back_kernel, (in_hbm((short_rows, width)), in_hbm((long_rows,...  11.2 us
    ppermute x9, waiting for transfers between devices, swap_heads(): lax.ppermute(pieces[bits], 'sp', [(src, src ^ bits) for src in range(size)])  10.9 us
    ppermute x9, starting transfers between devices, swap_heads(): lax.ppermute(pieces[bits], 'sp', [(src, src ^ bits) for src in range(size)])  10.5 us
    pallas_call x1, Pallas kernels, body(): call(long_back_kernel, (in_hbm((half, HW)),) * 2 + (shaped((long_rows, HW...  10.3 us
  transfers between devices with their start and end apart: 18, of which 10 were waited for; matrix products, arithmetic and copies ran while one was open for 1% of the time, Pallas kernels for 41%

profile of v1, /device:TPU:0, one launch (start us, length us, event | category | flops | bytes accessed | tf_op | source)
XLA Modules:
  0.0 146.2 jit_solution(5886410307507190200)
XLA Ops:
  0.6 5.2 %long_project.1 = (bf16[1024,1024]{1,0:T(8,128)(2,1)}, bf16[8,4,128,256]{3,2,1,0:T(8,128)(2,1)}, f32[128,1]{1,0:T(8,128)}, bf16[128,512]{1,0:T(8,128)(2,1)}, bf1...) custom-call(bf16[128,1024]{1,0:T(8,128)(2,1)} %x_ref.5, ...), custom_call_target="tpu_custom_call" | custom-call | flops 402653184 | bytes 10485760 | tf_op jit(solution)/shard_map/long_project/pallas_call | solution.py:622
  5.9 9.3 %all-to-all-start = ((bf16[32,128,256]{2,1,0:T(8,128)(2,1)}), bf16[32,128,256]{2,1,0:T(8,128)(2,1)S(1)}, u32[]{:S(2)}, u32[]{:S(2)}) async-start(bf16[32,128,256]{2,1,0:T(8,128)(2,1)} %bitcast.10), calls=%async_computation | async-start | bytes 4194304 | tf_op jit(solution)/shard_map/all_to_all | solution.py:592
  15.2 20.1 %short_forward.1 = (bf16[1024,1024]{1,0:T(8,128)(2,1)}, bf16[1024,1024]{1,0:T(8,128)(2,1)}, bf16[1024,512]{1,0:T(8,128)(2,1)}, bf16[1024,512]{1,0:T(8,128)(2,1)}...) custom-call(s32[1,2]{1,0:T(1,128)} %user_ref.3, ...), custom_call_target="tpu_custom_call" | custom-call | flops 20000000000 | bytes 25165824 | tf_op jit(solution)/shard_map/short_forward/pallas_call | solution.py:662
  35.4 2.9 %collective-permute-done.got_ref = bf16[512,1024]{1,0:T(8,128)(2,1)S(1)} collective-permute-done((bf16[512,1024]{1,0:T(8,128)(2,1)}, bf16[512,1024]{1,0:T(8,128)(2,1)S(1)}, u32[]{:S(2)}, u32[]{:S(2)}) %collective-permute-start) | collective-permute-done | bytes 1048608 | tf_op jit(solution)/shard_map/ppermute | solution.py:598
  38.3 1.0 copy-done.4
  39.2 6.1 %all-to-all-done = bf16[32,128,256]{2,1,0:T(8,128)(2,1)S(1)} async-done(((bf16[32,128,256]{2,1,0:T(8,128)(2,1)}), bf16[32,128,256]{2,1,0:T(8,128)(2,1)S(1)}, u32[]{:S(2)}, u32[]{:S(2)}) %all-to-all-start) | async-done | bytes 2097184 | tf_op jit(solution)/shard_map/all_to_all | solution.py:592
  45.4 1.2 long_attend.1
  47.1 3.0 %collective-permute-start.3 = (bf16[128,128]{1,0:T(8,128)(2,1)S(1)}, bf16[128,128]{1,0:T(8,128)(2,1)S(1)}, u32[]{:S(2)}, u32[]{:S(2)}) collective-permute-start(bf16[128,128]{1,0:T(8,128)(2,1)S(1)} %get-tuple-element.79), channel_id=1, source_target_pairs={{0,3},{1,2},{2,1},{3,0},{4,7},{5,6},{6,5},{7,4},{8,11},{9,10},{10,... | collective-permute-start | bytes 98312 | tf_op jit(solution)/shard_map/ppermute | solution.py:585
  50.7 1.7 %collective-permute-done.3.got_3 = bf16[128,128]{1,0:T(8,128)(2,1)S(1)} collective-permute-done((bf16[128,128]{1,0:T(8,128)(2,1)S(1)}, bf16[128,128]{1,0:T(8,128)(2,1)S(1)}, u32[]{:S(2)}, u32[]{:S(2)}) %collective-permute-start.3) | collective-permute-done | bytes 32800 | tf_op jit(solution)/shard_map/ppermute | solution.py:585
  52.4 2.1 %long_head.1 = (bf16[128,1024]{1,0:T(8,128)(2,1)}, bf16[8,4,128,128]{3,2,1,0:T(8,128)(2,1)}, bf16[128,1024]{1,0:T(8,128)(2,1)}) custom-call(bf16[128,128]{1,0:T(8,128)(2,1)S(1)} %get-tuple-element.76.got_0, bf16[128,128]{1,0:T(8,128)(2,1)S(1)} %collective-permute-done.1.got_1, bf16[128,128]{1,0:T(8,128)(2,1)S(1)} %collective-permute-done.2.got_2, ...), custom_call_target="tpu_custom_call" | custom-call | flops 268435456 | bytes 3145728 | tf_op jit(solution)/shard_map/long_head/pallas_call | solution.py:722
  54.5 7.6 %all-to-all-start.1 = ((bf16[32,128,128]{2,1,0:T(8,128)(2,1)}), bf16[32,128,128]{2,1,0:T(8,128)(2,1)}, u32[]{:S(2)}, u32[]{:S(2)}) async-start(bf16[32,128,128]{2,1,0:T(8,128)(2,1)} %bitcast.11), calls=%async_computation.1 | async-start | bytes 2097152 | tf_op jit(solution)/shard_map/all_to_all | solution.py:592
  62.7 1.7 %collective-permute-start.7 = (bf16[128,1280]{1,0:T(8,128)(2,1)}, bf16[128,1280]{1,0:T(8,128)(2,1)S(1)}, u32[]{:S(2)}, u32[]{:S(2)}) collective-permute-start(bf16[128,1280]{1,0:T(8,128)(2,1)} %get-tuple-element.102), channel_id=1, source_target_pairs={{0,1},{1,0},{2,3},{3,2},{4,5},{5,4},{6,7},{7,6},{8,9},{9,8},{10,11... | collective-permute-start | bytes 983048 | tf_op jit(solution)/shard_map/ppermute | solution.py:585
  64.5 1.5 %collective-permute-start.8 = (bf16[128,1280]{1,0:T(8,128)(2,1)}, bf16[128,1280]{1,0:T(8,128)(2,1)S(1)}, u32[]{:S(2)}, u32[]{:S(2)}) collective-permute-start(bf16[128,1280]{1,0:T(8,128)(2,1)} %get-tuple-element.103), channel_id=1, source_target_pairs={{0,2},{1,3},{2,0},{3,1},{4,6},{5,7},{6,4},{7,5},{8,10},{9,11},{10,... | collective-permute-start | bytes 983048 | tf_op jit(solution)/shard_map/ppermute | solution.py:585
  66.2 13.6 %short_back.1 = (bf16[1024,1024]{1,0:T(8,128)(2,1)}, bf16[512,1024]{1,0:T(8,128)(2,1)}, bf16[512,1024]{1,0:T(8,128)(2,1)}) custom-call(s32[1,2]{1,0:T(1,128)} %user_ref.3, bf16[1024,1024]{1,0:T(8,128)(2,1)} %get-tuple-element.92.qkv_ref, bf16[1024,512]{1,0:T(8,128)(2,1)} %get-tuple-element.93.g_ref, bf16[1024,1024]{1,0:T(8,128)(2,1)} %get-tuple-element.94.slope_ref, ...), custom_call_target="tpu_custom_call" | custom-call | flops 16000000000 | bytes 13631488 | tf_op jit(solution)/shard_map/short_back/pallas_call | solution.py:742
  80.0 3.6 %collective-permute-done.7.refs_1_ = bf16[128,1280]{1,0:T(8,128)(2,1)S(1)} collective-permute-done((bf16[128,1280]{1,0:T(8,128)(2,1)}, bf16[128,1280]{1,0:T(8,128)(2,1)S(1)}, u32[]{:S(2)}, u32[]{:S(2)}) %collective-permute-start.7) | collective-permute-done | bytes 327712 | tf_op jit(solution)/shard_map/ppermute | solution.py:585
  83.7 0.7 copy-done.11
  84.4 3.7 %collective-permute-done.9.refs_3_ = bf16[128,1280]{1,0:T(8,128)(2,1)S(1)} collective-permute-done((bf16[128,1280]{1,0:T(8,128)(2,1)}, bf16[128,1280]{1,0:T(8,128)(2,1)S(1)}, u32[]{:S(2)}, u32[]{:S(2)}) %collective-permute-start.9) | collective-permute-done | bytes 327712 | tf_op jit(solution)/shard_map/ppermute | solution.py:585
  88.1 0.7 copy-done.13
  88.9 1.5 %early_sums.1 = bf16[512,1024]{1,0:T(8,128)(2,1)} custom-call(bf16[128,1280]{1,0:T(8,128)(2,1)S(1)} %copy-done.1, bf16[128,1024]{1,0:T(8,128)(2,1)S(1)} %copy-done, bf16[128,1024]{1,0:T(8,128)(2,1)S(1)} %copy-done.2, bf16[128,1024]{1,0:T(8,128)(2,1)S(1)} %collective-permute-done.6.half_ref, bf16[128,1024]{1,0:T(8,128)(2,1)S(1)} %collective-permute-done.5.mid_got, ...), custom_call_target="tpu_custom_call" | custom-call | flops 268435456 | bytes 5242880 | tf_op jit(solution)/shard_map/early_sums/pallas_call | solution.py:771
  90.4 9.8 %all-to-all-start.2 = ((bf16[64,8,1024]{2,1,0:T(8,128)(2,1)}), bf16[64,8,1024]{2,1,0:T(8,128)(2,1)}, u32[]{:S(2)}, u32[]{:S(2)}) async-start(bf16[64,8,1024]{2,1,0:T(8,128)(2,1)} %bitcast.8), calls=%async_computation.2 | async-start | bytes 2097152 | tf_op jit(solution)/shard_map/all_to_all | solution.py:609
  100.2 1.0 copy-done.12
  101.2 1.0 copy-done.14
  102.2 10.3 %long_back.1 = (bf16[512,256]{1,0:T(8,128)(2,1)}, bf16[512,256]{1,0:T(8,128)(2,1)}, bf16[128,256]{1,0:T(8,128)(2,1)S(1)}, bf16[128,256]{1,0:T(8,128)(2,1)S(1)}, ...) custom-call(s32[4]{0:T(128)S(1)} %copy-done.15, bf16[4096,256]{1,0:T(8,128)(2,1)S(1)} %bitcast.7, ...), custom_call_target="tpu_custom_call" | custom-call | flops 7000000000 | bytes 6291456 | tf_op jit(solution)/shard_map/long_back/pallas_call | solution.py:781
  113.1 1.5 %collective-permute-start.11 = (bf16[128,256]{1,0:T(8,128)(2,1)S(1)}, bf16[128,256]{1,0:T(8,128)(2,1)S(1)}, u32[]{:S(2)}, u32[]{:S(2)}) collective-permute-start(bf16[128,256]{1,0:T(8,128)(2,1)S(1)} %get-tuple-element.118), channel_id=1, source_target_pairs={{0,1},{1,0},{2,3},{3,2},{4,5},{5,4},{6,7},{7,6},{8,9},{9,8},{10,11... | collective-permute-start | bytes 196616 | tf_op jit(solution)/shard_map/ppermute | solution.py:585
  114.6 1.5 %collective-permute-start.12 = (bf16[128,256]{1,0:T(8,128)(2,1)S(1)}, bf16[128,256]{1,0:T(8,128)(2,1)S(1)}, u32[]{:S(2)}, u32[]{:S(2)}) collective-permute-start(bf16[128,256]{1,0:T(8,128)(2,1)S(1)} %get-tuple-element.119), channel_id=1, source_target_pairs={{0,2},{1,3},{2,0},{3,1},{4,6},{5,7},{6,4},{7,5},{8,10},{9,11},{10,... | collective-permute-start | bytes 196616 | tf_op jit(solution)/shard_map/ppermute | solution.py:585
  117.3 2.7 %late_pair_sum.1 = bf16[512,1024]{1,0:T(8,128)(2,1)} custom-call(bf16[512,1024]{1,0:T(8,128)(2,1)} %get-tuple-element.96.short_mine, bf16[512,1024]{1,0:T(8,128)(2,1)} %collective-permute-done.4.short_got, bf16[512,256]{1,0:T(8,128)(2,1)} %get-tuple-element.115.long_mine, bf16[512,256]{1,0:T(8,128)(2,1)} %copy-done.16), custom_call_target="tpu_custom_call" | custom-call | flops 524288 | bytes 4194304 | tf_op jit(solution)/shard_map/late_pair_sum/pallas_call | solution.py:797
  120.0 1.2 collective-permute-done.13.got_3
  121.2 6.7 %all-to-all-start.3 = ((bf16[64,8,1024]{2,1,0:T(8,128)(2,1)}), bf16[64,8,1024]{2,1,0:T(8,128)(2,1)S(1)}, u32[]{:S(2)}, u32[]{:S(2)}) async-start(bf16[64,8,1024]{2,1,0:T(8,128)(2,1)} %bitcast.9), calls=%async_computation.3 | async-start | bytes 2097152 | tf_op jit(solution)/shard_map/all_to_all | solution.py:609
  128.0 11.2 %input_back.1 = (bf16[1024,1024]{1,0:T(8,128)(2,1)}, bf16[128,1024]{1,0:T(8,128)(2,1)}) custom-call(bf16[1024,512]{1,0:T(8,128)(2,1)} %get-tuple-element.122.grad_gate_ref, bf16[1024,1024]{1,0:T(8,128)(2,1)} %get-tuple-element.123.grad_ref, bf16[1024,1024]{1,0:T(8,128)(2,1)} %cot_ref.9, bf16[1024,1024]{1,0:T(8,128)(2,1)} %get-tuple-element.95.xbf_ref, ...), custom_call_target="tpu_custom_call" | custom-call | flops 3623878656 | bytes 14680064 | tf_op jit(solution)/shard_map/input_back/pallas_call | solution.py:814
  139.2 1.4 convert_reduce_fusion.early_ref
  140.6 4.8 %all-to-all-done.3.late_ref = bf16[64,8,1024]{2,1,0:T(8,128)(2,1)S(1)} async-done(((bf16[64,8,1024]{2,1,0:T(8,128)(2,1)}), bf16[64,8,1024]{2,1,0:T(8,128)(2,1)S(1)}, u32[]{:S(2)}, u32[]{:S(2)}) %all-to-all-start.3) | async-done | bytes 1048608 | tf_op jit(solution)/shard_map/all_to_all | solution.py:609
  145.3 0.9 final_sums.1
  (57 shorter events, 4.2 us)
Async XLA Ops:
  5.9 39.5 %all-to-all-start = ((bf16[32,128,256]{2,1,0:T(8,128)(2,1)}), bf16[32,128,256]{2,1,0:T(8,128)(2,1)S(1)}, u32[]{:S(2)}, u32[]{:S(2)}) async-start(bf16[32,128,256]{2,1,0:T(8,128)(2,1)} %bitcast.10), calls=%async_computation | async-start | bytes 4194304 | tf_op jit(solution)/shard_map/all_to_all | solution.py:592
  15.2 30.2 %copy-start.15 = (s32[4]{0:T(128)S(1)}, s32[4]{0:T(128)}, u32[]{:S(2)}) copy-start(s32[4]{0:T(128)} %blocks_smem.3) | copy-start | bytes 52
  35.3 3.0 %collective-permute-start = (bf16[512,1024]{1,0:T(8,128)(2,1)}, bf16[512,1024]{1,0:T(8,128)(2,1)S(1)}, u32[]{:S(2)}, u32[]{:S(2)}) collective-permute-start(bf16[512,1024]{1,0:T(8,128)(2,1)} %get-tuple-element.73), channel_id=1, source_target_pairs={{0,32},{32,0},{64,96},{96,64},{1,33},{33,1},{65,97},{97,65},{2,34}... | collective-permute-start | bytes 3145736 | tf_op jit(solution)/shard_map/ppermute | solution.py:598
  45.4 7.0 %copy-start = (bf16[128,1024]{1,0:T(8,128)(2,1)S(1)}, bf16[128,1024]{1,0:T(8,128)(2,1)}, u32[]{:S(2)}) copy-start(bf16[128,1024]{1,0:T(8,128)(2,1)} %long_cot_ref.1) | copy-start | bytes 786436
  45.4 7.0 %copy-start.6 = (bf16[128,1024]{1,0:T(8,128)(2,1)S(1)}, bf16[128,1024]{1,0:T(8,128)(2,1)}, u32[]{:S(2)}) copy-start(bf16[128,1024]{1,0:T(8,128)(2,1)} %x_ref.5) | copy-start | bytes 786436
  45.4 7.0 %copy-start.7 = (bf16[512,1024]{1,0:T(8,128)(2,1)S(1)}, bf16[512,1024]{1,0:T(8,128)(2,1)}, u32[]{:S(2)}) copy-start(bf16[512,1024]{1,0:T(8,128)(2,1)} %pout_ref.3) | copy-start | bytes 3145732
  45.4 7.0 %copy-start.8 = (bf16[128,512]{1,0:T(8,128)(2,1)S(1)}, bf16[128,512]{1,0:T(8,128)(2,1)}, u32[]{:S(2)}) copy-start(bf16[128,512]{1,0:T(8,128)(2,1)} %get-tuple-element.80.gate_ref) | copy-start | bytes 393220
  45.4 7.0 %copy-start.9 = (bf16[128,512]{1,0:T(8,128)(2,1)S(1)}, bf16[128,512]{1,0:T(8,128)(2,1)}, u32[]{:S(2)}) copy-start(bf16[128,512]{1,0:T(8,128)(2,1)} %get-tuple-element.81.slope_ref) | copy-start | bytes 393220
  46.6 15.5 %copy-start.20 = (bf16[128,1024]{1,0:T(8,128)(2,1)S(1)}, bf16[128,1024]{1,0:T(8,128)(2,1)}, u32[]{:S(2)}) copy-start(bf16[128,1024]{1,0:T(8,128)(2,1)} %get-tuple-element.100) | copy-start | bytes 786436
  46.6 4.0 %collective-permute-start.1 = (bf16[128,128]{1,0:T(8,128)(2,1)S(1)}, bf16[128,128]{1,0:T(8,128)(2,1)S(1)}, u32[]{:S(2)}, u32[]{:S(2)}) collective-permute-start(bf16[128,128]{1,0:T(8,128)(2,1)S(1)} %get-tuple-element.77), channel_id=1, source_target_pairs={{0,1},{1,0},{2,3},{3,2},{4,5},{5,4},{6,7},{7,6},{8,9},{9,8},{10,11... | collective-permute-start | bytes 98312 | tf_op jit(solution)/shard_map/ppermute | solution.py:585
  46.7 4.0 %collective-permute-start.2 = (bf16[128,128]{1,0:T(8,128)(2,1)S(1)}, bf16[128,128]{1,0:T(8,128)(2,1)S(1)}, u32[]{:S(2)}, u32[]{:S(2)}) collective-permute-start(bf16[128,128]{1,0:T(8,128)(2,1)S(1)} %get-tuple-element.78), channel_id=1, source_target_pairs={{0,2},{1,3},{2,0},{3,1},{4,6},{5,7},{6,4},{7,5},{8,10},{9,11},{10,... | collective-permute-start | bytes 98312 | tf_op jit(solution)/shard_map/ppermute | solution.py:585
  47.1 5.3 %collective-permute-start.3 = (bf16[128,128]{1,0:T(8,128)(2,1)S(1)}, bf16[128,128]{1,0:T(8,128)(2,1)S(1)}, u32[]{:S(2)}, u32[]{:S(2)}) collective-permute-start(bf16[128,128]{1,0:T(8,128)(2,1)S(1)} %get-tuple-element.79), channel_id=1, source_target_pairs={{0,3},{1,2},{2,1},{3,0},{4,7},{5,6},{6,5},{7,4},{8,11},{9,10},{10,... | collective-permute-start | bytes 98312 | tf_op jit(solution)/shard_map/ppermute | solution.py:585
  54.5 7.7 %copy-start.2 = (bf16[128,1024]{1,0:T(8,128)(2,1)S(1)}, bf16[128,1024]{1,0:T(8,128)(2,1)}, u32[]{:S(2)}) copy-start(bf16[128,1024]{1,0:T(8,128)(2,1)} %get-tuple-element.99.mid_ref.long_gate_ref) | copy-start | bytes 786436
  54.5 35.9 %all-to-all-start.1 = ((bf16[32,128,128]{2,1,0:T(8,128)(2,1)}), bf16[32,128,128]{2,1,0:T(8,128)(2,1)}, u32[]{:S(2)}, u32[]{:S(2)}) async-start(bf16[32,128,128]{2,1,0:T(8,128)(2,1)} %bitcast.11), calls=%async_computation.1 | async-start | bytes 2097152 | tf_op jit(solution)/shard_map/all_to_all | solution.py:592
  62.1 17.7 %collective-permute-start.6 = (bf16[128,1024]{1,0:T(8,128)(2,1)S(1)}, bf16[128,1024]{1,0:T(8,128)(2,1)S(1)}, u32[]{:S(2)}, u32[]{:S(2)}) collective-permute-start(bf16[128,1024]{1,0:T(8,128)(2,1)S(1)} %copy-done.20), channel_id=1, source_target_pairs={{0,32},{32,0},{64,96},{96,64},{1,33},{33,1},{65,97},{97,65},{2,34}... | collective-permute-start | bytes 786440 | tf_op jit(solution)/shard_map/ppermute | solution.py:598
  62.2 17.7 %collective-permute-start.5 = (bf16[128,1024]{1,0:T(8,128)(2,1)S(1)}, bf16[128,1024]{1,0:T(8,128)(2,1)S(1)}, u32[]{:S(2)}, u32[]{:S(2)}) collective-permute-start(bf16[128,1024]{1,0:T(8,128)(2,1)S(1)} %copy-done.2), channel_id=1, source_target_pairs={{0,32},{32,0},{64,96},{96,64},{1,33},{33,1},{65,97},{97,65},{2,34}... | collective-permute-start | bytes 786440 | tf_op jit(solution)/shard_map/ppermute | solution.py:598
  62.7 20.8 %collective-permute-start.7 = (bf16[128,1280]{1,0:T(8,128)(2,1)}, bf16[128,1280]{1,0:T(8,128)(2,1)S(1)}, u32[]{:S(2)}, u32[]{:S(2)}) collective-permute-start(bf16[128,1280]{1,0:T(8,128)(2,1)} %get-tuple-element.102), channel_id=1, source_target_pairs={{0,1},{1,0},{2,3},{3,2},{4,5},{5,4},{6,7},{7,6},{8,9},{9,8},{10,11... | collective-permute-start | bytes 983048 | tf_op jit(solution)/shard_map/ppermute | solution.py:585
  64.5 19.3 %collective-permute-start.8 = (bf16[128,1280]{1,0:T(8,128)(2,1)}, bf16[128,1280]{1,0:T(8,128)(2,1)S(1)}, u32[]{:S(2)}, u32[]{:S(2)}) collective-permute-start(bf16[128,1280]{1,0:T(8,128)(2,1)} %get-tuple-element.103), channel_id=1, source_target_pairs={{0,2},{1,3},{2,0},{3,1},{4,6},{5,7},{6,4},{7,5},{8,10},{9,11},{10,... | collective-permute-start | bytes 983048 | tf_op jit(solution)/shard_map/ppermute | solution.py:585
  65.9 22.2 %collective-permute-start.9 = (bf16[128,1280]{1,0:T(8,128)(2,1)}, bf16[128,1280]{1,0:T(8,128)(2,1)S(1)}, u32[]{:S(2)}, u32[]{:S(2)}) collective-permute-start(bf16[128,1280]{1,0:T(8,128)(2,1)} %get-tuple-element.104), channel_id=1, source_target_pairs={{0,3},{1,2},{2,1},{3,0},{4,7},{5,6},{6,5},{7,4},{8,11},{9,10},{10,... | collective-permute-start | bytes 983048 | tf_op jit(solution)/shard_map/ppermute | solution.py:585
  66.2 22.6 %copy-start.1 = (bf16[128,1280]{1,0:T(8,128)(2,1)S(1)}, bf16[128,1280]{1,0:T(8,128)(2,1)}, u32[]{:S(2)}) copy-start(bf16[128,1280]{1,0:T(8,128)(2,1)} %get-tuple-element.106.pack_ref.refs_0_) | copy-start | bytes 983044
  66.2 22.6 %copy-start.3 = (bf16[512,1024]{1,0:T(8,128)(2,1)S(1)}, bf16[512,1024]{1,0:T(8,128)(2,1)}, u32[]{:S(2)}) copy-start(bf16[512,1024]{1,0:T(8,128)(2,1)} %get-tuple-element.109.mine_ref) | copy-start | bytes 3145732
  66.2 22.6 %copy-start.5 = (bf16[512,1024]{1,0:T(8,128)(2,1)S(1)}, bf16[512,1024]{1,0:T(8,128)(2,1)}, u32[]{:S(2)}) copy-start(bf16[512,1024]{1,0:T(8,128)(2,1)} %copy-done.4) | copy-start | bytes 3145732
  79.9 36.7 %collective-permute-start.4 = (bf16[512,1024]{1,0:T(8,128)(2,1)}, bf16[512,1024]{1,0:T(8,128)(2,1)}, u32[]{:S(2)}, u32[]{:S(2)}) collective-permute-start(bf16[512,1024]{1,0:T(8,128)(2,1)} %get-tuple-element.97), channel_id=1, source_target_pairs={{0,32},{32,0},{64,96},{96,64},{1,33},{33,1},{65,97},{97,65},{2,34}... | collective-permute-start | bytes 3145736 | tf_op jit(solution)/shard_map/ppermute | solution.py:598
  90.4 30.9 %all-to-all-start.2 = ((bf16[64,8,1024]{2,1,0:T(8,128)(2,1)}), bf16[64,8,1024]{2,1,0:T(8,128)(2,1)}, u32[]{:S(2)}, u32[]{:S(2)}) async-start(bf16[64,8,1024]{2,1,0:T(8,128)(2,1)} %bitcast.8), calls=%async_computation.2 | async-start | bytes 2097152 | tf_op jit(solution)/shard_map/all_to_all | solution.py:609
  113.1 3.5 %collective-permute-start.10 = (bf16[512,256]{1,0:T(8,128)(2,1)}, bf16[512,256]{1,0:T(8,128)(2,1)S(1)}, u32[]{:S(2)}, u32[]{:S(2)}) collective-permute-start(bf16[512,256]{1,0:T(8,128)(2,1)} %get-tuple-element.116), channel_id=1, source_target_pairs={{0,32},{32,0},{64,96},{96,64},{1,33},{33,1},{65,97},{97,65},{2,34}... | collective-permute-start | bytes 786440 | tf_op jit(solution)/shard_map/ppermute | solution.py:598
  113.1 6.9 %collective-permute-start.11 = (bf16[128,256]{1,0:T(8,128)(2,1)S(1)}, bf16[128,256]{1,0:T(8,128)(2,1)S(1)}, u32[]{:S(2)}, u32[]{:S(2)}) collective-permute-start(bf16[128,256]{1,0:T(8,128)(2,1)S(1)} %get-tuple-element.118), channel_id=1, source_target_pairs={{0,1},{1,0},{2,3},{3,2},{4,5},{5,4},{6,7},{7,6},{8,9},{9,8},{10,11... | collective-permute-start | bytes 196616 | tf_op jit(solution)/shard_map/ppermute | solution.py:585
  114.6 5.4 %collective-permute-start.12 = (bf16[128,256]{1,0:T(8,128)(2,1)S(1)}, bf16[128,256]{1,0:T(8,128)(2,1)S(1)}, u32[]{:S(2)}, u32[]{:S(2)}) collective-permute-start(bf16[128,256]{1,0:T(8,128)(2,1)S(1)} %get-tuple-element.119), channel_id=1, source_target_pairs={{0,2},{1,3},{2,0},{3,1},{4,6},{5,7},{6,4},{7,5},{8,10},{9,11},{10,... | collective-permute-start | bytes 196616 | tf_op jit(solution)/shard_map/ppermute | solution.py:585
  116.1 5.2 %collective-permute-start.13 = (bf16[128,256]{1,0:T(8,128)(2,1)S(1)}, bf16[128,256]{1,0:T(8,128)(2,1)S(1)}, u32[]{:S(2)}, u32[]{:S(2)}) collective-permute-start(bf16[128,256]{1,0:T(8,128)(2,1)S(1)} %get-tuple-element.120), channel_id=1, source_target_pairs={{0,3},{1,2},{2,1},{3,0},{4,7},{5,6},{6,5},{7,4},{8,11},{9,10},{10,... | collective-permute-start | bytes 196616 | tf_op jit(solution)/shard_map/ppermute | solution.py:585
  120.0 7.9 %copy-start.17 = (bf16[128,256]{1,0:T(8,128)(2,1)}, bf16[128,256]{1,0:T(8,128)(2,1)S(1)}, u32[]{:S(2)}) copy-start(bf16[128,256]{1,0:T(8,128)(2,1)S(1)} %collective-permute-done.11.got_1) | copy-start | bytes 196612
  120.0 7.9 %copy-start.18 = (bf16[128,256]{1,0:T(8,128)(2,1)}, bf16[128,256]{1,0:T(8,128)(2,1)S(1)}, u32[]{:S(2)}) copy-start(bf16[128,256]{1,0:T(8,128)(2,1)S(1)} %collective-permute-done.12.got_2) | copy-start | bytes 196612
  121.2 6.7 %copy-start.19 = (bf16[128,256]{1,0:T(8,128)(2,1)}, bf16[128,256]{1,0:T(8,128)(2,1)S(1)}, u32[]{:S(2)}) copy-start(bf16[128,256]{1,0:T(8,128)(2,1)S(1)} %collective-permute-done.13.got_3) | copy-start | bytes 196612
  121.2 24.1 %all-to-all-start.3 = ((bf16[64,8,1024]{2,1,0:T(8,128)(2,1)}), bf16[64,8,1024]{2,1,0:T(8,128)(2,1)S(1)}, u32[]{:S(2)}, u32[]{:S(2)}) async-start(bf16[64,8,1024]{2,1,0:T(8,128)(2,1)} %bitcast.9), calls=%async_computation.3 | async-start | bytes 2097152 | tf_op jit(solution)/shard_map/all_to_all | solution.py:609
  (7 other events, 5.7 us)

commit v2 on v1

--- a/solution.py
+++ b/solution.py
@@ -96,58 +96,36 @@
 
 
 def long_project_kernel(
-    x_ref,
-    cot_ref,
-    pin_gate_ref,
-    pin_q_ref,
-    pin_k_ref,
-    pin_v_ref,
-    proj_ref,
-    send_ref,
-    inv_ref,
-    gate_ref,
-    slope_ref,
-    half_ref,
-    *refs,
+    x_ref, pin_q_ref, pin_k_ref, pin_v_ref, proj_ref, send_ref, inv_ref, xbf_ref, slope_ref
 ):
-    pack_refs, (xbf_ref, rest_ref) = refs[:H], refs[H:]
-    step = pl.program_id(0)
-    width = x_ref.shape[1]
-
-    @pl.when(step == 0)
+    @pl.when(pl.program_id(0) == 0)
     def _():
         normed, inv_std = norm_rows(x_ref[...].astype(F32))
         xbf_ref[...] = normed.astype(BF16)
         inv_ref[...] = inv_std
 
-    x_bf = xbf_ref[...]
-    act, slope = project(x_bf, pin_gate_ref[...])
-    gate_ref[...] = act
-    slope_ref[...] = slope.astype(BF16)
     q_pair, k_pair = pin_q_ref[...], pin_k_ref[...]
     low = low_lanes(q_pair.shape)
     even = jnp.where(low, q_pair.astype(F32), turned(k_pair)).astype(BF16)
     odd = jnp.where(low, turned(q_pair), k_pair.astype(F32)).astype(BF16)
     proj = jnp.concatenate([even, pin_v_ref[:, :VW], odd, pin_v_ref[:, VW:]], axis=1)
     proj_ref[...] = proj
-    act, slope = project(x_bf, proj)
-    rest_ref[step] = slope.astype(BF16)
+    act, slope = project(xbf_ref[...], proj)
+    slope_ref[...] = slope.astype(BF16)
     for copy in range(send_ref.shape[0]):
         for which in range(2):
             send_ref[copy, which] = act[:, HW * which : HW * (which + 1)]
 
-    @pl.when(step == 1)
-    def _():
-        mine, _, group = run_place()
-        part = width // 4
-        for block, features in split_rows(part, (1 - lax.rem(group, 2)) * part):
-            half_ref[:, block * part : (block + 1) * part] = cot_ref[:, features]
-            half_ref[:, (block + 2) * part : (block + 3) * part] = xbf_ref[:, features]
-        for bits in range(H):
-            head = mine ^ bits
-            start = pl.multiple_of(lax.rem(head, 2) * HW, HW)
-            pack_refs[bits][:, :width] = xbf_ref[...]
-            pack_refs[bits][:, width:] = rest_ref[lax.div(head, 2), :, pl.ds(start, HW)]
+
+def long_gate_kernel(xbf_ref, pin_ref, cot_ref, gate_ref, slope_gate_ref, half_ref):
+    _, _, group = run_place()
+    part = xbf_ref.shape[1] // 4
+    act, slope = project(xbf_ref[...], pin_ref[...])
+    gate_ref[...] = act
+    slope_gate_ref[...] = slope.astype(BF16)
+    for block, features in split_rows(part, (1 - lax.rem(group, 2)) * part):
+        half_ref[:, block * part : (block + 1) * part] = cot_ref[:, features]
+        half_ref[:, (block + 2) * part : (block + 3) * part] = xbf_ref[:, features]
 
 
 def short_forward_kernel(
@@ -163,6 +141,7 @@
     grad_gate_ref,
     slope_ref,
     xbf_ref,
+    turned_ref,
     inv_ref,
     mine_ref,
     other_ref,
@@ -177,6 +156,7 @@
     normed, inv_std = norm_rows(x_ref[...].astype(F32))
     x_bf = normed.astype(BF16)
     xbf_ref[...] = x_bf
+    turned_ref[...] = x_bf.T
     inv_ref[...] = inv_std
     act, slope = project(x_bf, proj_ref[...])
     slope_ref[...] = slope.astype(BF16)
@@ -228,7 +208,7 @@
     @pl.when(step == 0)
     def _():
         sum_ref[:, :gates] = dot(cot_ref[...], gated, 0, 0)
-        sum_ref[:, gates:] = dot(xbf_ref[...], grad_gate_ref[...], 0, 0)
+        sum_ref[:, gates:] = dot(turned_ref[...], grad_gate_ref[...], 1, 0)
 
     @pl.when(step == 1)
     def _():
@@ -239,7 +219,7 @@
                 here = slice(block * part, (block + 1) * part)
                 total = sum_ref[features, :gates] + dot(cot_ref[:, features], gated, 0, 0)
                 target[here, :gates] = total.astype(BF16)
-                total = dot(xbf_ref[:, features], grad_gate_ref[...], 0, 0)
+                total = dot(turned_ref[features, :], grad_gate_ref[...], 1, 0)
                 target[here, gates:] = (sum_ref[features, gates:] + total).astype(BF16)
 
 
@@ -257,7 +237,7 @@
 
 
 def short_back_kernel(
-    user_ref, qkv_ref, g_ref, slope_ref, xbf_ref, grad_ref, mine_ref, other_ref, acc_ref, side_ref
+    user_ref, qkv_ref, g_ref, slope_ref, turned_ref, grad_ref, mine_ref, other_ref, acc_ref, side_ref
 ):
     joined = user_ref[0, 0] == user_ref[0, 1]
     half = BLOCK // 2
@@ -315,7 +295,7 @@
     core = lax.rem(lax.axis_index("dp"), 2)
     for target, side in ((mine_ref, core), (other_ref, 1 - core)):
         for block, features in split_rows(part, side * part):
-            total = dot(xbf_ref[:, features], grad_pre, 0, 0)
+            total = dot(turned_ref[features, :], grad_pre, 1, 0)
             target[block * part : (block + 1) * part] = total.astype(BF16)
 
 
@@ -352,8 +332,7 @@
 
 
 def long_back_kernel(blocks_smem, all_ref, g_ref, *refs):
-    pack_refs, sum_refs, grad_refs = refs[:H], refs[H : H + 2], refs[H + 2 : 2 * H + 2]
-    dq_ref, dk_ref, dv_ref, x_ref, pre_ref = refs[2 * H + 2 :]
+    grad_refs, (dq_ref, dk_ref, dv_ref) = refs[:H], refs[H:]
     mine, chunk, group = run_place()
     valid = blocks_smem[group]
     dq_ref[...] = jnp.zeros_like(dq_ref)
@@ -392,23 +371,12 @@
 
     coeff = 1.0 / (valid * BLOCK).astype(F32)
     rows = grad_refs[0].shape[0]
-    width = x_ref.shape[1]
     lanes = low_lanes((rows, 2 * KW))
     for bits in range(H):
         part = pl.ds(pl.multiple_of((mine ^ bits) * rows, rows), rows)
         pair = turned(jnp.where(lanes, dk_ref[part, :], dq_ref[part, :])) * HALF_SCALE
-        slope = pack_refs[bits][:, width:].astype(F32)
-        here = slice(bits * rows, (bits + 1) * rows)
-        pre_ref[here, : 2 * KW] = (pair * coeff * slope[:, : 2 * KW]).astype(BF16)
-        pre_ref[here, 2 * KW :] = (dv_ref[part, :] * coeff * slope[:, 2 * KW :]).astype(BF16)
-        grad_refs[bits][...] = pre_ref[here, :]
-        x_ref[here, :] = pack_refs[bits][:, :width]
-    part = sum_refs[0].shape[0] // 2
-    core = lax.rem(group, 2)
-    for target, side in zip(sum_refs, (core, 1 - core)):
-        for block, features in split_rows(part, side * part):
-            total = dot(x_ref[:, features], pre_ref[...], 0, 0)
-            target[block * part : (block + 1) * part] = total.astype(BF16)
+        grad_refs[bits][:, : 2 * KW] = (pair * coeff).astype(BF16)
+        grad_refs[bits][:, 2 * KW :] = (dv_ref[part, :] * coeff).astype(BF16)
 
 
 def long_head_kernel(
@@ -449,7 +417,7 @@
 
 
 def early_sums_kernel(
-    pack_ref, cot_ref, mid_ref, half_ref, mid_got, mine_ref, got_ref, sum_ref
+    xbf_ref, cot_ref, mid_ref, half_ref, mid_got, mine_ref, got_ref, sum_ref
 ):
     cols = mid_ref.shape[1] // 2
     part = sum_ref.shape[0] // 2
@@ -457,7 +425,7 @@
     mid = jnp.concatenate([mid_ref[...], mid_got[...]], axis=0)
     for block, features in split_rows(part, core * part):
         here = slice(block * part, (block + 1) * part)
-        for place, own in ((0, cot_ref), (1, pack_ref)):
+        for place, own in ((0, cot_ref), (1, xbf_ref)):
             start = (2 * place + block) * part
             rows = jnp.concatenate([own[:, features], half_ref[:, start : start + part]], axis=0)
             there = slice(place * cols, (place + 1) * cols)
@@ -465,14 +433,23 @@
             sum_ref[here, there] = (total + dot(rows, mid[:, there], 0, 0)).astype(BF16)
 
 
-def late_pair_sum_kernel(short_mine, short_got, long_mine, long_got, sum_ref):
+def long_slopes_kernel(got_0, got_1, got_2, got_3, slope_ref, grad_ref):
     mine, _, _ = run_place()
-    total = short_mine[...].astype(F32) + short_got[...].astype(F32)
-    sum_ref[...] = total.astype(BF16)
-    head = pl.ds(pl.multiple_of(mine * HW, HW), HW)
-    total = short_mine[:, head].astype(F32) + short_got[:, head].astype(F32)
-    total += long_mine[...].astype(F32) + long_got[...].astype(F32)
-    sum_ref[:, head] = total.astype(BF16)
+    for bits, got in enumerate((got_0, got_1, got_2, got_3)):
+        there = pl.ds(pl.multiple_of((mine ^ bits) * HW, HW), HW)
+        grads = got[...].astype(F32) * slope_ref[:, there].astype(F32)
+        grad_ref[:, there] = grads.astype(BF16)
+
+
+def late_sums_kernel(mine_ref, got_ref, xbf_ref, half_ref, grad_ref, grad_got, sum_ref):
+    part = sum_ref.shape[0]
+    core = lax.rem(lax.axis_index("dp"), 2)
+    start = (core + 2 * pl.program_id(0)) * part
+    features = pl.ds(pl.multiple_of(start, part), part)
+    rows = jnp.concatenate([xbf_ref[:, features], half_ref[...]], axis=0)
+    grads = jnp.concatenate([grad_ref[...], grad_got[...]], axis=0)
+    total = mine_ref[...].astype(F32) + got_ref[...].astype(F32)
+    sum_ref[...] = (total + dot(rows, grads, 0, 0)).astype(BF16)
 
 
 def final_sums_kernel(factor, early_ref, late_ref, in_ref, out_ref):
@@ -504,20 +481,15 @@
     inv_ref,
     pin_ref,
     proj_ref,
-    got_0,
-    got_1,
-    got_2,
-    got_3,
     long_gate_ref,
+    long_grad_ref,
     long_cot_ref,
-    pack_ref,
+    long_xbf_ref,
     long_inv_ref,
     back_ref,
     long_back_ref,
-    long_grad_ref,
 ):
     step = pl.program_id(0)
-    width = cot_ref.shape[1]
 
     def finish(gate, grad, cot, normed, inv, target):
         grad_norm = dot(gate[...], pin_ref[...], 1, 1) + dot(grad[...], proj_ref[...], 1, 1)
@@ -530,15 +502,11 @@
 
     @pl.when(step == 2)
     def _():
-        mine, _, _ = run_place()
-        for bits, got in enumerate((got_0, got_1, got_2, got_3)):
-            start = pl.multiple_of((mine ^ bits) * HW, HW)
-            long_grad_ref[:, pl.ds(start, HW)] = got[...]
         finish(
             long_gate_ref,
             long_grad_ref,
             long_cot_ref,
-            pack_ref[:, :width],
+            long_xbf_ref[...],
             long_inv_ref,
             long_back_ref,
         )
@@ -619,26 +587,22 @@
     half = width // 2
     chunks = sp_size // H
 
-    proj, sent, inv_long, gate_long, slope_long, half_other, *packs = call(
+    proj, sent, inv_long, xbf_long, slope_rest = call(
         long_project_kernel,
         (
             in_hbm((width, rest)),
             in_hbm((chunks, H, long_rows, HW)),
             in_hbm((long_rows, 1), F32),
-            in_hbm((long_rows, gates)),
-            in_hbm((long_rows, gates)),
             in_hbm((long_rows, width)),
-        )
-        + (in_hbm((long_rows, width + HW)),) * H,
-        2 * long_rows * width * cols,
-        10 * 2**20,
+            in_hbm((long_rows, rest)),
+        ),
+        2 * long_rows * width * rest,
+        8 * 2**20,
         "long_project",
         vmem=60,
         grid=(2,),
         in_specs=[
             fixed_spec(long_rows, width),
-            fixed_spec(long_rows, width),
-            cols_spec(width, gates // 2),
             pl.BlockSpec((width, 2 * KW), lambda step: (0, step + gates // (2 * KW))),
             pl.BlockSpec((width, 2 * KW), lambda step: (0, step + (gates + H * KW) // (2 * KW))),
             pl.BlockSpec((width, 2 * VW), lambda step: (0, step + (gates + 2 * H * KW) // (2 * VW))),
@@ -647,17 +611,33 @@
             cols_spec(width, rest // 2),
             pl.BlockSpec((chunks, 2, long_rows, HW), lambda step: (0, step, 0, 0)),
             fixed_spec(long_rows, 1),
-            cols_spec(long_rows, gates // 2),
-            cols_spec(long_rows, gates // 2),
             fixed_spec(long_rows, width),
-        ]
-        + [fixed_spec(long_rows, width + HW)] * H,
-        scratch_shapes=[
-            pltpu.VMEM((long_rows, width), BF16),
-            pltpu.VMEM((2, long_rows, rest // 2), BF16),
-        ],
-    )(x_long, cot_long, proj_in, proj_in, proj_in, proj_in)
+            cols_spec(long_rows, rest // 2),
+        ],
+    )(x_long, proj_in, proj_in, proj_in)
     whole = spread_heads(sent)
+    gate_long, slope_long, half_other = call(
+        long_gate_kernel,
+        (
+            shaped((long_rows, gates)),
+            shaped((long_rows, gates)),
+            in_hbm((long_rows, width)),
+        ),
+        2 * long_rows * width * gates,
+        4 * 2**20,
+        "long_gate",
+        grid=(1,),
+        in_specs=[
+            fixed_spec(long_rows, width),
+            fixed_spec(width, gates),
+            fixed_spec(long_rows, width),
+        ],
+        out_specs=[
+            fixed_spec(long_rows, gates),
+            fixed_spec(long_rows, gates),
+            fixed_spec(long_rows, width),
+        ],
+    )(xbf_long, proj_in, cot_long)
 
     short_out = call(
         short_forward_kernel,
@@ -668,6 +648,7 @@
             in_hbm((short_rows, gates)),
             in_hbm((short_rows, rest)),
             in_hbm((short_rows, width)),
+            in_hbm((width, short_rows)),
             in_hbm((short_rows, 1), F32),
             in_hbm((half, 2 * gates)),
             in_hbm((half, 2 * gates)),
@@ -692,6 +673,7 @@
             rows_spec(BLOCK, gates),
             rows_spec(BLOCK, rest),
             rows_spec(BLOCK, width),
+            cols_spec(width, BLOCK),
             rows_spec(BLOCK, 1),
             fixed_spec(half, 2 * gates),
             fixed_spec(half, 2 * gates),
@@ -703,9 +685,10 @@
             pltpu.VMEM((BLOCK, 2 * KW * H), BF16),
         ],
     )(short_user, x_short, cot_short, proj_in, proj, proj_out)
-    out_short, qkv_short, g_short, gate_short, slope_short, xbf_short, inv_short = short_out[:7]
-    early_mine, early_other = short_out[7:]
+    out_short, qkv_short, g_short, gate_short, slope_short, xbf_short = short_out[:6]
+    turned_short, inv_short, early_mine, early_other = short_out[6:]
     early_got = swap_cores(early_other)
+
 
     whole, early_got, out_short = lax.optimization_barrier((whole, early_got, out_short))
     mixed = call(
@@ -732,11 +715,8 @@
         in_specs=[WHOLE] * 9,
         scratch_shapes=[pltpu.VMEM((long_rows, gates), F32)],
     )(*swap_heads(mixed), x_long, cot_long, proj_out, gate_long, slope_long)
-    sent, qkv_short, mid, packs, half_other = lax.optimization_barrier(
-        (sent, qkv_short, mid, packs, half_other)
-    )
+    sent, qkv_short, mid, half_other = lax.optimization_barrier((sent, qkv_short, mid, half_other))
     all_g = spread_heads(sent)
-    packs = swap_heads(packs)
     half_got = swap_cores(half_other)
     mid_got = swap_cores(mid)
     grad_short, short_mine, short_other = call(
@@ -752,7 +732,7 @@
             cols_spec(short_rows, rest // 2),
             cols_spec(short_rows, gates // 2),
             cols_spec(short_rows, rest // 2),
-            fixed_spec(short_rows, width),
+            fixed_spec(width, short_rows),
         ],
         out_specs=[
             cols_spec(short_rows, rest // 2),
@@ -763,10 +743,8 @@
             pltpu.VMEM((short_rows, rest // 2), F32),
             pltpu.VMEM((BLOCK, rest // 4), BF16),
         ],
-    )(short_user, qkv_short, g_short, slope_short, xbf_short)
-    mid_got, half_got, packs, grad_short = lax.optimization_barrier(
-        (mid_got, half_got, packs, grad_short)
-    )
+    )(short_user, qkv_short, g_short, slope_short, turned_short)
+    mid_got, half_got, grad_short = lax.optimization_barrier((mid_got, half_got, grad_short))
     short_got = swap_cores(short_other)
     early = call(
         early_sums_kernel,
@@ -774,38 +752,48 @@
         8 * long_rows * half * gates,
         5 * 2**20,
         "early_sums",
-    )(packs[0], cot_long, mid, half_got, mid_got, early_mine, early_got)
+    )(xbf_long, cot_long, mid, half_got, mid_got, early_mine, early_got)
     all_g, early = lax.optimization_barrier((all_g, early))
     early = scatter_pairs(early)
 
-    long_mine, long_other, *grads = call(
+    grads = call(
         long_back_kernel,
-        (in_hbm((half, HW)),) * 2 + (shaped((long_rows, HW)),) * H,
-        7 * 10**9,
-        6 * 2**20,
+        (shaped((long_rows, HW)),) * H,
+        6 * 10**9,
+        4 * 2**20,
         "long_back",
-        in_specs=[SMEM] + [WHOLE] * (2 + H),
+        in_specs=[SMEM, WHOLE, WHOLE],
         scratch_shapes=[
             pltpu.VMEM((BLOCK, 2 * KW), F32),
             pltpu.VMEM((BLOCK, 2 * KW), F32),
             pltpu.VMEM((BLOCK, VW), F32),
-            pltpu.VMEM((BLOCK, width), BF16),
-            pltpu.VMEM((BLOCK, HW), BF16),
-        ],
-    )(long_blocks, whole, all_g, *packs)
-    grads = swap_heads(grads)
+        ],
+    )(long_blocks, whole, all_g)
+    grad_long = call(
+        long_slopes_kernel,
+        shaped((long_rows, rest)),
+        long_rows * rest,
+        2**20,
+        "long_slopes",
+    )(*swap_heads(grads), slope_rest)
     late = call(
-        late_pair_sum_kernel,
+        late_sums_kernel,
         in_hbm((half, rest)),
-        half * rest,
-        4 * 2**20,
-        "late_pair_sum",
-        vmem=60,
+        4 * long_rows * half * rest,
+        5 * 2**20,
+        "late_sums",
         grid=(2,),
-        in_specs=[rows_spec(half // 2, rest)] * 2 + [rows_spec(half // 2, HW)] * 2,
+        in_specs=[
+            rows_spec(half // 2, rest),
+            rows_spec(half // 2, rest),
+            fixed_spec(long_rows, width),
+            pl.BlockSpec((long_rows, half // 2), lambda step: (0, step + 2)),
+            fixed_spec(long_rows, rest),
+            fixed_spec(long_rows, rest),
+        ],
         out_specs=rows_spec(half // 2, rest),
-    )(short_mine, short_got, long_mine, swap_cores(long_other))
-    late, grads, gate_short = lax.optimization_barrier((late, grads, gate_short))
+    )(short_mine, short_got, xbf_long, half_got, grad_long, swap_cores(grad_long))
+    late, gate_short = lax.optimization_barrier((late, gate_short))
     late = scatter_pairs(late)
 
     def short_rows_spec(cols):
@@ -828,15 +816,14 @@
             fixed_spec(width, gates),
             fixed_spec(width, rest),
         ]
-        + [fixed_spec(long_rows, HW)] * H
         + [
             pl.BlockSpec((long_rows, gates), lambda step: (0, 1)),
+            fixed_spec(long_rows, rest),
             fixed_spec(long_rows, width),
-            fixed_spec(long_rows, width + HW),
+            fixed_spec(long_rows, width),
             fixed_spec(long_rows, 1),
         ],
         out_specs=[short_rows_spec(width), fixed_spec(long_rows, width)],
-        scratch_shapes=[pltpu.VMEM((long_rows, rest), BF16)],
     )(
         gate_short,
         grad_short,
@@ -845,10 +832,10 @@
         inv_short,
         proj_in,
         proj,
-        *grads,
         mid,
+        grad_long,
         cot_long,
-        packs[0],
+        xbf_long,
         inv_long,
     )
     total_rows = lax.axis_size("dp") * sp_size * (long_rows + short_rows)

time: 147 us -> 145 us (0.986)
  waiting for transfers between devices: 24.7 us -> 22.4 us
  local copies, waits for them, and re-layouts: 5.76 us -> 3.97 us
    all_to_all x2, starting transfers between devices: 16.5 us -> 21.6 us  [scatter_pairs(): lax.all_to_all(sent, ('dp', 'sp'), 0, 0, tiled=True, axis_index_groups=gr...]
    pallas_call x1, Pallas kernels: 13.6 us -> 17.2 us  [body(): call(short_back_kernel, (in_hbm((short_rows, rest)), in_hbm((half, rest))...]
    ppermute x9 -> x6, starting transfers between devices: 10.5 us -> 7.13 us  [swap_heads(): lax.ppermute(pieces[bits], 'sp', [(src, src ^ bits) for src in range(size)])]
    ppermute x9 -> x6, waiting for transfers between devices: 10.9 us -> 7.97 us  [swap_heads(): lax.ppermute(pieces[bits], 'sp', [(src, src ^ bits) for src in range(size)])]
    pallas_call x2 -> x4, Pallas kernels: 13 us -> 10.2 us  [the longest x1 6.47 us: body(): call(long_back_kernel, (shaped((long_rows, HW)),) * H, 6 * 10 ** 9, 4 * 2...]
    unnamed x42 -> x36, local copies, waits for them, and re-layouts: 5.76 us -> 3.97 us
    all_to_all x2, waiting for transfers between devices: 6.15 us -> 4.54 us  [spread_heads(): lax.all_to_all(sent.reshape(chunks * heads, rows, cols), 'sp', 0, 0, tile...]
    pallas_call x1, Pallas kernels: 20.1 us -> 21.7 us  [body(): call(short_forward_kernel, (in_hbm((short_rows, width)), in_hbm((short_ro...]
  transfers between devices with their start and end apart: 18 -> 15, of which waited for: 10 -> 8; matrix products, arithmetic and copies ran while one was open for 1% -> 1% of each run, Pallas kernels for 41% -> 43%
where the time goes in v2:
time: 145 us; the launch traced here: 144 us
  Pallas kernels  70 us (48%)
  starting transfers between devices  45.6 us (31%)
  waiting for transfers between devices  22.4 us (15%)
  local copies, waits for them, and re-layouts  3.97 us (3%)
    pallas_call x1, Pallas kernels, body(): call(short_forward_kernel, (in_hbm((short_rows, width)), in_hbm((short_ro...  21.7 us
    all_to_all x2, starting transfers between devices, scatter_pairs(): lax.all_to_all(sent, ('dp', 'sp'), 0, 0, tiled=True, axis_index_groups=gr...  21.6 us
    pallas_call x1, Pallas kernels, body(): call(short_back_kernel, (in_hbm((short_rows, rest)), in_hbm((half, rest))...  17.2 us
    all_to_all x2, starting transfers between devices, spread_heads(): lax.all_to_all(sent.reshape(chunks * heads, rows, cols), 'sp', 0, 0, tile...  15.8 us
    pallas_call x1, Pallas kernels, body(): call(input_back_kernel, (in_hbm((short_rows, width)), in_hbm((long_rows,...  11.2 us
    ppermute x6, waiting for transfers between devices, swap_heads(): lax.ppermute(pieces[bits], 'sp', [(src, src ^ bits) for src in range(size)])  7.97 us
    ppermute x6, starting transfers between devices, swap_heads(): lax.ppermute(pieces[bits], 'sp', [(src, src ^ bits) for src in range(size)])  7.13 us
    pallas_call x1, Pallas kernels, body(): call(long_back_kernel, (shaped((long_rows, HW)),) * H, 6 * 10 ** 9, 4 * 2...  6.47 us
  transfers between devices with their start and end apart: 15, of which 8 were waited for; matrix products, arithmetic and copies ran while one was open for 1% of the time, Pallas kernels for 43%

profile of v2, /device:TPU:0, one launch (start us, length us, event | category | flops | bytes accessed | tf_op | source)
XLA Modules:
  0.0 144.3 jit_solution(2754010326127670356)
XLA Ops:
  0.6 4.2 %long_project.1 = (bf16[1024,1024]{1,0:T(8,128)(2,1)}, bf16[8,4,128,256]{3,2,1,0:T(8,128)(2,1)}, f32[128,1]{1,0:T(8,128)}, bf16[128,1024]{1,0:T(8,128)(2,1)}, bf16[128,1024]{1,0:T(8,128)(2,1)}) custom-call(bf16[128,1024]{1,0:T(8,128)(2,1)} %x_ref.5, bf16[1024,1536]{1,0:T(8,128)(2,1)} %pin_ref.5, bf16[1024,1536]{1,0:T(8,128)(2,1)} %pin_ref.5, ...), custom_call_target="tpu_custom_call" | custom-call | flops 268435456 | bytes 8388608 | tf_op jit(solution)/shard_map/long_project/pallas_call | solution.py:590
  4.8 9.3 %all-to-all-start = ((bf16[32,128,256]{2,1,0:T(8,128)(2,1)}), bf16[32,128,256]{2,1,0:T(8,128)(2,1)S(1)}, u32[]{:S(2)}, u32[]{:S(2)}) async-start(bf16[32,128,256]{2,1,0:T(8,128)(2,1)} %bitcast.10), calls=%async_computation | async-start | bytes 4194304 | tf_op jit(solution)/shard_map/all_to_all | solution.py:560
  14.1 21.7 %short_forward.1 = (bf16[1024,1024]{1,0:T(8,128)(2,1)}, bf16[1024,1024]{1,0:T(8,128)(2,1)}, bf16[1024,512]{1,0:T(8,128)(2,1)}, bf16[1024,512]{1,0:T(8,128)(2,1)}...) custom-call(s32[1,2]{1,0:T(1,128)} %user_ref.3, ...), custom_call_target="tpu_custom_call" | custom-call | flops 20000000000 | bytes 25165824 | tf_op jit(solution)/shard_map/short_forward/pallas_call | solution.py:642
  35.9 2.9 %collective-permute-done.got_ref = bf16[512,1024]{1,0:T(8,128)(2,1)S(1)} collective-permute-done((bf16[512,1024]{1,0:T(8,128)(2,1)}, bf16[512,1024]{1,0:T(8,128)(2,1)S(1)}, u32[]{:S(2)}, u32[]{:S(2)}) %collective-permute-start) | collective-permute-done | bytes 1048608 | tf_op jit(solution)/shard_map/ppermute | solution.py:566
  38.8 1.0 copy-done.10
  39.8 4.5 %all-to-all-done = bf16[32,128,256]{2,1,0:T(8,128)(2,1)S(1)} async-done(((bf16[32,128,256]{2,1,0:T(8,128)(2,1)}), bf16[32,128,256]{2,1,0:T(8,128)(2,1)S(1)}, u32[]{:S(2)}, u32[]{:S(2)}) %all-to-all-start) | async-done | bytes 2097184 | tf_op jit(solution)/shard_map/all_to_all | solution.py:560
  44.3 1.3 copy-done.5
  45.6 1.6 %copy-done.6 = bf16[32,128,256]{2,1,0:T(8,128)(2,1)S(1)} copy-done((bf16[32,128,256]{2,1,0:T(8,128)(2,1)S(1)}, bf16[32,128,256]{2,1,0:T(8,128)(2,1)}, u32[]{:S(2)}) %copy-start.6) | copy-done | bytes 2097176
  47.2 1.2 long_attend.1
  48.5 0.4 collective-permute-start.2
  49.0 3.0 %collective-permute-start.3 = (bf16[128,128]{1,0:T(8,128)(2,1)S(1)}, bf16[128,128]{1,0:T(8,128)(2,1)S(1)}, u32[]{:S(2)}, u32[]{:S(2)}) collective-permute-start(bf16[128,128]{1,0:T(8,128)(2,1)S(1)} %get-tuple-element.64), channel_id=1, source_target_pairs={{0,3},{1,2},{2,1},{3,0},{4,7},{5,6},{6,5},{7,4},{8,11},{9,10},{10,... | collective-permute-start | bytes 98312 | tf_op jit(solution)/shard_map/ppermute | solution.py:553
  52.0 1.0 long_gate.1
  53.1 1.2 collective-permute-done.3.got_3
  54.3 2.1 %long_head.1 = (bf16[128,1024]{1,0:T(8,128)(2,1)}, bf16[8,4,128,128]{3,2,1,0:T(8,128)(2,1)}, bf16[128,1024]{1,0:T(8,128)(2,1)}) custom-call(bf16[128,128]{1,0:T(8,128)(2,1)S(1)} %get-tuple-element.61.got_0, bf16[128,128]{1,0:T(8,128)(2,1)S(1)} %collective-permute-done.1.got_1, bf16[128,128]{1,0:T(8,128)(2,1)S(1)} %collective-permute-done.2.got_2, ...), custom_call_target="tpu_custom_call" | custom-call | flops 268435456 | bytes 3145728 | tf_op jit(solution)/shard_map/long_head/pallas_call | solution.py:705
  56.3 6.5 %all-to-all-start.1 = ((bf16[32,128,128]{2,1,0:T(8,128)(2,1)}), bf16[32,128,128]{2,1,0:T(8,128)(2,1)}, u32[]{:S(2)}, u32[]{:S(2)}) async-start(bf16[32,128,128]{2,1,0:T(8,128)(2,1)} %bitcast.11), calls=%async_computation.1 | async-start | bytes 2097152 | tf_op jit(solution)/shard_map/all_to_all | solution.py:560
  63.0 0.5 collective-permute-start.5
  63.5 17.2 %short_back.1 = (bf16[1024,1024]{1,0:T(8,128)(2,1)}, bf16[512,1024]{1,0:T(8,128)(2,1)}, bf16[512,1024]{1,0:T(8,128)(2,1)}) custom-call(s32[1,2]{1,0:T(1,128)} %user_ref.3, bf16[1024,1024]{1,0:T(8,128)(2,1)} %get-tuple-element.74.qkv_ref, bf16[1024,512]{1,0:T(8,128)(2,1)} %get-tuple-element.75.g_ref, bf16[1024,1024]{1,0:T(8,128)(2,1)} %get-tuple-element.76.slope_ref, ...), custom_call_target="tpu_custom_call" | custom-call | flops 16000000000 | bytes 13631488 | tf_op jit(solution)/shard_map/short_back/pallas_call | solution.py:722
  80.8 1.5 %early_sums.1 = bf16[512,1024]{1,0:T(8,128)(2,1)} custom-call(bf16[128,1024]{1,0:T(8,128)(2,1)S(1)} %copy-done.3, bf16[128,1024]{1,0:T(8,128)(2,1)S(1)} %copy-done.1, bf16[128,1024]{1,0:T(8,128)(2,1)S(1)} %copy-done.8, bf16[128,1024]{1,0:T(8,128)(2,1)S(1)} %collective-permute-done.6.half_ref, bf16[128,1024]{1,0:T(8,128)(2,1)S(1)} %collective-permute-done.5.mid_got, ...), custom_call_target="tpu_custom_call" | custom-call | flops 268435456 | bytes 5242880 | tf_op jit(solution)/shard_map/early_sums/pallas_call | solution.py:749
  82.2 11.9 %all-to-all-start.2 = ((bf16[64,8,1024]{2,1,0:T(8,128)(2,1)}), bf16[64,8,1024]{2,1,0:T(8,128)(2,1)}, u32[]{:S(2)}, u32[]{:S(2)}) async-start(bf16[64,8,1024]{2,1,0:T(8,128)(2,1)} %bitcast.8), calls=%async_computation.2 | async-start | bytes 2097152 | tf_op jit(solution)/shard_map/all_to_all | solution.py:577
  94.2 6.5 %long_back.1 = (bf16[128,256]{1,0:T(8,128)(2,1)S(1)}, bf16[128,256]{1,0:T(8,128)(2,1)S(1)}, bf16[128,256]{1,0:T(8,128)(2,1)S(1)}, bf16[128,256]{1,0:T(8,128)(2,1)S(1)}) custom-call(s32[4]{0:T(128)S(1)} %copy-done.16, bf16[4096,256]{1,0:T(8,128)(2,1)S(1)} %bitcast.7, bf16[4096,128]{1,0:T(8,128)(2,1)} %bitcast.3.g_ref), custom_call_target="tpu_custom_call" | custom-call | flops 6000000000 | bytes 4194304 | tf_op jit(solution)/shard_map/long_back/pallas_call | solution.py:759
  100.6 1.6 %collective-permute-start.7 = (bf16[128,256]{1,0:T(8,128)(2,1)S(1)}, bf16[128,256]{1,0:T(8,128)(2,1)S(1)}, u32[]{:S(2)}, u32[]{:S(2)}) collective-permute-start(bf16[128,256]{1,0:T(8,128)(2,1)S(1)} %get-tuple-element.90), channel_id=1, source_target_pairs={{0,1},{1,0},{2,3},{3,2},{4,5},{5,4},{6,7},{7,6},{8,9},{9,8},{10,11... | collective-permute-start | bytes 196616 | tf_op jit(solution)/shard_map/ppermute | solution.py:553
  102.2 1.5 %collective-permute-start.8 = (bf16[128,256]{1,0:T(8,128)(2,1)S(1)}, bf16[128,256]{1,0:T(8,128)(2,1)S(1)}, u32[]{:S(2)}, u32[]{:S(2)}) collective-permute-start(bf16[128,256]{1,0:T(8,128)(2,1)S(1)} %get-tuple-element.91), channel_id=1, source_target_pairs={{0,2},{1,3},{2,0},{3,1},{4,6},{5,7},{6,4},{7,5},{8,10},{9,11},{10,... | collective-permute-start | bytes 196616 | tf_op jit(solution)/shard_map/ppermute | solution.py:553
  103.7 0.5 collective-permute-start.9
  104.2 4.9 %collective-permute-done.7.got_1 = bf16[128,256]{1,0:T(8,128)(2,1)S(1)} collective-permute-done((bf16[128,256]{1,0:T(8,128)(2,1)S(1)}, bf16[128,256]{1,0:T(8,128)(2,1)S(1)}, u32[]{:S(2)}, u32[]{:S(2)}) %collective-permute-start.7) | collective-permute-done | bytes 65568 | tf_op jit(solution)/shard_map/ppermute | solution.py:553
  109.3 1.7 %collective-permute-done.9.got_3 = bf16[128,256]{1,0:T(8,128)(2,1)S(1)} collective-permute-done((bf16[128,256]{1,0:T(8,128)(2,1)S(1)}, bf16[128,256]{1,0:T(8,128)(2,1)S(1)}, u32[]{:S(2)}, u32[]{:S(2)}) %collective-permute-start.9) | collective-permute-done | bytes 65568 | tf_op jit(solution)/shard_map/ppermute | solution.py:553
  111.5 1.2 collective-permute-done.10.grad_got
  112.7 2.6 %late_sums.1 = bf16[512,1024]{1,0:T(8,128)(2,1)} custom-call(bf16[512,1024]{1,0:T(8,128)(2,1)S(1)} %copy-done.14, bf16[512,1024]{1,0:T(8,128)(2,1)} %collective-permute-done.4.got_ref, bf16[128,1024]{1,0:T(8,128)(2,1)S(1)} %copy-done.3, bf16[128,1024]{1,0:T(8,128)(2,1)S(1)} %collective-permute-done.6.half_ref, ...), custom_call_target="tpu_custom_call" | custom-call | flops 268435456 | bytes 5242880 | tf_op jit(solution)/shard_map/late_sums/pallas_call | solution.py:779
  115.4 9.7 %all-to-all-start.3 = ((bf16[64,8,1024]{2,1,0:T(8,128)(2,1)}), bf16[64,8,1024]{2,1,0:T(8,128)(2,1)S(1)}, u32[]{:S(2)}, u32[]{:S(2)}) async-start(bf16[64,8,1024]{2,1,0:T(8,128)(2,1)} %bitcast.9), calls=%async_computation.3 | async-start | bytes 2097152 | tf_op jit(solution)/shard_map/all_to_all | solution.py:577
  125.0 11.2 %input_back.1 = (bf16[1024,1024]{1,0:T(8,128)(2,1)}, bf16[128,1024]{1,0:T(8,128)(2,1)}) custom-call(bf16[1024,512]{1,0:T(8,128)(2,1)} %get-tuple-element.95.grad_gate_ref, bf16[1024,1024]{1,0:T(8,128)(2,1)} %get-tuple-element.96.grad_ref, bf16[1024,1024]{1,0:T(8,128)(2,1)} %cot_ref.9, bf16[1024,1024]{1,0:T(8,128)(2,1)} %get-tuple-element.97.xbf_ref, ...), custom_call_target="tpu_custom_call" | custom-call | flops 3623878656 | bytes 14680064 | tf_op jit(solution)/shard_map/input_back/pallas_call | solution.py:802
  136.2 1.4 convert_reduce_fusion.early_ref
  137.6 5.8 %all-to-all-done.3.late_ref = bf16[64,8,1024]{2,1,0:T(8,128)(2,1)S(1)} async-done(((bf16[64,8,1024]{2,1,0:T(8,128)(2,1)}), bf16[64,8,1024]{2,1,0:T(8,128)(2,1)S(1)}, u32[]{:S(2)}, u32[]{:S(2)}) %all-to-all-start.3) | async-done | bytes 1048608 | tf_op jit(solution)/shard_map/all_to_all | solution.py:577
  143.4 0.9 final_sums.1
  (47 shorter events, 1.2 us)
Async XLA Ops:
  4.8 39.5 %all-to-all-start = ((bf16[32,128,256]{2,1,0:T(8,128)(2,1)}), bf16[32,128,256]{2,1,0:T(8,128)(2,1)S(1)}, u32[]{:S(2)}, u32[]{:S(2)}) async-start(bf16[32,128,256]{2,1,0:T(8,128)(2,1)} %bitcast.10), calls=%async_computation | async-start | bytes 4194304 | tf_op jit(solution)/shard_map/all_to_all | solution.py:560
  14.1 31.5 %copy-start.16 = (s32[4]{0:T(128)S(1)}, s32[4]{0:T(128)}, u32[]{:S(2)}) copy-start(s32[4]{0:T(128)} %blocks_smem.3) | copy-start | bytes 52
  35.8 3.0 %collective-permute-start = (bf16[512,1024]{1,0:T(8,128)(2,1)}, bf16[512,1024]{1,0:T(8,128)(2,1)S(1)}, u32[]{:S(2)}, u32[]{:S(2)}) collective-permute-start(bf16[512,1024]{1,0:T(8,128)(2,1)} %get-tuple-element.58), channel_id=1, source_target_pairs={{0,32},{32,0},{64,96},{96,64},{1,33},{33,1},{65,97},{97,65},{2,34}... | collective-permute-start | bytes 3145736 | tf_op jit(solution)/shard_map/ppermute | solution.py:566
  44.3 1.3 copy-start.5
  45.6 1.6 %copy-start.6 = (bf16[32,128,256]{2,1,0:T(8,128)(2,1)S(1)}, bf16[32,128,256]{2,1,0:T(8,128)(2,1)}, u32[]{:S(2)}) copy-start(bf16[32,128,256]{2,1,0:T(8,128)(2,1)} %copy-done.5) | copy-start | bytes 6291460
  47.2 4.8 %copy-start = (bf16[1024,1536]{1,0:T(8,128)(2,1)S(1)}, bf16[1024,1536]{1,0:T(8,128)(2,1)}, u32[]{:S(2)}) copy-start(bf16[1024,1536]{1,0:T(8,128)(2,1)} %pin_ref.5) | copy-start | bytes 9437188
  47.2 4.8 %copy-start.1 = (bf16[128,1024]{1,0:T(8,128)(2,1)S(1)}, bf16[128,1024]{1,0:T(8,128)(2,1)}, u32[]{:S(2)}) copy-start(bf16[128,1024]{1,0:T(8,128)(2,1)} %long_cot_ref.1) | copy-start | bytes 786436
  47.2 4.8 %copy-start.2 = (bf16[128,1024]{1,0:T(8,128)(2,1)S(1)}, bf16[128,1024]{1,0:T(8,128)(2,1)}, u32[]{:S(2)}) copy-start(bf16[128,1024]{1,0:T(8,128)(2,1)} %get-tuple-element.65.xbf_ref.long_xbf_ref) | copy-start | bytes 786436
  48.4 5.8 %copy-start.12 = (bf16[128,1024]{1,0:T(8,128)(2,1)S(1)}, bf16[128,1024]{1,0:T(8,128)(2,1)}, u32[]{:S(2)}) copy-start(bf16[128,1024]{1,0:T(8,128)(2,1)} %x_ref.5) | copy-start | bytes 786436
  48.4 5.8 %copy-start.13 = (bf16[512,1024]{1,0:T(8,128)(2,1)S(1)}, bf16[512,1024]{1,0:T(8,128)(2,1)}, u32[]{:S(2)}) copy-start(bf16[512,1024]{1,0:T(8,128)(2,1)} %pout_ref.3) | copy-start | bytes 3145732
  48.4 4.6 %collective-permute-start.1 = (bf16[128,128]{1,0:T(8,128)(2,1)S(1)}, bf16[128,128]{1,0:T(8,128)(2,1)S(1)}, u32[]{:S(2)}, u32[]{:S(2)}) collective-permute-start(bf16[128,128]{1,0:T(8,128)(2,1)S(1)} %get-tuple-element.62), channel_id=1, source_target_pairs={{0,1},{1,0},{2,3},{3,2},{4,5},{5,4},{6,7},{7,6},{8,9},{9,8},{10,11... | collective-permute-start | bytes 98312 | tf_op jit(solution)/shard_map/ppermute | solution.py:553
  48.5 4.5 %collective-permute-start.2 = (bf16[128,128]{1,0:T(8,128)(2,1)S(1)}, bf16[128,128]{1,0:T(8,128)(2,1)S(1)}, u32[]{:S(2)}, u32[]{:S(2)}) collective-permute-start(bf16[128,128]{1,0:T(8,128)(2,1)S(1)} %get-tuple-element.63), channel_id=1, source_target_pairs={{0,2},{1,3},{2,0},{3,1},{4,6},{5,7},{6,4},{7,5},{8,10},{9,11},{10,... | collective-permute-start | bytes 98312 | tf_op jit(solution)/shard_map/ppermute | solution.py:553
  49.0 5.3 %collective-permute-start.3 = (bf16[128,128]{1,0:T(8,128)(2,1)S(1)}, bf16[128,128]{1,0:T(8,128)(2,1)S(1)}, u32[]{:S(2)}, u32[]{:S(2)}) collective-permute-start(bf16[128,128]{1,0:T(8,128)(2,1)S(1)} %get-tuple-element.64), channel_id=1, source_target_pairs={{0,3},{1,2},{2,1},{3,0},{4,7},{5,6},{6,5},{7,4},{8,11},{9,10},{10,... | collective-permute-start | bytes 98312 | tf_op jit(solution)/shard_map/ppermute | solution.py:553
  53.1 9.8 %copy-start.17 = (bf16[128,1024]{1,0:T(8,128)(2,1)S(1)}, bf16[128,1024]{1,0:T(8,128)(2,1)}, u32[]{:S(2)}) copy-start(bf16[128,1024]{1,0:T(8,128)(2,1)} %get-tuple-element.81) | copy-start | bytes 786436
  56.3 6.6 %copy-start.8 = (bf16[128,1024]{1,0:T(8,128)(2,1)S(1)}, bf16[128,1024]{1,0:T(8,128)(2,1)}, u32[]{:S(2)}) copy-start(bf16[128,1024]{1,0:T(8,128)(2,1)} %get-tuple-element.80.mid_ref.long_gate_ref) | copy-start | bytes 786436
  56.3 25.9 %all-to-all-start.1 = ((bf16[32,128,128]{2,1,0:T(8,128)(2,1)}), bf16[32,128,128]{2,1,0:T(8,128)(2,1)}, u32[]{:S(2)}, u32[]{:S(2)}) async-start(bf16[32,128,128]{2,1,0:T(8,128)(2,1)} %bitcast.11), calls=%async_computation.1 | async-start | bytes 2097152 | tf_op jit(solution)/shard_map/all_to_all | solution.py:560
  62.9 17.9 %collective-permute-start.6 = (bf16[128,1024]{1,0:T(8,128)(2,1)S(1)}, bf16[128,1024]{1,0:T(8,128)(2,1)S(1)}, u32[]{:S(2)}, u32[]{:S(2)}) collective-permute-start(bf16[128,1024]{1,0:T(8,128)(2,1)S(1)} %copy-done.17), channel_id=1, source_target_pairs={{0,32},{32,0},{64,96},{96,64},{1,33},{33,1},{65,97},{97,65},{2,34}... | collective-permute-start | bytes 786440 | tf_op jit(solution)/shard_map/ppermute | solution.py:566
  63.0 17.8 %collective-permute-start.5 = (bf16[128,1024]{1,0:T(8,128)(2,1)S(1)}, bf16[128,1024]{1,0:T(8,128)(2,1)S(1)}, u32[]{:S(2)}, u32[]{:S(2)}) collective-permute-start(bf16[128,1024]{1,0:T(8,128)(2,1)S(1)} %copy-done.8), channel_id=1, source_target_pairs={{0,32},{32,0},{64,96},{96,64},{1,33},{33,1},{65,97},{97,65},{2,34}... | collective-permute-start | bytes 786440 | tf_op jit(solution)/shard_map/ppermute | solution.py:566
  63.4 17.3 %copy-start.3 = (bf16[128,1024]{1,0:T(8,128)(2,1)S(1)}, bf16[128,1024]{1,0:T(8,128)(2,1)}, u32[]{:S(2)}) copy-start(bf16[128,1024]{1,0:T(8,128)(2,1)} %get-tuple-element.65.xbf_ref.long_xbf_ref) | copy-start | bytes 786436
  63.5 17.3 %copy-start.9 = (bf16[512,1024]{1,0:T(8,128)(2,1)S(1)}, bf16[512,1024]{1,0:T(8,128)(2,1)}, u32[]{:S(2)}) copy-start(bf16[512,1024]{1,0:T(8,128)(2,1)} %get-tuple-element.86.mine_ref) | copy-start | bytes 3145732
  63.5 17.3 %copy-start.11 = (bf16[512,1024]{1,0:T(8,128)(2,1)S(1)}, bf16[512,1024]{1,0:T(8,128)(2,1)}, u32[]{:S(2)}) copy-start(bf16[512,1024]{1,0:T(8,128)(2,1)} %copy-done.10) | copy-start | bytes 3145732
  80.6 30.9 %collective-permute-start.4 = (bf16[512,1024]{1,0:T(8,128)(2,1)}, bf16[512,1024]{1,0:T(8,128)(2,1)}, u32[]{:S(2)}, u32[]{:S(2)}) collective-permute-start(bf16[512,1024]{1,0:T(8,128)(2,1)} %get-tuple-element.79), channel_id=1, source_target_pairs={{0,32},{32,0},{64,96},{96,64},{1,33},{33,1},{65,97},{97,65},{2,34}... | collective-permute-start | bytes 3145736 | tf_op jit(solution)/shard_map/ppermute | solution.py:566
  82.2 11.9 %copy-start.7 = (bf16[32,128,256]{2,1,0:T(8,128)(2,1)S(1)}, bf16[32,128,256]{2,1,0:T(8,128)(2,1)}, u32[]{:S(2)}) copy-start(bf16[32,128,256]{2,1,0:T(8,128)(2,1)} %copy-done.5) | copy-start | bytes 6291460
  82.2 33.1 %all-to-all-start.2 = ((bf16[64,8,1024]{2,1,0:T(8,128)(2,1)}), bf16[64,8,1024]{2,1,0:T(8,128)(2,1)}, u32[]{:S(2)}, u32[]{:S(2)}) async-start(bf16[64,8,1024]{2,1,0:T(8,128)(2,1)} %bitcast.8), calls=%async_computation.2 | async-start | bytes 2097152 | tf_op jit(solution)/shard_map/all_to_all | solution.py:577
  94.1 16.9 %copy-start.15 = (bf16[128,1024]{1,0:T(8,128)(2,1)S(1)}, bf16[128,1024]{1,0:T(8,128)(2,1)}, u32[]{:S(2)}) copy-start(bf16[128,1024]{1,0:T(8,128)(2,1)} %get-tuple-element.93.slope_ref) | copy-start | bytes 786436
  94.2 18.6 %copy-start.14 = (bf16[512,1024]{1,0:T(8,128)(2,1)S(1)}, bf16[512,1024]{1,0:T(8,128)(2,1)}, u32[]{:S(2)}) copy-start(bf16[512,1024]{1,0:T(8,128)(2,1)} %get-tuple-element.78.mine_ref) | copy-start | bytes 3145732
  100.6 8.5 %collective-permute-start.7 = (bf16[128,256]{1,0:T(8,128)(2,1)S(1)}, bf16[128,256]{1,0:T(8,128)(2,1)S(1)}, u32[]{:S(2)}, u32[]{:S(2)}) collective-permute-start(bf16[128,256]{1,0:T(8,128)(2,1)S(1)} %get-tuple-element.90), channel_id=1, source_target_pairs={{0,1},{1,0},{2,3},{3,2},{4,5},{5,4},{6,7},{7,6},{8,9},{9,8},{10,11... | collective-permute-start | bytes 196616 | tf_op jit(solution)/shard_map/ppermute | solution.py:553
  102.2 7.1 %collective-permute-start.8 = (bf16[128,256]{1,0:T(8,128)(2,1)S(1)}, bf16[128,256]{1,0:T(8,128)(2,1)S(1)}, u32[]{:S(2)}, u32[]{:S(2)}) collective-permute-start(bf16[128,256]{1,0:T(8,128)(2,1)S(1)} %get-tuple-element.91), channel_id=1, source_target_pairs={{0,2},{1,3},{2,0},{3,1},{4,6},{5,7},{6,4},{7,5},{8,10},{9,11},{10,... | collective-permute-start | bytes 196616 | tf_op jit(solution)/shard_map/ppermute | solution.py:553
  103.7 7.3 %collective-permute-start.9 = (bf16[128,256]{1,0:T(8,128)(2,1)S(1)}, bf16[128,256]{1,0:T(8,128)(2,1)S(1)}, u32[]{:S(2)}, u32[]{:S(2)}) collective-permute-start(bf16[128,256]{1,0:T(8,128)(2,1)S(1)} %get-tuple-element.92), channel_id=1, source_target_pairs={{0,3},{1,2},{2,1},{3,0},{4,7},{5,6},{6,5},{7,4},{8,11},{9,10},{10,... | collective-permute-start | bytes 196616 | tf_op jit(solution)/shard_map/ppermute | solution.py:553
  111.1 4.3 %copy-start.4 = (bf16[128,1024]{1,0:T(8,128)(2,1)}, bf16[128,1024]{1,0:T(8,128)(2,1)S(1)}, u32[]{:S(2)}) copy-start(bf16[128,1024]{1,0:T(8,128)(2,1)S(1)} %long_slopes.1.grad_ref.long_grad_ref) | copy-start | bytes 786436
  111.1 1.6 %collective-permute-start.10 = (bf16[128,1024]{1,0:T(8,128)(2,1)S(1)}, bf16[128,1024]{1,0:T(8,128)(2,1)S(1)}, u32[]{:S(2)}, u32[]{:S(2)}) collective-permute-start(bf16[128,1024]{1,0:T(8,128)(2,1)S(1)} %long_slopes.1.grad_ref.long_grad_ref), channel_id=1, source_target_pairs={{0,32},{32,0},{64,96},{96,64},{1,33},{33,1},{65,97},{97,65},{2,34}... | collective-permute-start | bytes 786440 | tf_op jit(solution)/shard_map/ppermute | solution.py:566
  115.4 28.0 %all-to-all-start.3 = ((bf16[64,8,1024]{2,1,0:T(8,128)(2,1)}), bf16[64,8,1024]{2,1,0:T(8,128)(2,1)S(1)}, u32[]{:S(2)}, u32[]{:S(2)}) async-start(bf16[64,8,1024]{2,1,0:T(8,128)(2,1)} %bitcast.9), calls=%async_computation.3 | async-start | bytes 2097152 | tf_op jit(solution)/shard_map/all_to_all | solution.py:577
  (1 other events, 1.0 us)

commit v3 on v2

--- a/solution.py
+++ b/solution.py
@@ -126,6 +126,25 @@
     for block, features in split_rows(part, (1 - lax.rem(group, 2)) * part):
         half_ref[:, block * part : (block + 1) * part] = cot_ref[:, features]
         half_ref[:, (block + 2) * part : (block + 3) * part] = xbf_ref[:, features]
+
+
+def head_lanes(which):
+    first = pl.multiple_of(which * HW, HW)
+    last = pl.multiple_of(which * HW + 2 * KW, VW)
+    return pl.ds(first, 2 * KW), pl.ds(last, VW), pl.ds(pl.multiple_of(which * VW, VW), VW)
+
+
+def back_block(query_side, query_qk, key_qk, values, g_rows, mask):
+    act, slope = silu_both(dot(key_qk, query_side, 1, 1))
+    slopes = dot(values, g_rows, 1, 1) * slope
+    if mask is not None:
+        act = jnp.where(mask, act, 0.0)
+        slopes = jnp.where(mask, slopes, 0.0)
+    slopes = slopes.astype(BF16)
+    grad_q = dot(slopes, key_qk, 0, 0)
+    grad_k = dot(slopes, query_qk, 1, 0)
+    grad_v = dot(act.astype(BF16), g_rows, 1, 0)
+    return grad_q, grad_k, grad_v
 
 
 def short_forward_kernel(
@@ -145,6 +164,7 @@
     inv_ref,
     mine_ref,
     other_ref,
+    join_ref,
     sum_ref,
     seen_ref,
     mixed_ref,
@@ -180,13 +200,12 @@
 
     @pl.when(jnp.logical_and(step == 1, joined))
     def _():
-        for which in range(H):
-            first = HW * which
-            side = side_ref[:, 2 * KW * which : 2 * KW * (which + 1)]
-            scores = dot(side, seen_ref[:, first : first + 2 * KW], 1, 1)
-            mixed_ref[:, VW * which : VW * (which + 1)] += dot(
-                silu_half(scores).astype(BF16), seen_ref[:, first + 2 * KW : first + HW], 1, 0
-            )
+        @pl.loop(0, H)
+        def _(which):
+            pair, rest, narrow = head_lanes(which)
+            scores = dot(side_ref[:, narrow], seen_ref[:, pair], 1, 1)
+            weights = silu_half(scores).astype(BF16)
+            mixed_ref[:, narrow] += dot(weights, seen_ref[:, rest], 1, 0)
 
     @pl.when(step == 0)
     def _():
@@ -205,6 +224,26 @@
     g_ref[...] = (grad_mixed.astype(BF16).astype(F32) * share).astype(BF16)
     gates = gated.shape[1]
 
+    @pl.when(jnp.logical_and(step == 1, joined))
+    def _():
+        lanes = low_lanes((BLOCK, 2 * KW))
+
+        @pl.loop(0, H)
+        def _(which):
+            pair, rest, narrow = head_lanes(which)
+            grad_q, grad_k, grad_v = back_block(
+                side_ref[:, narrow],
+                qkv_ref[:, pair],
+                seen_ref[:, pair],
+                seen_ref[:, rest],
+                g_ref[:, narrow],
+                None,
+            )
+            join_ref[:BLOCK, pair] = jnp.where(lanes, grad_k, 0.0).astype(BF16)
+            join_ref[:BLOCK, rest] = grad_v.astype(BF16)
+            join_ref[BLOCK:, pair] = jnp.where(lanes, 0.0, grad_q).astype(BF16)
+            join_ref[BLOCK:, rest] = jnp.zeros(grad_v.shape, BF16)
+
     @pl.when(step == 0)
     def _():
         sum_ref[:, :gates] = dot(cot_ref[...], gated, 0, 0)
@@ -223,21 +262,8 @@
                 target[here, gates:] = (sum_ref[features, gates:] + total).astype(BF16)
 
 
-def back_block(query_side, query_qk, key_qk, values, g_rows, mask):
-    act, slope = silu_both(dot(key_qk, query_side, 1, 1))
-    slopes = dot(values, g_rows, 1, 1) * slope
-    if mask is not None:
-        act = jnp.where(mask, act, 0.0)
-        slopes = jnp.where(mask, slopes, 0.0)
-    slopes = slopes.astype(BF16)
-    grad_q = dot(slopes, key_qk, 0, 0)
-    grad_k = dot(slopes, query_qk, 1, 0)
-    grad_v = dot(act.astype(BF16), g_rows, 1, 0)
-    return grad_q, grad_k, grad_v
-
-
 def short_back_kernel(
-    user_ref, qkv_ref, g_ref, slope_ref, turned_ref, grad_ref, mine_ref, other_ref, acc_ref, side_ref
+    user_ref, qkv_ref, g_ref, slope_ref, turned_ref, join_ref, grad_ref, mine_ref, other_ref, acc_ref
 ):
     joined = user_ref[0, 0] == user_ref[0, 1]
     half = BLOCK // 2
@@ -263,26 +289,10 @@
             acc_ref[end, first : first + 2 * KW] = jnp.where(lanes, dk_two, dq_one[half:] + dq_two)
             acc_ref[top, first + 2 * KW : first + HW] = dv_one
             acc_ref[end, first + 2 * KW : first + HW] = dv_two
-        side_ref[:, 2 * KW * which : 2 * KW * (which + 1)] = side[BLOCK:]
 
     @pl.when(joined)
     def _():
-        one, two = slice(0, BLOCK), slice(BLOCK, 2 * BLOCK)
-        for which in heads:
-            first = HW * which
-            pair = slice(first, first + 2 * KW)
-            grad_q, grad_k, grad_v = back_block(
-                side_ref[:, 2 * KW * which : 2 * KW * (which + 1)],
-                qkv_ref[two, pair],
-                qkv_ref[one, pair],
-                qkv_ref[one, first + 2 * KW : first + HW],
-                g_ref[two, VW * which : VW * (which + 1)],
-                None,
-            )
-            lanes = low_lanes((BLOCK, 2 * KW))
-            acc_ref[one, pair] += jnp.where(lanes, grad_k, 0.0)
-            acc_ref[two, pair] += jnp.where(lanes, 0.0, grad_q)
-            acc_ref[one, first + 2 * KW : first + HW] += grad_v
+        acc_ref[...] += join_ref[...].astype(F32)
 
     for which in heads:
         first = HW * which
@@ -626,6 +636,7 @@
         2 * long_rows * width * gates,
         4 * 2**20,
         "long_gate",
+        vmem=60,
         grid=(1,),
         in_specs=[
             fixed_spec(long_rows, width),
@@ -652,6 +663,7 @@
             in_hbm((short_rows, 1), F32),
             in_hbm((half, 2 * gates)),
             in_hbm((half, 2 * gates)),
+            in_hbm((short_rows, rest)),
         ),
         20 * 10**9,
         24 * 2**20,
@@ -677,6 +689,7 @@
             rows_spec(BLOCK, 1),
             fixed_spec(half, 2 * gates),
             fixed_spec(half, 2 * gates),
+            fixed_spec(short_rows, rest),
         ],
         scratch_shapes=[
             pltpu.VMEM((width, 2 * gates), F32),
@@ -686,17 +699,16 @@
         ],
     )(short_user, x_short, cot_short, proj_in, proj, proj_out)
     out_short, qkv_short, g_short, gate_short, slope_short, xbf_short = short_out[:6]
-    turned_short, inv_short, early_mine, early_other = short_out[6:]
-    early_got = swap_cores(early_other)
-
-
-    whole, early_got, out_short = lax.optimization_barrier((whole, early_got, out_short))
+    turned_short, inv_short, early_mine, early_other, join_short = short_out[6:]
+
+    whole, out_short = lax.optimization_barrier((whole, out_short))
     mixed = call(
         long_attend_kernel,
         (shaped((long_rows, VW)),) * H,
         2 * 10**9,
         2 * 2**20,
         "long_attend",
+        vmem=62,
         in_specs=[SMEM, WHOLE],
         scratch_shapes=[
             pltpu.VMEM((BLOCK, VW), F32),
@@ -712,12 +724,16 @@
         4 * long_rows * width * gates,
         3 * 2**20,
         "long_head",
+        vmem=60,
         in_specs=[WHOLE] * 9,
         scratch_shapes=[pltpu.VMEM((long_rows, gates), F32)],
     )(*swap_heads(mixed), x_long, cot_long, proj_out, gate_long, slope_long)
-    sent, qkv_short, mid, half_other = lax.optimization_barrier((sent, qkv_short, mid, half_other))
+    sent, qkv_short, mid, half_other, early_other = lax.optimization_barrier(
+        (sent, qkv_short, mid, half_other, early_other)
+    )
     all_g = spread_heads(sent)
     half_got = swap_cores(half_other)
+    early_got = swap_cores(early_other)
     mid_got = swap_cores(mid)
     grad_short, short_mine, short_other = call(
         short_back_kernel,
@@ -725,7 +741,7 @@
         16 * 10**9,
         13 * 2**20,
         "short_back",
-        vmem=56,
+        vmem=58,
         grid=(2,),
         in_specs=[
             SMEM,
@@ -733,6 +749,7 @@
             cols_spec(short_rows, gates // 2),
             cols_spec(short_rows, rest // 2),
             fixed_spec(width, short_rows),
+            cols_spec(short_rows, rest // 2),
         ],
         out_specs=[
             cols_spec(short_rows, rest // 2),
@@ -741,10 +758,11 @@
         ],
         scratch_shapes=[
             pltpu.VMEM((short_rows, rest // 2), F32),
-            pltpu.VMEM((BLOCK, rest // 4), BF16),
-        ],
-    )(short_user, qkv_short, g_short, slope_short, turned_short)
-    mid_got, half_got, grad_short = lax.optimization_barrier((mid_got, half_got, grad_short))
+        ],
+    )(short_user, qkv_short, g_short, slope_short, turned_short, join_short)
+    mid_got, half_got, early_got, grad_short = lax.optimization_barrier(
+        (mid_got, half_got, early_got, grad_short)
+    )
     short_got = swap_cores(short_other)
     early = call(
         early_sums_kernel,
@@ -762,6 +780,7 @@
         6 * 10**9,
         4 * 2**20,
         "long_back",
+        vmem=62,
         in_specs=[SMEM, WHOLE, WHOLE],
         scratch_shapes=[
             pltpu.VMEM((BLOCK, 2 * KW), F32),

time: 145 us -> 147 us (1.014)
  Pallas kernels: 70 us -> 74.1 us
    all_to_all x2, waiting for transfers between devices: 4.54 us -> 9.16 us  [spread_heads(): lax.all_to_all(sent.reshape(chunks * heads, rows, cols), 'sp', 0, 0, tile...]
    pallas_call x1, Pallas kernels: 6.47 us -> 10 us  [body(): call(long_back_kernel, (shaped((long_rows, HW)),) * H, 6 * 10 ** 9, 4 * 2...]
    pallas_call x1, Pallas kernels: 17.2 us -> 13.7 us  [body(): call(short_back_kernel, (in_hbm((short_rows, rest)), in_hbm((half, rest))...]
    all_to_all x2, starting transfers between devices: 21.6 us -> 18.5 us  [scatter_pairs(): lax.all_to_all(sent, ('dp', 'sp'), 0, 0, tiled=True, axis_index_groups=gr...]
    ppermute x6, waiting for transfers between devices: 7.97 us -> 4.93 us  [swap_heads(): lax.ppermute(pieces[bits], 'sp', [(src, src ^ bits) for src in range(size)])]
    all_to_all x2, starting transfers between devices: 15.8 us -> 18.8 us  [spread_heads(): lax.all_to_all(sent.reshape(chunks * heads, rows, cols), 'sp', 0, 0, tile...]
    ppermute x5, waiting for transfers between devices: 4.09 us -> 1.52 us  [swap_cores(): return lax.ppermute(half, 'dp', [(src, src ^ 1) for src in range(size)])]
    pallas_call x1, Pallas kernels: 1.17 us -> 2.85 us  [body(): call(long_attend_kernel, (shaped((long_rows, VW)),) * H, 2 * 10 ** 9, 2 *...]
  transfers between devices with their start and end apart: 15 -> 15, of which waited for: 8 -> 5; matrix products, arithmetic and copies ran while one was open for 1% -> 0% of each run, Pallas kernels for 43% -> 43%
where the time goes in v3:
time: 147 us
  Pallas kernels  74.1 us (50%)
  starting transfers between devices  45.6 us (31%)
  waiting for transfers between devices  22.6 us (15%)
  local copies, waits for them, and re-layouts  3.66 us (2%)
    pallas_call x1, Pallas kernels, body(): call(short_forward_kernel, (in_hbm((short_rows, width)), in_hbm((short_ro...  21 us
    all_to_all x2, starting transfers between devices, spread_heads(): lax.all_to_all(sent.reshape(chunks * heads, rows, cols), 'sp', 0, 0, tile...  18.8 us
    all_to_all x2, starting transfers between devices, scatter_pairs(): lax.all_to_all(sent, ('dp', 'sp'), 0, 0, tiled=True, axis_index_groups=gr...  18.5 us
    pallas_call x1, Pallas kernels, body(): call(short_back_kernel, (in_hbm((short_rows, rest)), in_hbm((half, rest))...  13.7 us
    pallas_call x1, Pallas kernels, body(): call(input_back_kernel, (in_hbm((short_rows, width)), in_hbm((long_rows,...  11.2 us
    pallas_call x1, Pallas kernels, body(): call(long_back_kernel, (shaped((long_rows, HW)),) * H, 6 * 10 ** 9, 4 * 2...  10 us
    all_to_all x2, waiting for transfers between devices, spread_heads(): lax.all_to_all(sent.reshape(chunks * heads, rows, cols), 'sp', 0, 0, tile...  9.16 us
    all_to_all x2, waiting for transfers between devices, scatter_pairs(): lax.all_to_all(sent, ('dp', 'sp'), 0, 0, tiled=True, axis_index_groups=gr...  7.01 us
  transfers between devices with their start and end apart: 15, of which 5 were waited for; matrix products, arithmetic and copies ran while one was open for 0% of the time, Pallas kernels for 43%

profile of v3, /device:TPU:0, one launch (start us, length us, event | category | flops | bytes accessed | tf_op | source)
XLA Modules:
  0.0 147.0 jit_solution(5304072250766967084)
XLA Ops:
  0.6 4.2 %long_project.1 = (bf16[1024,1024]{1,0:T(8,128)(2,1)}, bf16[8,4,128,256]{3,2,1,0:T(8,128)(2,1)}, f32[128,1]{1,0:T(8,128)}, bf16[128,1024]{1,0:T(8,128)(2,1)}, bf16[128,1024]{1,0:T(8,128)(2,1)}) custom-call(bf16[128,1024]{1,0:T(8,128)(2,1)} %x_ref.5, bf16[1024,1536]{1,0:T(8,128)(2,1)} %pin_ref.5, bf16[1024,1536]{1,0:T(8,128)(2,1)} %pin_ref.5, ...), custom_call_target="tpu_custom_call" | custom-call | flops 268435456 | bytes 8388608 | tf_op jit(solution)/shard_map/long_project/pallas_call | solution.py:600
  4.8 9.4 %all-to-all-start = ((bf16[32,128,256]{2,1,0:T(8,128)(2,1)}), bf16[32,128,256]{2,1,0:T(8,128)(2,1)}, u32[]{:S(2)}, u32[]{:S(2)}) async-start(bf16[32,128,256]{2,1,0:T(8,128)(2,1)} %bitcast.8), calls=%async_computation | async-start | bytes 4194304 | tf_op jit(solution)/shard_map/all_to_all | solution.py:570
  14.2 21.0 %short_forward.1 = (bf16[1024,1024]{1,0:T(8,128)(2,1)}, bf16[1024,1024]{1,0:T(8,128)(2,1)}, bf16[1024,512]{1,0:T(8,128)(2,1)}, bf16[1024,512]{1,0:T(8,128)(2,1)}...) custom-call(s32[1,2]{1,0:T(1,128)} %user_ref.3, ...), custom_call_target="tpu_custom_call" | custom-call | flops 20000000000 | bytes 25165824 | tf_op jit(solution)/shard_map/short_forward/pallas_call | solution.py:653
  35.3 9.2 %all-to-all-done = bf16[32,128,256]{2,1,0:T(8,128)(2,1)} async-done(((bf16[32,128,256]{2,1,0:T(8,128)(2,1)}), bf16[32,128,256]{2,1,0:T(8,128)(2,1)}, u32[]{:S(2)}, u32[]{:S(2)}) %all-to-all-start) | async-done | bytes 2097184 | tf_op jit(solution)/shard_map/all_to_all | solution.py:570
  44.4 2.9 %long_attend.1 = (bf16[128,128]{1,0:T(8,128)(2,1)}, bf16[128,128]{1,0:T(8,128)(2,1)}, bf16[128,128]{1,0:T(8,128)(2,1)}, bf16[128,128]{1,0:T(8,128)(2,1)}) custom-call(s32[4]{0:T(128)} %blocks_smem.3, bf16[4096,256]{1,0:T(8,128)(2,1)} %bitcast.1.all_ref), custom_call_target="tpu_custom_call" | custom-call | flops 2000000000 | bytes 2097152 | tf_op jit(solution)/shard_map/long_attend/pallas_call | solution.py:705
  47.3 0.7 collective-permute-start.1
  48.0 2.8 %collective-permute-start.2 = (bf16[128,128]{1,0:T(8,128)(2,1)}, bf16[128,128]{1,0:T(8,128)(2,1)S(1)}, u32[]{:S(2)}, u32[]{:S(2)}) collective-permute-start(bf16[128,128]{1,0:T(8,128)(2,1)} %get-tuple-element.65), channel_id=1, source_target_pairs={{0,3},{1,2},{2,1},{3,0},{4,7},{5,6},{6,5},{7,4},{8,11},{9,10},{10,... | collective-permute-start | bytes 98312 | tf_op jit(solution)/shard_map/ppermute | solution.py:563
  50.8 2.6 %long_gate.1 = (bf16[128,512]{1,0:T(8,128)(2,1)}, bf16[128,512]{1,0:T(8,128)(2,1)}, bf16[128,1024]{1,0:T(8,128)(2,1)}) custom-call(bf16[128,1024]{1,0:T(8,128)(2,1)} %get-tuple-element.66.xbf_ref.long_xbf_ref, bf16[1024,1536]{1,0:T(8,128)(2,1)} %pin_ref.5, bf16[128,1024]{1,0:T(8,128)(2,1)} %long_cot_ref.1), custom_call_target="tpu_custom_call" | custom-call | flops 134217728 | bytes 4194304 | tf_op jit(solution)/shard_map/long_gate/pallas_call | solution.py:629
  53.4 0.5 copy-done.9
  54.0 3.6 %long_head.1 = (bf16[128,1024]{1,0:T(8,128)(2,1)}, bf16[8,4,128,128]{3,2,1,0:T(8,128)(2,1)}, bf16[128,1024]{1,0:T(8,128)(2,1)}) custom-call(bf16[128,128]{1,0:T(8,128)(2,1)} %get-tuple-element.62.got_0, bf16[128,128]{1,0:T(8,128)(2,1)} %copy-done.9, bf16[128,128]{1,0:T(8,128)(2,1)} %copy-done.10, bf16[128,128]{1,0:T(8,128)(2,1)} %copy-done.11, ...), custom_call_target="tpu_custom_call" | custom-call | flops 268435456 | bytes 3145728 | tf_op jit(solution)/shard_map/long_head/pallas_call | solution.py:717
  57.6 9.4 %all-to-all-start.1 = ((bf16[32,128,128]{2,1,0:T(8,128)(2,1)}), bf16[32,128,128]{2,1,0:T(8,128)(2,1)S(1)}, u32[]{:S(2)}, u32[]{:S(2)}) async-start(bf16[32,128,128]{2,1,0:T(8,128)(2,1)} %bitcast.10), calls=%async_computation.1 | async-start | bytes 2097152 | tf_op jit(solution)/shard_map/all_to_all | solution.py:570
  67.1 0.5 collective-permute-start.4
  67.7 13.7 %short_back.1 = (bf16[1024,1024]{1,0:T(8,128)(2,1)}, bf16[512,1024]{1,0:T(8,128)(2,1)}, bf16[512,1024]{1,0:T(8,128)(2,1)}) custom-call(s32[1,2]{1,0:T(1,128)} %user_ref.3, bf16[1024,1024]{1,0:T(8,128)(2,1)} %get-tuple-element.76.qkv_ref, bf16[1024,512]{1,0:T(8,128)(2,1)} %get-tuple-element.77.g_ref, bf16[1024,1024]{1,0:T(8,128)(2,1)} %get-tuple-element.78.slope_ref, ...), custom_call_target="tpu_custom_call" | custom-call | flops 16000000000 | bytes 13631488 | tf_op jit(solution)/shard_map/short_back/pallas_call | solution.py:738
  81.3 0.4 collective-permute-start.3
  81.8 1.5 %early_sums.1 = bf16[512,1024]{1,0:T(8,128)(2,1)} custom-call(bf16[128,1024]{1,0:T(8,128)(2,1)S(1)} %copy-done.1, bf16[128,1024]{1,0:T(8,128)(2,1)S(1)} %copy-done, bf16[128,1024]{1,0:T(8,128)(2,1)S(1)} %copy-done.3, bf16[128,1024]{1,0:T(8,128)(2,1)S(1)} %collective-permute-done.5.half_ref, bf16[128,1024]{1,0:T(8,128)(2,1)S(1)} %collective-permute-done.4.mid_got, ...), custom_call_target="tpu_custom_call" | custom-call | flops 268435456 | bytes 5242880 | tf_op jit(solution)/shard_map/early_sums/pallas_call | solution.py:767
  83.3 1.0 copy-done.8
  84.2 10.0 %all-to-all-start.2 = ((bf16[64,8,1024]{2,1,0:T(8,128)(2,1)}), bf16[64,8,1024]{2,1,0:T(8,128)(2,1)S(1)}, u32[]{:S(2)}, u32[]{:S(2)}) async-start(bf16[64,8,1024]{2,1,0:T(8,128)(2,1)} %bitcast.6), calls=%async_computation.2 | async-start | bytes 2097152 | tf_op jit(solution)/shard_map/all_to_all | solution.py:587
  94.3 10.0 %long_back.1 = (bf16[128,256]{1,0:T(8,128)(2,1)}, bf16[128,256]{1,0:T(8,128)(2,1)}, bf16[128,256]{1,0:T(8,128)(2,1)}, bf16[128,256]{1,0:T(8,128)(2,1)}) custom-call(s32[4]{0:T(128)} %blocks_smem.3, bf16[4096,256]{1,0:T(8,128)(2,1)} %bitcast.1.all_ref, bf16[4096,128]{1,0:T(8,128)(2,1)} %bitcast.9), custom_call_target="tpu_custom_call" | custom-call | flops 6000000000 | bytes 4194304 | tf_op jit(solution)/shard_map/long_back/pallas_call | solution.py:777
  104.3 1.6 %collective-permute-start.7 = (bf16[128,256]{1,0:T(8,128)(2,1)}, bf16[128,256]{1,0:T(8,128)(2,1)S(1)}, u32[]{:S(2)}, u32[]{:S(2)}) collective-permute-start(bf16[128,256]{1,0:T(8,128)(2,1)} %get-tuple-element.94), channel_id=1, source_target_pairs={{0,1},{1,0},{2,3},{3,2},{4,5},{5,4},{6,7},{7,6},{8,9},{9,8},{10,11... | collective-permute-start | bytes 196616 | tf_op jit(solution)/shard_map/ppermute | solution.py:563
  105.9 1.5 collective-permute-start.8
  107.4 0.4 collective-permute-start.9
  107.8 3.3 %collective-permute-done.7.got_1 = bf16[128,256]{1,0:T(8,128)(2,1)S(1)} collective-permute-done((bf16[128,256]{1,0:T(8,128)(2,1)}, bf16[128,256]{1,0:T(8,128)(2,1)S(1)}, u32[]{:S(2)}, u32[]{:S(2)}) %collective-permute-start.7) | collective-permute-done | bytes 65568 | tf_op jit(solution)/shard_map/ppermute | solution.py:563
  111.1 1.7 %collective-permute-done.9.got_3 = bf16[128,256]{1,0:T(8,128)(2,1)S(1)} collective-permute-done((bf16[128,256]{1,0:T(8,128)(2,1)}, bf16[128,256]{1,0:T(8,128)(2,1)S(1)}, u32[]{:S(2)}, u32[]{:S(2)}) %collective-permute-start.9) | collective-permute-done | bytes 65568 | tf_op jit(solution)/shard_map/ppermute | solution.py:563
  112.8 0.8 copy-done.7
  113.7 0.3 collective-permute-start.10
  114.0 1.5 %collective-permute-done.10.grad_got = bf16[128,1024]{1,0:T(8,128)(2,1)S(1)} collective-permute-done((bf16[128,1024]{1,0:T(8,128)(2,1)S(1)}, bf16[128,1024]{1,0:T(8,128)(2,1)S(1)}, u32[]{:S(2)}, u32[]{:S(2)}) %collective-permute-start.10) | collective-permute-done | bytes 262176 | tf_op jit(solution)/shard_map/ppermute | solution.py:576
  115.5 1.2 copy-done.5
  116.8 2.6 %late_sums.1 = bf16[512,1024]{1,0:T(8,128)(2,1)} custom-call(bf16[512,1024]{1,0:T(8,128)(2,1)S(1)} %copy-done.5, bf16[512,1024]{1,0:T(8,128)(2,1)} %collective-permute-done.3.got_ref, bf16[128,1024]{1,0:T(8,128)(2,1)S(1)} %copy-done.1, bf16[128,1024]{1,0:T(8,128)(2,1)S(1)} %collective-permute-done.5.half_ref, ...), custom_call_target="tpu_custom_call" | custom-call | flops 268435456 | bytes 5242880 | tf_op jit(solution)/shard_map/late_sums/pallas_call | solution.py:798
  119.3 8.5 %all-to-all-start.3 = ((bf16[64,8,1024]{2,1,0:T(8,128)(2,1)}), bf16[64,8,1024]{2,1,0:T(8,128)(2,1)S(1)}, u32[]{:S(2)}, u32[]{:S(2)}) async-start(bf16[64,8,1024]{2,1,0:T(8,128)(2,1)} %bitcast.7), calls=%async_computation.3 | async-start | bytes 2097152 | tf_op jit(solution)/shard_map/all_to_all | solution.py:587
  127.8 11.2 %input_back.1 = (bf16[1024,1024]{1,0:T(8,128)(2,1)}, bf16[128,1024]{1,0:T(8,128)(2,1)}) custom-call(bf16[1024,512]{1,0:T(8,128)(2,1)} %get-tuple-element.99.grad_gate_ref, bf16[1024,1024]{1,0:T(8,128)(2,1)} %get-tuple-element.100.grad_ref, bf16[1024,1024]{1,0:T(8,128)(2,1)} %cot_ref.9, bf16[1024,1024]{1,0:T(8,128)(2,1)} %get-tuple-element.101.xbf_ref, ...), custom_call_target="tpu_custom_call" | custom-call | flops 3623878656 | bytes 14680064 | tf_op jit(solution)/shard_map/input_back/pallas_call | solution.py:821
  139.1 7.0 %all-to-all-done.3.late_ref = bf16[64,8,1024]{2,1,0:T(8,128)(2,1)S(1)} async-done(((bf16[64,8,1024]{2,1,0:T(8,128)(2,1)}), bf16[64,8,1024]{2,1,0:T(8,128)(2,1)S(1)}, u32[]{:S(2)}, u32[]{:S(2)}) %all-to-all-start.3) | async-done | bytes 1048608 | tf_op jit(solution)/shard_map/all_to_all | solution.py:587
  146.1 0.9 final_sums.1
  (39 shorter events, 0.6 us)
Async XLA Ops:
  4.8 39.6 %all-to-all-start = ((bf16[32,128,256]{2,1,0:T(8,128)(2,1)}), bf16[32,128,256]{2,1,0:T(8,128)(2,1)}, u32[]{:S(2)}, u32[]{:S(2)}) async-start(bf16[32,128,256]{2,1,0:T(8,128)(2,1)} %bitcast.8), calls=%async_computation | async-start | bytes 4194304 | tf_op jit(solution)/shard_map/all_to_all | solution.py:570
  47.3 6.1 %collective-permute-start = (bf16[128,128]{1,0:T(8,128)(2,1)}, bf16[128,128]{1,0:T(8,128)(2,1)S(1)}, u32[]{:S(2)}, u32[]{:S(2)}) collective-permute-start(bf16[128,128]{1,0:T(8,128)(2,1)} %get-tuple-element.63), channel_id=1, source_target_pairs={{0,1},{1,0},{2,3},{3,2},{4,5},{5,4},{6,7},{7,6},{8,9},{9,8},{10,11... | collective-permute-start | bytes 98312 | tf_op jit(solution)/shard_map/ppermute | solution.py:563
  47.3 6.1 %collective-permute-start.1 = (bf16[128,128]{1,0:T(8,128)(2,1)}, bf16[128,128]{1,0:T(8,128)(2,1)S(1)}, u32[]{:S(2)}, u32[]{:S(2)}) collective-permute-start(bf16[128,128]{1,0:T(8,128)(2,1)} %get-tuple-element.64), channel_id=1, source_target_pairs={{0,2},{1,3},{2,0},{3,1},{4,6},{5,7},{6,4},{7,5},{8,10},{9,11},{10,... | collective-permute-start | bytes 98312 | tf_op jit(solution)/shard_map/ppermute | solution.py:563
  48.0 5.4 %collective-permute-start.2 = (bf16[128,128]{1,0:T(8,128)(2,1)}, bf16[128,128]{1,0:T(8,128)(2,1)S(1)}, u32[]{:S(2)}, u32[]{:S(2)}) collective-permute-start(bf16[128,128]{1,0:T(8,128)(2,1)} %get-tuple-element.65), channel_id=1, source_target_pairs={{0,3},{1,2},{2,1},{3,0},{4,7},{5,6},{6,5},{7,4},{8,11},{9,10},{10,... | collective-permute-start | bytes 98312 | tf_op jit(solution)/shard_map/ppermute | solution.py:563
  53.3 13.6 %copy-start.13 = (bf16[128,1024]{1,0:T(8,128)(2,1)S(1)}, bf16[128,1024]{1,0:T(8,128)(2,1)}, u32[]{:S(2)}) copy-start(bf16[128,1024]{1,0:T(8,128)(2,1)} %get-tuple-element.84) | copy-start | bytes 786436
  53.3 14.2 %copy-start.12 = (bf16[512,1024]{1,0:T(8,128)(2,1)S(1)}, bf16[512,1024]{1,0:T(8,128)(2,1)}, u32[]{:S(2)}) copy-start(bf16[512,1024]{1,0:T(8,128)(2,1)} %get-tuple-element.85) | copy-start | bytes 3145732
  53.3 0.6 copy-start.9
  53.4 0.6 copy-start.10
  53.4 0.6 copy-start.11
  57.6 9.5 %copy-start.3 = (bf16[128,1024]{1,0:T(8,128)(2,1)S(1)}, bf16[128,1024]{1,0:T(8,128)(2,1)}, u32[]{:S(2)}) copy-start(bf16[128,1024]{1,0:T(8,128)(2,1)} %get-tuple-element.83.mid_ref.long_gate_ref) | copy-start | bytes 786436
  57.6 25.7 %all-to-all-start.1 = ((bf16[32,128,128]{2,1,0:T(8,128)(2,1)}), bf16[32,128,128]{2,1,0:T(8,128)(2,1)S(1)}, u32[]{:S(2)}, u32[]{:S(2)}) async-start(bf16[32,128,128]{2,1,0:T(8,128)(2,1)} %bitcast.10), calls=%async_computation.1 | async-start | bytes 2097152 | tf_op jit(solution)/shard_map/all_to_all | solution.py:570
  67.0 14.8 %collective-permute-start.5 = (bf16[128,1024]{1,0:T(8,128)(2,1)S(1)}, bf16[128,1024]{1,0:T(8,128)(2,1)S(1)}, u32[]{:S(2)}, u32[]{:S(2)}) collective-permute-start(bf16[128,1024]{1,0:T(8,128)(2,1)S(1)} %copy-done.13), channel_id=1, source_target_pairs={{0,32},{32,0},{64,96},{96,64},{1,33},{33,1},{65,97},{97,65},{2,34}... | collective-permute-start | bytes 786440 | tf_op jit(solution)/shard_map/ppermute | solution.py:576
  67.1 14.7 %collective-permute-start.4 = (bf16[128,1024]{1,0:T(8,128)(2,1)S(1)}, bf16[128,1024]{1,0:T(8,128)(2,1)S(1)}, u32[]{:S(2)}, u32[]{:S(2)}) collective-permute-start(bf16[128,1024]{1,0:T(8,128)(2,1)S(1)} %copy-done.3), channel_id=1, source_target_pairs={{0,32},{32,0},{64,96},{96,64},{1,33},{33,1},{65,97},{97,65},{2,34}... | collective-permute-start | bytes 786440 | tf_op jit(solution)/shard_map/ppermute | solution.py:576
  67.6 14.2 %collective-permute-start.6 = (bf16[512,1024]{1,0:T(8,128)(2,1)S(1)}, bf16[512,1024]{1,0:T(8,128)(2,1)S(1)}, u32[]{:S(2)}, u32[]{:S(2)}) collective-permute-start(bf16[512,1024]{1,0:T(8,128)(2,1)S(1)} %copy-done.12), channel_id=1, source_target_pairs={{0,32},{32,0},{64,96},{96,64},{1,33},{33,1},{65,97},{97,65},{2,34}... | collective-permute-start | bytes 3145736 | tf_op jit(solution)/shard_map/ppermute | solution.py:576
  67.7 14.1 %copy-start = (bf16[128,1024]{1,0:T(8,128)(2,1)S(1)}, bf16[128,1024]{1,0:T(8,128)(2,1)}, u32[]{:S(2)}) copy-start(bf16[128,1024]{1,0:T(8,128)(2,1)} %long_cot_ref.1) | copy-start | bytes 786436
  67.7 14.1 %copy-start.1 = (bf16[128,1024]{1,0:T(8,128)(2,1)S(1)}, bf16[128,1024]{1,0:T(8,128)(2,1)}, u32[]{:S(2)}) copy-start(bf16[128,1024]{1,0:T(8,128)(2,1)} %get-tuple-element.66.xbf_ref.long_xbf_ref) | copy-start | bytes 786436
  67.7 14.1 %copy-start.4 = (bf16[512,1024]{1,0:T(8,128)(2,1)S(1)}, bf16[512,1024]{1,0:T(8,128)(2,1)}, u32[]{:S(2)}) copy-start(bf16[512,1024]{1,0:T(8,128)(2,1)} %get-tuple-element.90.mine_ref) | copy-start | bytes 3145732
  81.3 32.7 %collective-permute-start.3 = (bf16[512,1024]{1,0:T(8,128)(2,1)}, bf16[512,1024]{1,0:T(8,128)(2,1)}, u32[]{:S(2)}, u32[]{:S(2)}) collective-permute-start(bf16[512,1024]{1,0:T(8,128)(2,1)} %get-tuple-element.82), channel_id=1, source_target_pairs={{0,32},{32,0},{64,96},{96,64},{1,33},{33,1},{65,97},{97,65},{2,34}... | collective-permute-start | bytes 3145736 | tf_op jit(solution)/shard_map/ppermute | solution.py:576
  83.3 1.0 copy-start.8
  84.2 35.1 %all-to-all-start.2 = ((bf16[64,8,1024]{2,1,0:T(8,128)(2,1)}), bf16[64,8,1024]{2,1,0:T(8,128)(2,1)S(1)}, u32[]{:S(2)}, u32[]{:S(2)}) async-start(bf16[64,8,1024]{2,1,0:T(8,128)(2,1)} %bitcast.6), calls=%async_computation.2 | async-start | bytes 2097152 | tf_op jit(solution)/shard_map/all_to_all | solution.py:587
  94.3 18.5 %copy-start.6 = (bf16[128,1024]{1,0:T(8,128)(2,1)S(1)}, bf16[128,1024]{1,0:T(8,128)(2,1)}, u32[]{:S(2)}) copy-start(bf16[128,1024]{1,0:T(8,128)(2,1)} %get-tuple-element.97.slope_ref) | copy-start | bytes 786436
  104.3 6.7 %collective-permute-start.7 = (bf16[128,256]{1,0:T(8,128)(2,1)}, bf16[128,256]{1,0:T(8,128)(2,1)S(1)}, u32[]{:S(2)}, u32[]{:S(2)}) collective-permute-start(bf16[128,256]{1,0:T(8,128)(2,1)} %get-tuple-element.94), channel_id=1, source_target_pairs={{0,1},{1,0},{2,3},{3,2},{4,5},{5,4},{6,7},{7,6},{8,9},{9,8},{10,11... | collective-permute-start | bytes 196616 | tf_op jit(solution)/shard_map/ppermute | solution.py:563
  105.9 5.2 %collective-permute-start.8 = (bf16[128,256]{1,0:T(8,128)(2,1)}, bf16[128,256]{1,0:T(8,128)(2,1)S(1)}, u32[]{:S(2)}, u32[]{:S(2)}) collective-permute-start(bf16[128,256]{1,0:T(8,128)(2,1)} %get-tuple-element.95), channel_id=1, source_target_pairs={{0,2},{1,3},{2,0},{3,1},{4,6},{5,7},{6,4},{7,5},{8,10},{9,11},{10,... | collective-permute-start | bytes 196616 | tf_op jit(solution)/shard_map/ppermute | solution.py:563
  107.4 5.4 %collective-permute-start.9 = (bf16[128,256]{1,0:T(8,128)(2,1)}, bf16[128,256]{1,0:T(8,128)(2,1)S(1)}, u32[]{:S(2)}, u32[]{:S(2)}) collective-permute-start(bf16[128,256]{1,0:T(8,128)(2,1)} %get-tuple-element.96), channel_id=1, source_target_pairs={{0,3},{1,2},{2,1},{3,0},{4,7},{5,6},{6,5},{7,4},{8,11},{9,10},{10,... | collective-permute-start | bytes 196616 | tf_op jit(solution)/shard_map/ppermute | solution.py:563
  112.8 0.8 copy-start.7
  113.7 5.6 %copy-start.2 = (bf16[128,1024]{1,0:T(8,128)(2,1)}, bf16[128,1024]{1,0:T(8,128)(2,1)S(1)}, u32[]{:S(2)}) copy-start(bf16[128,1024]{1,0:T(8,128)(2,1)S(1)} %long_slopes.1.grad_ref.long_grad_ref) | copy-start | bytes 786436
  113.7 1.8 %collective-permute-start.10 = (bf16[128,1024]{1,0:T(8,128)(2,1)S(1)}, bf16[128,1024]{1,0:T(8,128)(2,1)S(1)}, u32[]{:S(2)}, u32[]{:S(2)}) collective-permute-start(bf16[128,1024]{1,0:T(8,128)(2,1)S(1)} %long_slopes.1.grad_ref.long_grad_ref), channel_id=1, source_target_pairs={{0,32},{32,0},{64,96},{96,64},{1,33},{33,1},{65,97},{97,65},{2,34}... | collective-permute-start | bytes 786440 | tf_op jit(solution)/shard_map/ppermute | solution.py:576
  115.5 1.2 copy-start.5
  119.3 26.8 %all-to-all-start.3 = ((bf16[64,8,1024]{2,1,0:T(8,128)(2,1)}), bf16[64,8,1024]{2,1,0:T(8,128)(2,1)S(1)}, u32[]{:S(2)}, u32[]{:S(2)}) async-start(bf16[64,8,1024]{2,1,0:T(8,128)(2,1)} %bitcast.7), calls=%async_computation.3 | async-start | bytes 2097152 | tf_op jit(solution)/shard_map/all_to_all | solution.py:587

commit v4 on v3

--- a/solution.py
+++ b/solution.py
@@ -228,21 +228,22 @@
     def _():
         lanes = low_lanes((BLOCK, 2 * KW))
 
-        @pl.loop(0, H)
-        def _(which):
-            pair, rest, narrow = head_lanes(which)
-            grad_q, grad_k, grad_v = back_block(
-                side_ref[:, narrow],
-                qkv_ref[:, pair],
-                seen_ref[:, pair],
-                seen_ref[:, rest],
-                g_ref[:, narrow],
-                None,
-            )
-            join_ref[:BLOCK, pair] = jnp.where(lanes, grad_k, 0.0).astype(BF16)
-            join_ref[:BLOCK, rest] = grad_v.astype(BF16)
-            join_ref[BLOCK:, pair] = jnp.where(lanes, 0.0, grad_q).astype(BF16)
-            join_ref[BLOCK:, rest] = jnp.zeros(grad_v.shape, BF16)
+        @pl.loop(0, H // 2)
+        def _(two):
+            for which in (2 * two, 2 * two + 1):
+                pair, rest, narrow = head_lanes(which)
+                grad_q, grad_k, grad_v = back_block(
+                    side_ref[:, narrow],
+                    qkv_ref[:, pair],
+                    seen_ref[:, pair],
+                    seen_ref[:, rest],
+                    g_ref[:, narrow],
+                    None,
+                )
+                join_ref[:BLOCK, pair] = jnp.where(lanes, grad_k, 0.0).astype(BF16)
+                join_ref[:BLOCK, rest] = grad_v.astype(BF16)
+                join_ref[BLOCK:, pair] = jnp.where(lanes, 0.0, grad_q).astype(BF16)
+                join_ref[BLOCK:, rest] = jnp.zeros(grad_v.shape, BF16)
 
     @pl.when(step == 0)
     def _():
@@ -313,18 +314,37 @@
     return pl.ds(pl.multiple_of(index * BLOCK, BLOCK), BLOCK)
 
 
-def long_attend_kernel(blocks_smem, all_ref, *refs):
-    mixed_refs, acc_ref = refs[:H], refs[H]
+def long_attend_kernel(blocks_smem, all_hbm, *refs):
+    mixed_refs, (acc_ref, all_ref, sems) = refs[:H], refs[H:]
     mine, chunk, group = run_place()
     valid = blocks_smem[group]
+
+    def block_copy(index):
+        rows = rows_at(index)
+        return pltpu.make_async_copy(all_hbm.at[rows], all_ref.at[rows], sems.at[index])
+
+    block_copy(chunk).start()
+
+    @pl.loop(0, chunk)
+    def _(index):
+        block_copy(index).start()
+
     acc_ref[...] = jnp.zeros_like(acc_ref)
-
-    @pl.when(chunk < valid)
-    def _():
-        side = score_side(all_ref[rows_at(chunk), : 2 * KW])
-
+    block_copy(chunk).wait()
+
+    @pl.when(chunk >= valid)
+    def _():
         @pl.loop(0, chunk)
         def _(index):
+            block_copy(index).wait()
+
+    @pl.when(chunk < valid)
+    def _():
+        side = score_side(all_ref[rows_at(chunk), : 2 * KW])
+
+        @pl.loop(0, chunk)
+        def _(index):
+            block_copy(index).wait()
             scores = dot(side, all_ref[rows_at(index), : 2 * KW], 1, 1)
             acc_ref[...] += dot(
                 silu_half(scores).astype(BF16), all_ref[rows_at(index), 2 * KW :], 1, 0
@@ -636,7 +656,6 @@
         2 * long_rows * width * gates,
         4 * 2**20,
         "long_gate",
-        vmem=60,
         grid=(1,),
         in_specs=[
             fixed_spec(long_rows, width),
@@ -708,10 +727,11 @@
         2 * 10**9,
         2 * 2**20,
         "long_attend",
-        vmem=62,
-        in_specs=[SMEM, WHOLE],
+        in_specs=[SMEM, pl.BlockSpec(memory_space=pl.ANY)],
         scratch_shapes=[
             pltpu.VMEM((BLOCK, VW), F32),
+            pltpu.VMEM((chunks * BLOCK, HW), BF16),
+            pltpu.SemaphoreType.DMA((chunks,)),
         ],
     )(long_blocks, whole)
     out_long, sent, mid = call(
@@ -724,7 +744,6 @@
         4 * long_rows * width * gates,
         3 * 2**20,
         "long_head",
-        vmem=60,
         in_specs=[WHOLE] * 9,
         scratch_shapes=[pltpu.VMEM((long_rows, gates), F32)],
     )(*swap_heads(mixed), x_long, cot_long, proj_out, gate_long, slope_long)

time: 147 us -> 145 us (0.986); the launches traced: 147 us -> 143 us
  Pallas kernels: 74.1 us -> 66 us
  waiting for transfers between devices: 22.6 us -> 27.1 us
  starting transfers between devices: 45.6 us -> 43 us
  local copies, waits for them, and re-layouts: 3.66 us -> 6 us
    all_to_all x2, starting transfers between devices: 18.8 us -> 15 us  [spread_heads(): lax.all_to_all(sent.reshape(chunks * heads, rows, cols), 'sp', 0, 0, tile...]
    pallas_call x1, Pallas kernels: 10 us -> 6.56 us  [body(): call(long_back_kernel, (shaped((long_rows, HW)),) * H, 6 * 10 ** 9, 4 * 2...]
    ppermute x6, waiting for transfers between devices: 4.93 us -> 7.43 us  [swap_heads(): lax.ppermute(pieces[bits], 'sp', [(src, src ^ bits) for src in range(size)])]
    all_to_all x2, waiting for transfers between devices: 9.16 us -> 11.5 us  [spread_heads(): lax.all_to_all(sent.reshape(chunks * heads, rows, cols), 'sp', 0, 0, tile...]
    unnamed x28 -> x32, local copies, waits for them, and re-layouts: 3.66 us -> 6 us
    pallas_call x1, Pallas kernels: 2.85 us -> 1.28 us  [body(): call(long_attend_kernel, (shaped((long_rows, VW)),) * H, 2 * 10 ** 9, 2 *...]
    pallas_call x1, Pallas kernels: 2.58 us -> 1.05 us  [body(): call(long_gate_kernel, (shaped((long_rows, gates)), shaped((long_rows, ga...]
    pallas_call x1, Pallas kernels: 3.59 us -> 2.07 us  [body(): call(long_head_kernel, (shaped((long_rows, width)), in_hbm((chunks, H, lo...]
  transfers between devices with their start and end apart: 15 -> 15, of which waited for: 5 -> 7; matrix products, arithmetic and copies ran while one was open for 0% -> 0% of each run, Pallas kernels for 43% -> 40%
where the time goes in v4:
time: 145 us; the launch traced here: 143 us
  Pallas kernels  66 us (46%)
  starting transfers between devices  43 us (30%)
  waiting for transfers between devices  27.1 us (19%)
  local copies, waits for them, and re-layouts  6 us (4%)
    pallas_call x1, Pallas kernels, body(): call(short_forward_kernel, (in_hbm((short_rows, width)), in_hbm((short_ro...  21 us
    all_to_all x2, starting transfers between devices, scatter_pairs(): lax.all_to_all(sent, ('dp', 'sp'), 0, 0, tiled=True, axis_index_groups=gr...  18.2 us
    all_to_all x2, starting transfers between devices, spread_heads(): lax.all_to_all(sent.reshape(chunks * heads, rows, cols), 'sp', 0, 0, tile...  15 us
    pallas_call x1, Pallas kernels, body(): call(short_back_kernel, (in_hbm((short_rows, rest)), in_hbm((half, rest))...  13.6 us
    all_to_all x2, waiting for transfers between devices, spread_heads(): lax.all_to_all(sent.reshape(chunks * heads, rows, cols), 'sp', 0, 0, tile...  11.5 us
    pallas_call x1, Pallas kernels, body(): call(input_back_kernel, (in_hbm((short_rows, width)), in_hbm((long_rows,...  11.1 us
    ppermute x6, waiting for transfers between devices, swap_heads(): lax.ppermute(pieces[bits], 'sp', [(src, src ^ bits) for src in range(size)])  7.43 us
    ppermute x6, starting transfers between devices, swap_heads(): lax.ppermute(pieces[bits], 'sp', [(src, src ^ bits) for src in range(size)])  7.23 us
  transfers between devices with their start and end apart: 15, of which 7 were waited for; matrix products, arithmetic and copies ran while one was open for 0% of the time, Pallas kernels for 40%

profile of v4, /device:TPU:0, one launch (start us, length us, event | category | flops | bytes accessed | tf_op | source)
XLA Modules:
  0.0 143.1 jit_solution(10410666793695329081)
XLA Ops:
  0.6 4.2 %long_project.1 = (bf16[1024,1024]{1,0:T(8,128)(2,1)}, bf16[8,4,128,256]{3,2,1,0:T(8,128)(2,1)}, f32[128,1]{1,0:T(8,128)}, bf16[128,1024]{1,0:T(8,128)(2,1)}, bf16[128,1024]{1,0:T(8,128)(2,1)}) custom-call(bf16[128,1024]{1,0:T(8,128)(2,1)} %x_ref.5, bf16[1024,1536]{1,0:T(8,128)(2,1)} %pin_ref.5, bf16[1024,1536]{1,0:T(8,128)(2,1)} %pin_ref.5, ...), custom_call_target="tpu_custom_call" | custom-call | flops 268435456 | bytes 8388608 | tf_op jit(solution)/shard_map/long_project/pallas_call | solution.py:620
  4.8 9.3 %all-to-all-start = ((bf16[32,128,256]{2,1,0:T(8,128)(2,1)}), bf16[32,128,256]{2,1,0:T(8,128)(2,1)S(1)}, u32[]{:S(2)}, u32[]{:S(2)}) async-start(bf16[32,128,256]{2,1,0:T(8,128)(2,1)} %bitcast.10), calls=%async_computation | async-start | bytes 4194304 | tf_op jit(solution)/shard_map/all_to_all | solution.py:590
  14.1 21.0 %short_forward.1 = (bf16[1024,1024]{1,0:T(8,128)(2,1)}, bf16[1024,1024]{1,0:T(8,128)(2,1)}, bf16[1024,512]{1,0:T(8,128)(2,1)}, bf16[1024,512]{1,0:T(8,128)(2,1)}...) custom-call(s32[1,2]{1,0:T(1,128)} %user_ref.3, ...), custom_call_target="tpu_custom_call" | custom-call | flops 20000000000 | bytes 25165824 | tf_op jit(solution)/shard_map/short_forward/pallas_call | solution.py:672
  35.2 9.2 %all-to-all-done = bf16[32,128,256]{2,1,0:T(8,128)(2,1)S(1)} async-done(((bf16[32,128,256]{2,1,0:T(8,128)(2,1)}), bf16[32,128,256]{2,1,0:T(8,128)(2,1)S(1)}, u32[]{:S(2)}, u32[]{:S(2)}) %all-to-all-start) | async-done | bytes 2097184 | tf_op jit(solution)/shard_map/all_to_all | solution.py:590
  44.3 1.3 copy-done.4
  45.6 1.6 %copy-done.5 = bf16[32,128,256]{2,1,0:T(8,128)(2,1)S(1)} copy-done((bf16[32,128,256]{2,1,0:T(8,128)(2,1)S(1)}, bf16[32,128,256]{2,1,0:T(8,128)(2,1)}, u32[]{:S(2)}) %copy-start.5) | copy-done | bytes 2097176
  47.2 1.3 long_attend.1
  49.3 3.0 %collective-permute-start.2 = (bf16[128,128]{1,0:T(8,128)(2,1)S(1)}, bf16[128,128]{1,0:T(8,128)(2,1)S(1)}, u32[]{:S(2)}, u32[]{:S(2)}) collective-permute-start(bf16[128,128]{1,0:T(8,128)(2,1)S(1)} %get-tuple-element.65), channel_id=1, source_target_pairs={{0,3},{1,2},{2,1},{3,0},{4,7},{5,6},{6,5},{7,4},{8,11},{9,10},{10,... | collective-permute-start | bytes 98312 | tf_op jit(solution)/shard_map/ppermute | solution.py:583
  52.3 1.0 long_gate.1
  53.4 1.2 collective-permute-done.2.got_3
  54.5 2.1 %long_head.1 = (bf16[128,1024]{1,0:T(8,128)(2,1)}, bf16[8,4,128,128]{3,2,1,0:T(8,128)(2,1)}, bf16[128,1024]{1,0:T(8,128)(2,1)}) custom-call(bf16[128,128]{1,0:T(8,128)(2,1)S(1)} %get-tuple-element.62.got_0, bf16[128,128]{1,0:T(8,128)(2,1)S(1)} %collective-permute-done.got_1, bf16[128,128]{1,0:T(8,128)(2,1)S(1)} %collective-permute-done.1.got_2, ...), custom_call_target="tpu_custom_call" | custom-call | flops 268435456 | bytes 3145728 | tf_op jit(solution)/shard_map/long_head/pallas_call | solution.py:737
  56.6 5.7 %all-to-all-start.1 = ((bf16[32,128,128]{2,1,0:T(8,128)(2,1)}), bf16[32,128,128]{2,1,0:T(8,128)(2,1)S(1)}, u32[]{:S(2)}, u32[]{:S(2)}) async-start(bf16[32,128,128]{2,1,0:T(8,128)(2,1)} %bitcast.12), calls=%async_computation.1 | async-start | bytes 2097152 | tf_op jit(solution)/shard_map/all_to_all | solution.py:590
  62.4 0.8 collective-permute-start.5
  63.7 13.6 %short_back.1 = (bf16[1024,1024]{1,0:T(8,128)(2,1)}, bf16[512,1024]{1,0:T(8,128)(2,1)}, bf16[512,1024]{1,0:T(8,128)(2,1)}) custom-call(s32[1,2]{1,0:T(1,128)} %user_ref.3, bf16[1024,1024]{1,0:T(8,128)(2,1)} %get-tuple-element.76.qkv_ref, bf16[1024,512]{1,0:T(8,128)(2,1)} %get-tuple-element.77.g_ref, bf16[1024,1024]{1,0:T(8,128)(2,1)} %get-tuple-element.78.slope_ref, ...), custom_call_target="tpu_custom_call" | custom-call | flops 16000000000 | bytes 13631488 | tf_op jit(solution)/shard_map/short_back/pallas_call | solution.py:757
  77.7 1.6 %early_sums.1 = bf16[512,1024]{1,0:T(8,128)(2,1)} custom-call(bf16[128,1024]{1,0:T(8,128)(2,1)S(1)} %copy-done.2, bf16[128,1024]{1,0:T(8,128)(2,1)S(1)} %copy-done.1, bf16[128,1024]{1,0:T(8,128)(2,1)S(1)} %copy-done.6, bf16[128,1024]{1,0:T(8,128)(2,1)S(1)} %collective-permute-done.5.half_ref, bf16[128,1024]{1,0:T(8,128)(2,1)S(1)} %collective-permute-done.4.mid_got, ...), custom_call_target="tpu_custom_call" | custom-call | flops 268435456 | bytes 5242880 | tf_op jit(solution)/shard_map/early_sums/pallas_call | solution.py:786
  79.3 2.4 %all-to-all-done.1 = bf16[32,128,128]{2,1,0:T(8,128)(2,1)S(1)} async-done(((bf16[32,128,128]{2,1,0:T(8,128)(2,1)}), bf16[32,128,128]{2,1,0:T(8,128)(2,1)S(1)}, u32[]{:S(2)}, u32[]{:S(2)}) %all-to-all-start.1) | async-done | bytes 1048608 | tf_op jit(solution)/shard_map/all_to_all | solution.py:590
  81.7 1.0 copy-done.14
  82.6 8.4 %all-to-all-start.2 = ((bf16[64,8,1024]{2,1,0:T(8,128)(2,1)}), bf16[64,8,1024]{2,1,0:T(8,128)(2,1)S(1)}, u32[]{:S(2)}, u32[]{:S(2)}) async-start(bf16[64,8,1024]{2,1,0:T(8,128)(2,1)} %bitcast.8), calls=%async_computation.2 | async-start | bytes 2097152 | tf_op jit(solution)/shard_map/all_to_all | solution.py:607
  91.1 6.6 %long_back.1 = (bf16[128,256]{1,0:T(8,128)(2,1)}, bf16[128,256]{1,0:T(8,128)(2,1)}, bf16[128,256]{1,0:T(8,128)(2,1)}, bf16[128,256]{1,0:T(8,128)(2,1)}) custom-call(s32[4]{0:T(128)} %blocks_smem.3, bf16[4096,256]{1,0:T(8,128)(2,1)} %bitcast.6, bf16[4096,128]{1,0:T(8,128)(2,1)} %bitcast.11), custom_call_target="tpu_custom_call" | custom-call | flops 6000000000 | bytes 4194304 | tf_op jit(solution)/shard_map/long_back/pallas_call | solution.py:796
  97.7 1.6 %collective-permute-start.7 = (bf16[128,256]{1,0:T(8,128)(2,1)}, bf16[128,256]{1,0:T(8,128)(2,1)S(1)}, u32[]{:S(2)}, u32[]{:S(2)}) collective-permute-start(bf16[128,256]{1,0:T(8,128)(2,1)} %get-tuple-element.94), channel_id=1, source_target_pairs={{0,1},{1,0},{2,3},{3,2},{4,5},{5,4},{6,7},{7,6},{8,9},{9,8},{10,11... | collective-permute-start | bytes 196616 | tf_op jit(solution)/shard_map/ppermute | solution.py:583
  99.2 1.5 %collective-permute-start.8 = (bf16[128,256]{1,0:T(8,128)(2,1)}, bf16[128,256]{1,0:T(8,128)(2,1)S(1)}, u32[]{:S(2)}, u32[]{:S(2)}) collective-permute-start(bf16[128,256]{1,0:T(8,128)(2,1)} %get-tuple-element.95), channel_id=1, source_target_pairs={{0,2},{1,3},{2,0},{3,1},{4,6},{5,7},{6,4},{7,5},{8,10},{9,11},{10,... | collective-permute-start | bytes 196616 | tf_op jit(solution)/shard_map/ppermute | solution.py:583
  101.1 4.6 %collective-permute-done.7.got_1 = bf16[128,256]{1,0:T(8,128)(2,1)S(1)} collective-permute-done((bf16[128,256]{1,0:T(8,128)(2,1)}, bf16[128,256]{1,0:T(8,128)(2,1)S(1)}, u32[]{:S(2)}, u32[]{:S(2)}) %collective-permute-start.7) | collective-permute-done | bytes 65568 | tf_op jit(solution)/shard_map/ppermute | solution.py:583
  105.7 1.7 %collective-permute-done.9.got_3 = bf16[128,256]{1,0:T(8,128)(2,1)S(1)} collective-permute-done((bf16[128,256]{1,0:T(8,128)(2,1)}, bf16[128,256]{1,0:T(8,128)(2,1)S(1)}, u32[]{:S(2)}, u32[]{:S(2)}) %collective-permute-start.9) | collective-permute-done | bytes 65568 | tf_op jit(solution)/shard_map/ppermute | solution.py:583
  107.4 0.8 copy-done.12
  108.3 0.9 collective-permute-start.10
  109.2 1.2 collective-permute-done.10.grad_got
  110.4 1.2 copy-done.10
  111.6 2.5 %late_sums.1 = bf16[512,1024]{1,0:T(8,128)(2,1)} custom-call(bf16[512,1024]{1,0:T(8,128)(2,1)S(1)} %copy-done.10, bf16[512,1024]{1,0:T(8,128)(2,1)} %collective-permute-done.3.got_ref, bf16[128,1024]{1,0:T(8,128)(2,1)S(1)} %copy-done.2, bf16[128,1024]{1,0:T(8,128)(2,1)S(1)} %collective-permute-done.5.half_ref, ...), custom_call_target="tpu_custom_call" | custom-call | flops 268435456 | bytes 5242880 | tf_op jit(solution)/shard_map/late_sums/pallas_call | solution.py:817
  114.2 9.7 %all-to-all-start.3 = ((bf16[64,8,1024]{2,1,0:T(8,128)(2,1)}), bf16[64,8,1024]{2,1,0:T(8,128)(2,1)S(1)}, u32[]{:S(2)}, u32[]{:S(2)}) async-start(bf16[64,8,1024]{2,1,0:T(8,128)(2,1)} %bitcast.9), calls=%async_computation.3 | async-start | bytes 2097152 | tf_op jit(solution)/shard_map/all_to_all | solution.py:607
  123.9 11.1 %input_back.1 = (bf16[1024,1024]{1,0:T(8,128)(2,1)}, bf16[128,1024]{1,0:T(8,128)(2,1)}) custom-call(bf16[1024,512]{1,0:T(8,128)(2,1)} %get-tuple-element.99.grad_gate_ref, bf16[1024,1024]{1,0:T(8,128)(2,1)} %get-tuple-element.100.grad_ref, bf16[1024,1024]{1,0:T(8,128)(2,1)} %cot_ref.9, bf16[1024,1024]{1,0:T(8,128)(2,1)} %get-tuple-element.101.xbf_ref, ...), custom_call_target="tpu_custom_call" | custom-call | flops 3623878656 | bytes 14680064 | tf_op jit(solution)/shard_map/input_back/pallas_call | solution.py:840
  135.2 7.0 %all-to-all-done.3.late_ref = bf16[64,8,1024]{2,1,0:T(8,128)(2,1)S(1)} async-done(((bf16[64,8,1024]{2,1,0:T(8,128)(2,1)}), bf16[64,8,1024]{2,1,0:T(8,128)(2,1)S(1)}, u32[]{:S(2)}, u32[]{:S(2)}) %all-to-all-start.3) | async-done | bytes 1048608 | tf_op jit(solution)/shard_map/all_to_all | solution.py:607
  142.2 0.9 final_sums.1
  (43 shorter events, 2.4 us)
Async XLA Ops:
  4.8 39.5 %all-to-all-start = ((bf16[32,128,256]{2,1,0:T(8,128)(2,1)}), bf16[32,128,256]{2,1,0:T(8,128)(2,1)S(1)}, u32[]{:S(2)}, u32[]{:S(2)}) async-start(bf16[32,128,256]{2,1,0:T(8,128)(2,1)} %bitcast.10), calls=%async_computation | async-start | bytes 4194304 | tf_op jit(solution)/shard_map/all_to_all | solution.py:590
  14.1 31.5 %copy-start.13 = (s32[4]{0:T(128)S(1)}, s32[4]{0:T(128)}, u32[]{:S(2)}) copy-start(s32[4]{0:T(128)} %blocks_smem.3) | copy-start | bytes 52
  44.3 1.3 copy-start.4
  45.6 1.6 %copy-start.5 = (bf16[32,128,256]{2,1,0:T(8,128)(2,1)S(1)}, bf16[32,128,256]{2,1,0:T(8,128)(2,1)}, u32[]{:S(2)}) copy-start(bf16[32,128,256]{2,1,0:T(8,128)(2,1)} %copy-done.4) | copy-start | bytes 6291460
  47.2 5.1 %copy-start = (bf16[1024,1536]{1,0:T(8,128)(2,1)S(1)}, bf16[1024,1536]{1,0:T(8,128)(2,1)}, u32[]{:S(2)}) copy-start(bf16[1024,1536]{1,0:T(8,128)(2,1)} %pin_ref.5) | copy-start | bytes 9437188
  47.2 5.1 %copy-start.1 = (bf16[128,1024]{1,0:T(8,128)(2,1)S(1)}, bf16[128,1024]{1,0:T(8,128)(2,1)}, u32[]{:S(2)}) copy-start(bf16[128,1024]{1,0:T(8,128)(2,1)} %long_cot_ref.1) | copy-start | bytes 786436
  47.2 5.1 %copy-start.2 = (bf16[128,1024]{1,0:T(8,128)(2,1)S(1)}, bf16[128,1024]{1,0:T(8,128)(2,1)}, u32[]{:S(2)}) copy-start(bf16[128,1024]{1,0:T(8,128)(2,1)} %get-tuple-element.66.xbf_ref.long_xbf_ref) | copy-start | bytes 786436
  48.5 6.0 %copy-start.8 = (bf16[128,1024]{1,0:T(8,128)(2,1)S(1)}, bf16[128,1024]{1,0:T(8,128)(2,1)}, u32[]{:S(2)}) copy-start(bf16[128,1024]{1,0:T(8,128)(2,1)} %x_ref.5) | copy-start | bytes 786436
  48.5 6.0 %copy-start.9 = (bf16[512,1024]{1,0:T(8,128)(2,1)S(1)}, bf16[512,1024]{1,0:T(8,128)(2,1)}, u32[]{:S(2)}) copy-start(bf16[512,1024]{1,0:T(8,128)(2,1)} %pout_ref.3) | copy-start | bytes 3145732
  48.5 4.8 %collective-permute-start = (bf16[128,128]{1,0:T(8,128)(2,1)S(1)}, bf16[128,128]{1,0:T(8,128)(2,1)S(1)}, u32[]{:S(2)}, u32[]{:S(2)}) collective-permute-start(bf16[128,128]{1,0:T(8,128)(2,1)S(1)} %get-tuple-element.63), channel_id=1, source_target_pairs={{0,1},{1,0},{2,3},{3,2},{4,5},{5,4},{6,7},{7,6},{8,9},{9,8},{10,11... | collective-permute-start | bytes 98312 | tf_op jit(solution)/shard_map/ppermute | solution.py:583
  48.8 4.5 %collective-permute-start.1 = (bf16[128,128]{1,0:T(8,128)(2,1)S(1)}, bf16[128,128]{1,0:T(8,128)(2,1)S(1)}, u32[]{:S(2)}, u32[]{:S(2)}) collective-permute-start(bf16[128,128]{1,0:T(8,128)(2,1)S(1)} %get-tuple-element.64), channel_id=1, source_target_pairs={{0,2},{1,3},{2,0},{3,1},{4,6},{5,7},{6,4},{7,5},{8,10},{9,11},{10,... | collective-permute-start | bytes 98312 | tf_op jit(solution)/shard_map/ppermute | solution.py:583
  49.3 5.3 %collective-permute-start.2 = (bf16[128,128]{1,0:T(8,128)(2,1)S(1)}, bf16[128,128]{1,0:T(8,128)(2,1)S(1)}, u32[]{:S(2)}, u32[]{:S(2)}) collective-permute-start(bf16[128,128]{1,0:T(8,128)(2,1)S(1)} %get-tuple-element.65), channel_id=1, source_target_pairs={{0,3},{1,2},{2,1},{3,0},{4,7},{5,6},{6,5},{7,4},{8,11},{9,10},{10,... | collective-permute-start | bytes 98312 | tf_op jit(solution)/shard_map/ppermute | solution.py:583
  53.4 9.0 %copy-start.15 = (bf16[128,1024]{1,0:T(8,128)(2,1)S(1)}, bf16[128,1024]{1,0:T(8,128)(2,1)}, u32[]{:S(2)}) copy-start(bf16[128,1024]{1,0:T(8,128)(2,1)} %get-tuple-element.84) | copy-start | bytes 786436
  56.6 6.5 %copy-start.6 = (bf16[128,1024]{1,0:T(8,128)(2,1)S(1)}, bf16[128,1024]{1,0:T(8,128)(2,1)}, u32[]{:S(2)}) copy-start(bf16[128,1024]{1,0:T(8,128)(2,1)} %get-tuple-element.83.mid_ref.long_gate_ref) | copy-start | bytes 786436
  56.6 25.1 %all-to-all-start.1 = ((bf16[32,128,128]{2,1,0:T(8,128)(2,1)}), bf16[32,128,128]{2,1,0:T(8,128)(2,1)S(1)}, u32[]{:S(2)}, u32[]{:S(2)}) async-start(bf16[32,128,128]{2,1,0:T(8,128)(2,1)} %bitcast.12), calls=%async_computation.1 | async-start | bytes 2097152 | tf_op jit(solution)/shard_map/all_to_all | solution.py:590
  62.4 15.3 %collective-permute-start.5 = (bf16[128,1024]{1,0:T(8,128)(2,1)S(1)}, bf16[128,1024]{1,0:T(8,128)(2,1)S(1)}, u32[]{:S(2)}, u32[]{:S(2)}) collective-permute-start(bf16[128,1024]{1,0:T(8,128)(2,1)S(1)} %copy-done.15), channel_id=1, source_target_pairs={{0,32},{32,0},{64,96},{96,64},{1,33},{33,1},{65,97},{97,65},{2,34}... | collective-permute-start | bytes 786440 | tf_op jit(solution)/shard_map/ppermute | solution.py:596
  63.1 14.6 %collective-permute-start.4 = (bf16[128,1024]{1,0:T(8,128)(2,1)S(1)}, bf16[128,1024]{1,0:T(8,128)(2,1)S(1)}, u32[]{:S(2)}, u32[]{:S(2)}) collective-permute-start(bf16[128,1024]{1,0:T(8,128)(2,1)S(1)} %copy-done.6), channel_id=1, source_target_pairs={{0,32},{32,0},{64,96},{96,64},{1,33},{33,1},{65,97},{97,65},{2,34}... | collective-permute-start | bytes 786440 | tf_op jit(solution)/shard_map/ppermute | solution.py:596
  63.2 14.5 %collective-permute-start.6 = (bf16[512,1024]{1,0:T(8,128)(2,1)}, bf16[512,1024]{1,0:T(8,128)(2,1)S(1)}, u32[]{:S(2)}, u32[]{:S(2)}) collective-permute-start(bf16[512,1024]{1,0:T(8,128)(2,1)} %get-tuple-element.85), channel_id=1, source_target_pairs={{0,32},{32,0},{64,96},{96,64},{1,33},{33,1},{65,97},{97,65},{2,34}... | collective-permute-start | bytes 3145736 | tf_op jit(solution)/shard_map/ppermute | solution.py:596
  63.7 14.1 %copy-start.7 = (bf16[512,1024]{1,0:T(8,128)(2,1)S(1)}, bf16[512,1024]{1,0:T(8,128)(2,1)}, u32[]{:S(2)}) copy-start(bf16[512,1024]{1,0:T(8,128)(2,1)} %get-tuple-element.90.mine_ref) | copy-start | bytes 3145732
  77.3 31.9 %collective-permute-start.3 = (bf16[512,1024]{1,0:T(8,128)(2,1)}, bf16[512,1024]{1,0:T(8,128)(2,1)}, u32[]{:S(2)}, u32[]{:S(2)}) collective-permute-start(bf16[512,1024]{1,0:T(8,128)(2,1)} %get-tuple-element.82), channel_id=1, source_target_pairs={{0,32},{32,0},{64,96},{96,64},{1,33},{33,1},{65,97},{97,65},{2,34}... | collective-permute-start | bytes 3145736 | tf_op jit(solution)/shard_map/ppermute | solution.py:596
  81.7 1.0 copy-start.14
  82.6 31.5 %all-to-all-start.2 = ((bf16[64,8,1024]{2,1,0:T(8,128)(2,1)}), bf16[64,8,1024]{2,1,0:T(8,128)(2,1)S(1)}, u32[]{:S(2)}, u32[]{:S(2)}) async-start(bf16[64,8,1024]{2,1,0:T(8,128)(2,1)} %bitcast.8), calls=%async_computation.2 | async-start | bytes 2097152 | tf_op jit(solution)/shard_map/all_to_all | solution.py:607
  91.1 16.3 %copy-start.11 = (bf16[128,1024]{1,0:T(8,128)(2,1)S(1)}, bf16[128,1024]{1,0:T(8,128)(2,1)}, u32[]{:S(2)}) copy-start(bf16[128,1024]{1,0:T(8,128)(2,1)} %get-tuple-element.97.slope_ref) | copy-start | bytes 786436
  97.7 8.0 %collective-permute-start.7 = (bf16[128,256]{1,0:T(8,128)(2,1)}, bf16[128,256]{1,0:T(8,128)(2,1)S(1)}, u32[]{:S(2)}, u32[]{:S(2)}) collective-permute-start(bf16[128,256]{1,0:T(8,128)(2,1)} %get-tuple-element.94), channel_id=1, source_target_pairs={{0,1},{1,0},{2,3},{3,2},{4,5},{5,4},{6,7},{7,6},{8,9},{9,8},{10,11... | collective-permute-start | bytes 196616 | tf_op jit(solution)/shard_map/ppermute | solution.py:583
  99.2 6.5 %collective-permute-start.8 = (bf16[128,256]{1,0:T(8,128)(2,1)}, bf16[128,256]{1,0:T(8,128)(2,1)S(1)}, u32[]{:S(2)}, u32[]{:S(2)}) collective-permute-start(bf16[128,256]{1,0:T(8,128)(2,1)} %get-tuple-element.95), channel_id=1, source_target_pairs={{0,2},{1,3},{2,0},{3,1},{4,6},{5,7},{6,4},{7,5},{8,10},{9,11},{10,... | collective-permute-start | bytes 196616 | tf_op jit(solution)/shard_map/ppermute | solution.py:583
  100.7 6.7 %collective-permute-start.9 = (bf16[128,256]{1,0:T(8,128)(2,1)}, bf16[128,256]{1,0:T(8,128)(2,1)S(1)}, u32[]{:S(2)}, u32[]{:S(2)}) collective-permute-start(bf16[128,256]{1,0:T(8,128)(2,1)} %get-tuple-element.96), channel_id=1, source_target_pairs={{0,3},{1,2},{2,1},{3,0},{4,7},{5,6},{6,5},{7,4},{8,11},{9,10},{10,... | collective-permute-start | bytes 196616 | tf_op jit(solution)/shard_map/ppermute | solution.py:583
  107.4 0.8 copy-start.12
  108.3 5.8 %copy-start.3 = (bf16[128,1024]{1,0:T(8,128)(2,1)}, bf16[128,1024]{1,0:T(8,128)(2,1)S(1)}, u32[]{:S(2)}) copy-start(bf16[128,1024]{1,0:T(8,128)(2,1)S(1)} %long_slopes.1.grad_ref.long_grad_ref) | copy-start | bytes 786436
  108.3 2.0 %collective-permute-start.10 = (bf16[128,1024]{1,0:T(8,128)(2,1)S(1)}, bf16[128,1024]{1,0:T(8,128)(2,1)S(1)}, u32[]{:S(2)}, u32[]{:S(2)}) collective-permute-start(bf16[128,1024]{1,0:T(8,128)(2,1)S(1)} %long_slopes.1.grad_ref.long_grad_ref), channel_id=1, source_target_pairs={{0,32},{32,0},{64,96},{96,64},{1,33},{33,1},{65,97},{97,65},{2,34}... | collective-permute-start | bytes 786440 | tf_op jit(solution)/shard_map/ppermute | solution.py:596
  110.4 1.2 copy-start.10
  114.2 28.1 %all-to-all-start.3 = ((bf16[64,8,1024]{2,1,0:T(8,128)(2,1)}), bf16[64,8,1024]{2,1,0:T(8,128)(2,1)S(1)}, u32[]{:S(2)}, u32[]{:S(2)}) async-start(bf16[64,8,1024]{2,1,0:T(8,128)(2,1)} %bitcast.9), calls=%async_computation.3 | async-start | bytes 2097152 | tf_op jit(solution)/shard_map/all_to_all | solution.py:607

commit v5 on v2

--- a/solution.py
+++ b/solution.py
@@ -117,17 +117,6 @@
             send_ref[copy, which] = act[:, HW * which : HW * (which + 1)]
 
 
-def long_gate_kernel(xbf_ref, pin_ref, cot_ref, gate_ref, slope_gate_ref, half_ref):
-    _, _, group = run_place()
-    part = xbf_ref.shape[1] // 4
-    act, slope = project(xbf_ref[...], pin_ref[...])
-    gate_ref[...] = act
-    slope_gate_ref[...] = slope.astype(BF16)
-    for block, features in split_rows(part, (1 - lax.rem(group, 2)) * part):
-        half_ref[:, block * part : (block + 1) * part] = cot_ref[:, features]
-        half_ref[:, (block + 2) * part : (block + 3) * part] = xbf_ref[:, features]
-
-
 def short_forward_kernel(
     user_ref,
     x_ref,
@@ -135,6 +124,8 @@
     pin_ref,
     proj_ref,
     pout_ref,
+    long_xbf_ref,
+    long_cot_ref,
     out_ref,
     qkv_ref,
     g_ref,
@@ -145,12 +136,27 @@
     inv_ref,
     mine_ref,
     other_ref,
+    long_gate_ref,
+    long_slope_ref,
+    half_ref,
     sum_ref,
     seen_ref,
     mixed_ref,
     side_ref,
 ):
     step = pl.program_id(0)
+
+    @pl.when(step == 0)
+    def _():
+        _, _, group = run_place()
+        part = long_xbf_ref.shape[1] // 4
+        act, slope = project(long_xbf_ref[...], pin_ref[...])
+        long_gate_ref[...] = act
+        long_slope_ref[...] = slope.astype(BF16)
+        for block, features in split_rows(part, (1 - lax.rem(group, 2)) * part):
+            half_ref[:, block * part : (block + 1) * part] = long_cot_ref[:, features]
+            half_ref[:, (block + 2) * part : (block + 3) * part] = long_xbf_ref[:, features]
+
     joined = user_ref[0, 0] == user_ref[0, 1]
     share = jnp.where(joined, 0.5 / BLOCK, 1.0 / BLOCK)
     normed, inv_std = norm_rows(x_ref[...].astype(F32))
@@ -303,18 +309,37 @@
     return pl.ds(pl.multiple_of(index * BLOCK, BLOCK), BLOCK)
 
 
-def long_attend_kernel(blocks_smem, all_ref, *refs):
-    mixed_refs, acc_ref = refs[:H], refs[H]
+def long_attend_kernel(blocks_smem, all_hbm, *refs):
+    mixed_refs, (acc_ref, all_ref, sems) = refs[:H], refs[H:]
     mine, chunk, group = run_place()
     valid = blocks_smem[group]
+
+    def block_copy(index):
+        rows = rows_at(index)
+        return pltpu.make_async_copy(all_hbm.at[rows], all_ref.at[rows], sems.at[index])
+
+    block_copy(chunk).start()
+
+    @pl.loop(0, chunk)
+    def _(index):
+        block_copy(index).start()
+
     acc_ref[...] = jnp.zeros_like(acc_ref)
-
-    @pl.when(chunk < valid)
-    def _():
-        side = score_side(all_ref[rows_at(chunk), : 2 * KW])
-
+    block_copy(chunk).wait()
+
+    @pl.when(chunk >= valid)
+    def _():
         @pl.loop(0, chunk)
         def _(index):
+            block_copy(index).wait()
+
+    @pl.when(chunk < valid)
+    def _():
+        side = score_side(all_ref[rows_at(chunk), : 2 * KW])
+
+        @pl.loop(0, chunk)
+        def _(index):
+            block_copy(index).wait()
             scores = dot(side, all_ref[rows_at(index), : 2 * KW], 1, 1)
             acc_ref[...] += dot(
                 silu_half(scores).astype(BF16), all_ref[rows_at(index), 2 * KW :], 1, 0
@@ -616,29 +641,6 @@
         ],
     )(x_long, proj_in, proj_in, proj_in)
     whole = spread_heads(sent)
-    gate_long, slope_long, half_other = call(
-        long_gate_kernel,
-        (
-            shaped((long_rows, gates)),
-            shaped((long_rows, gates)),
-            in_hbm((long_rows, width)),
-        ),
-        2 * long_rows * width * gates,
-        4 * 2**20,
-        "long_gate",
-        grid=(1,),
-        in_specs=[
-            fixed_spec(long_rows, width),
-            fixed_spec(width, gates),
-            fixed_spec(long_rows, width),
-        ],
-        out_specs=[
-            fixed_spec(long_rows, gates),
-            fixed_spec(long_rows, gates),
-            fixed_spec(long_rows, width),
-        ],
-    )(xbf_long, proj_in, cot_long)
-
     short_out = call(
         short_forward_kernel,
         (
@@ -652,6 +654,9 @@
             in_hbm((short_rows, 1), F32),
             in_hbm((half, 2 * gates)),
             in_hbm((half, 2 * gates)),
+            in_hbm((long_rows, gates)),
+            in_hbm((long_rows, gates)),
+            in_hbm((long_rows, width)),
         ),
         20 * 10**9,
         24 * 2**20,
@@ -665,6 +670,8 @@
             fixed_spec(width, gates),
             fixed_spec(width, rest),
             fixed_spec(gates, width),
+            fixed_spec(long_rows, width),
+            fixed_spec(long_rows, width),
         ],
         out_specs=[
             rows_spec(BLOCK, width),
@@ -677,6 +684,9 @@
             rows_spec(BLOCK, 1),
             fixed_spec(half, 2 * gates),
             fixed_spec(half, 2 * gates),
+            fixed_spec(long_rows, gates),
+            fixed_spec(long_rows, gates),
+            fixed_spec(long_rows, width),
         ],
         scratch_shapes=[
             pltpu.VMEM((width, 2 * gates), F32),
@@ -684,9 +694,10 @@
             pltpu.VMEM((BLOCK, gates), F32),
             pltpu.VMEM((BLOCK, 2 * KW * H), BF16),
         ],
-    )(short_user, x_short, cot_short, proj_in, proj, proj_out)
+    )(short_user, x_short, cot_short, proj_in, proj, proj_out, xbf_long, cot_long)
     out_short, qkv_short, g_short, gate_short, slope_short, xbf_short = short_out[:6]
-    turned_short, inv_short, early_mine, early_other = short_out[6:]
+    turned_short, inv_short, early_mine, early_other = short_out[6:10]
+    gate_long, slope_long, half_other = short_out[10:]
     early_got = swap_cores(early_other)
 
 
@@ -697,9 +708,12 @@
         2 * 10**9,
         2 * 2**20,
         "long_attend",
-        in_specs=[SMEM, WHOLE],
+        vmem=62,
+        in_specs=[SMEM, pl.BlockSpec(memory_space=pl.ANY)],
         scratch_shapes=[
             pltpu.VMEM((BLOCK, VW), F32),
+            pltpu.VMEM((chunks * BLOCK, HW), BF16),
+            pltpu.SemaphoreType.DMA((chunks,)),
         ],
     )(long_blocks, whole)
     out_long, sent, mid = call(
@@ -762,6 +776,7 @@
         6 * 10**9,
         4 * 2**20,
         "long_back",
+        vmem=62,
         in_specs=[SMEM, WHOLE, WHOLE],
         scratch_shapes=[
             pltpu.VMEM((BLOCK, 2 * KW), F32),

time: 145 us -> 147 us (1.014)
  starting transfers between devices: 45.6 us -> 49.4 us
  Pallas kernels: 70 us -> 67.4 us
    ppermute x5, starting transfers between devices: 1.15 us -> 5.68 us  [swap_cores(): return lax.ppermute(half, 'dp', [(src, src ^ 1) for src in range(size)])]
    pallas_call x1, Pallas kernels: 17.2 us -> 13.4 us  [body(): call(short_back_kernel, (in_hbm((short_rows, rest)), in_hbm((half, rest))...]
    pallas_call x1, Pallas kernels: 1.17 us -> 3.07 us  [body(): call(long_attend_kernel, (shaped((long_rows, VW)),) * H, 2 * 10 ** 9, 2 *...]
    unnamed x36 -> x32, local copies, waits for them, and re-layouts: 3.97 us -> 3.56 us
  transfers between devices with their start and end apart: 15 -> 15, of which waited for: 8 -> 8; matrix products, arithmetic and copies ran while one was open for 1% -> 1% of each run, Pallas kernels for 43% -> 39%
where the time goes in v5:
time: 147 us; the launch traced here: 146 us
  Pallas kernels  67.4 us (46%)
  starting transfers between devices  49.4 us (34%)
  waiting for transfers between devices  23.8 us (16%)
  local copies, waits for them, and re-layouts  3.56 us (2%)
    pallas_call x1, Pallas kernels, body(): call(short_forward_kernel, (in_hbm((short_rows, width)), in_hbm((short_ro...  21 us
    all_to_all x2, starting transfers between devices, scatter_pairs(): lax.all_to_all(sent, ('dp', 'sp'), 0, 0, tiled=True, axis_index_groups=gr...  20.8 us
    all_to_all x2, starting transfers between devices, spread_heads(): lax.all_to_all(sent.reshape(chunks * heads, rows, cols), 'sp', 0, 0, tile...  15.9 us
    pallas_call x1, Pallas kernels, body(): call(short_back_kernel, (in_hbm((short_rows, rest)), in_hbm((half, rest))...  13.4 us
    pallas_call x1, Pallas kernels, body(): call(input_back_kernel, (in_hbm((short_rows, width)), in_hbm((long_rows,...  11.2 us
    ppermute x6, waiting for transfers between devices, swap_heads(): lax.ppermute(pieces[bits], 'sp', [(src, src ^ bits) for src in range(size)])  8.58 us
    pallas_call x1, Pallas kernels, body(): call(long_back_kernel, (shaped((long_rows, HW)),) * H, 6 * 10 ** 9, 4 * 2...  7.49 us
    ppermute x6, starting transfers between devices, swap_heads(): lax.ppermute(pieces[bits], 'sp', [(src, src ^ bits) for src in range(size)])  7.05 us
  transfers between devices with their start and end apart: 15, of which 8 were waited for; matrix products, arithmetic and copies ran while one was open for 1% of the time, Pallas kernels for 39%

profile of v5, /device:TPU:0, one launch (start us, length us, event | category | flops | bytes accessed | tf_op | source)
XLA Modules:
  0.0 146.4 jit_solution(11868891165613722857)
XLA Ops:
  0.6 4.2 %long_project.1 = (bf16[1024,1024]{1,0:T(8,128)(2,1)}, bf16[8,4,128,256]{3,2,1,0:T(8,128)(2,1)}, f32[128,1]{1,0:T(8,128)}, bf16[128,1024]{1,0:T(8,128)(2,1)}, bf16[128,1024]{1,0:T(8,128)(2,1)}) custom-call(bf16[128,1024]{1,0:T(8,128)(2,1)} %x_ref.5, bf16[1024,1536]{1,0:T(8,128)(2,1)} %pin_ref.3, bf16[1024,1536]{1,0:T(8,128)(2,1)} %pin_ref.3, ...), custom_call_target="tpu_custom_call" | custom-call | flops 268435456 | bytes 8388608 | tf_op jit(solution)/shard_map/long_project/pallas_call | solution.py:615
  4.8 9.4 %all-to-all-start = ((bf16[32,128,256]{2,1,0:T(8,128)(2,1)}), bf16[32,128,256]{2,1,0:T(8,128)(2,1)}, u32[]{:S(2)}, u32[]{:S(2)}) async-start(bf16[32,128,256]{2,1,0:T(8,128)(2,1)} %bitcast.8), calls=%async_computation | async-start | bytes 4194304 | tf_op jit(solution)/shard_map/all_to_all | solution.py:585
  14.3 21.0 %short_forward.1 = (bf16[1024,1024]{1,0:T(8,128)(2,1)}, bf16[1024,1024]{1,0:T(8,128)(2,1)}, bf16[1024,512]{1,0:T(8,128)(2,1)}, bf16[1024,512]{1,0:T(8,128)(2,1)}...) custom-call(s32[1,2]{1,0:T(1,128)} %user_ref.3, ...), custom_call_target="tpu_custom_call" | custom-call | flops 20000000000 | bytes 25165824 | tf_op jit(solution)/shard_map/short_forward/pallas_call | solution.py:644
  35.3 0.9 collective-permute-start
  36.2 2.5 %collective-permute-done.got_ref = bf16[512,1024]{1,0:T(8,128)(2,1)S(1)} collective-permute-done((bf16[512,1024]{1,0:T(8,128)(2,1)}, bf16[512,1024]{1,0:T(8,128)(2,1)S(1)}, u32[]{:S(2)}, u32[]{:S(2)}) %collective-permute-start) | collective-permute-done | bytes 1048608 | tf_op jit(solution)/shard_map/ppermute | solution.py:591
  38.7 5.8 %all-to-all-done = bf16[32,128,256]{2,1,0:T(8,128)(2,1)} async-done(((bf16[32,128,256]{2,1,0:T(8,128)(2,1)}), bf16[32,128,256]{2,1,0:T(8,128)(2,1)}, u32[]{:S(2)}, u32[]{:S(2)}) %all-to-all-start) | async-done | bytes 2097184 | tf_op jit(solution)/shard_map/all_to_all | solution.py:585
  44.5 3.1 %long_attend.1 = (bf16[128,128]{1,0:T(8,128)(2,1)}, bf16[128,128]{1,0:T(8,128)(2,1)}, bf16[128,128]{1,0:T(8,128)(2,1)}, bf16[128,128]{1,0:T(8,128)(2,1)}) custom-call(s32[4]{0:T(128)} %blocks_smem.3, bf16[4096,256]{1,0:T(8,128)(2,1)} %bitcast.1.all_hbm.all_ref), custom_call_target="tpu_custom_call" | custom-call | flops 2000000000 | bytes 2097152 | tf_op jit(solution)/shard_map/long_attend/pallas_call | solution.py:705
  48.1 3.0 %collective-permute-start.3 = (bf16[128,128]{1,0:T(8,128)(2,1)}, bf16[128,128]{1,0:T(8,128)(2,1)S(1)}, u32[]{:S(2)}, u32[]{:S(2)}) collective-permute-start(bf16[128,128]{1,0:T(8,128)(2,1)} %get-tuple-element.65), channel_id=1, source_target_pairs={{0,3},{1,2},{2,1},{3,0},{4,7},{5,6},{6,5},{7,4},{8,11},{9,10},{10,... | collective-permute-start | bytes 98312 | tf_op jit(solution)/shard_map/ppermute | solution.py:578
  51.1 0.6 collective-permute-done.1.got_1
  51.8 1.7 %collective-permute-done.3.got_3 = bf16[128,128]{1,0:T(8,128)(2,1)S(1)} collective-permute-done((bf16[128,128]{1,0:T(8,128)(2,1)}, bf16[128,128]{1,0:T(8,128)(2,1)S(1)}, u32[]{:S(2)}, u32[]{:S(2)}) %collective-permute-start.3) | collective-permute-done | bytes 32800 | tf_op jit(solution)/shard_map/ppermute | solution.py:578
  53.6 1.2 copy-done.8
  54.8 0.8 copy-done.14
  55.6 2.1 %long_head.1 = (bf16[128,1024]{1,0:T(8,128)(2,1)}, bf16[8,4,128,128]{3,2,1,0:T(8,128)(2,1)}, bf16[128,1024]{1,0:T(8,128)(2,1)}) custom-call(bf16[128,128]{1,0:T(8,128)(2,1)S(1)} %copy-done.14, bf16[128,128]{1,0:T(8,128)(2,1)S(1)} %collective-permute-done.1.got_1, bf16[128,128]{1,0:T(8,128)(2,1)S(1)} %collective-permute-done.2.got_2, ...), custom_call_target="tpu_custom_call" | custom-call | flops 268435456 | bytes 3145728 | tf_op jit(solution)/shard_map/long_head/pallas_call | solution.py:719
  57.6 6.5 %all-to-all-start.1 = ((bf16[32,128,128]{2,1,0:T(8,128)(2,1)}), bf16[32,128,128]{2,1,0:T(8,128)(2,1)}, u32[]{:S(2)}, u32[]{:S(2)}) async-start(bf16[32,128,128]{2,1,0:T(8,128)(2,1)} %bitcast.9), calls=%async_computation.1 | async-start | bytes 2097152 | tf_op jit(solution)/shard_map/all_to_all | solution.py:585
  64.7 13.4 %short_back.1 = (bf16[1024,1024]{1,0:T(8,128)(2,1)}, bf16[512,1024]{1,0:T(8,128)(2,1)}, bf16[512,1024]{1,0:T(8,128)(2,1)}) custom-call(s32[1,2]{1,0:T(1,128)} %user_ref.3, bf16[1024,1024]{1,0:T(8,128)(2,1)} %get-tuple-element.74.qkv_ref, bf16[1024,512]{1,0:T(8,128)(2,1)} %get-tuple-element.75.g_ref, bf16[1024,1024]{1,0:T(8,128)(2,1)} %get-tuple-element.76.slope_ref, ...), custom_call_target="tpu_custom_call" | custom-call | flops 16000000000 | bytes 13631488 | tf_op jit(solution)/shard_map/short_back/pallas_call | solution.py:736
  78.1 3.7 %collective-permute-start.4 = (bf16[512,1024]{1,0:T(8,128)(2,1)}, bf16[512,1024]{1,0:T(8,128)(2,1)}, u32[]{:S(2)}, u32[]{:S(2)}) collective-permute-start(bf16[512,1024]{1,0:T(8,128)(2,1)} %get-tuple-element.79), channel_id=1, source_target_pairs={{0,32},{32,0},{64,96},{96,64},{1,33},{33,1},{65,97},{97,65},{2,34}... | collective-permute-start | bytes 3145736 | tf_op jit(solution)/shard_map/ppermute | solution.py:591
  81.9 1.5 %early_sums.1 = bf16[512,1024]{1,0:T(8,128)(2,1)} custom-call(bf16[128,1024]{1,0:T(8,128)(2,1)S(1)} %copy-done.1, bf16[128,1024]{1,0:T(8,128)(2,1)S(1)} %copy-done, bf16[128,1024]{1,0:T(8,128)(2,1)S(1)} %copy-done.3, bf16[128,1024]{1,0:T(8,128)(2,1)S(1)} %collective-permute-done.6.half_ref, bf16[128,1024]{1,0:T(8,128)(2,1)S(1)} %collective-permute-done.5.mid_got, ...), custom_call_target="tpu_custom_call" | custom-call | flops 268435456 | bytes 5242880 | tf_op jit(solution)/shard_map/early_sums/pallas_call | solution.py:763
  83.4 0.7 copy-done.6
  84.1 11.4 %all-to-all-start.2 = ((bf16[64,8,1024]{2,1,0:T(8,128)(2,1)}), bf16[64,8,1024]{2,1,0:T(8,128)(2,1)}, u32[]{:S(2)}, u32[]{:S(2)}) async-start(bf16[64,8,1024]{2,1,0:T(8,128)(2,1)} %bitcast.6), calls=%async_computation.2 | async-start | bytes 2097152 | tf_op jit(solution)/shard_map/all_to_all | solution.py:602
  95.5 7.5 %long_back.1 = (bf16[128,256]{1,0:T(8,128)(2,1)}, bf16[128,256]{1,0:T(8,128)(2,1)}, bf16[128,256]{1,0:T(8,128)(2,1)}, bf16[128,256]{1,0:T(8,128)(2,1)}) custom-call(s32[4]{0:T(128)} %blocks_smem.3, bf16[4096,256]{1,0:T(8,128)(2,1)} %bitcast.1.all_hbm.all_ref, bf16[4096,128]{1,0:T(8,128)(2,1)} %bitcast.3.g_ref), custom_call_target="tpu_custom_call" | custom-call | flops 6000000000 | bytes 4194304 | tf_op jit(solution)/shard_map/long_back/pallas_call | solution.py:773
  103.0 1.5 %collective-permute-start.7 = (bf16[128,256]{1,0:T(8,128)(2,1)}, bf16[128,256]{1,0:T(8,128)(2,1)S(1)}, u32[]{:S(2)}, u32[]{:S(2)}) collective-permute-start(bf16[128,256]{1,0:T(8,128)(2,1)} %get-tuple-element.90), channel_id=1, source_target_pairs={{0,1},{1,0},{2,3},{3,2},{4,5},{5,4},{6,7},{7,6},{8,9},{9,8},{10,11... | collective-permute-start | bytes 196616 | tf_op jit(solution)/shard_map/ppermute | solution.py:578
  104.5 1.5 %collective-permute-start.8 = (bf16[128,256]{1,0:T(8,128)(2,1)}, bf16[128,256]{1,0:T(8,128)(2,1)S(1)}, u32[]{:S(2)}, u32[]{:S(2)}) collective-permute-start(bf16[128,256]{1,0:T(8,128)(2,1)} %get-tuple-element.91), channel_id=1, source_target_pairs={{0,2},{1,3},{2,0},{3,1},{4,6},{5,7},{6,4},{7,5},{8,10},{9,11},{10,... | collective-permute-start | bytes 196616 | tf_op jit(solution)/shard_map/ppermute | solution.py:578
  105.9 0.5 collective-permute-start.9
  106.5 6.1 %collective-permute-done.7.got_1 = bf16[128,256]{1,0:T(8,128)(2,1)S(1)} collective-permute-done((bf16[128,256]{1,0:T(8,128)(2,1)}, bf16[128,256]{1,0:T(8,128)(2,1)S(1)}, u32[]{:S(2)}, u32[]{:S(2)}) %collective-permute-start.7) | collective-permute-done | bytes 65568 | tf_op jit(solution)/shard_map/ppermute | solution.py:578
  112.6 0.8 copy-done.13
  114.1 1.2 collective-permute-done.10.grad_got
  115.2 2.6 %late_sums.1 = bf16[512,1024]{1,0:T(8,128)(2,1)} custom-call(bf16[512,1024]{1,0:T(8,128)(2,1)S(1)} %copy-done.9, bf16[512,1024]{1,0:T(8,128)(2,1)} %collective-permute-done.4.got_ref, bf16[128,1024]{1,0:T(8,128)(2,1)S(1)} %copy-done.1, bf16[128,1024]{1,0:T(8,128)(2,1)S(1)} %copy-done.7, bf16[128,1024]{1,0:T(8,128)(2,1)S(1)} %long_slopes.1.grad_ref.long_grad_ref, ...), custom_call_target="tpu_custom_call" | custom-call | flops 268435456 | bytes 5242880 | tf_op jit(solution)/shard_map/late_sums/pallas_call | solution.py:794
  117.8 9.4 %all-to-all-start.3 = ((bf16[64,8,1024]{2,1,0:T(8,128)(2,1)}), bf16[64,8,1024]{2,1,0:T(8,128)(2,1)S(1)}, u32[]{:S(2)}, u32[]{:S(2)}) async-start(bf16[64,8,1024]{2,1,0:T(8,128)(2,1)} %bitcast.7), calls=%async_computation.3 | async-start | bytes 2097152 | tf_op jit(solution)/shard_map/all_to_all | solution.py:602
  127.2 11.2 %input_back.1 = (bf16[1024,1024]{1,0:T(8,128)(2,1)}, bf16[128,1024]{1,0:T(8,128)(2,1)}) custom-call(bf16[1024,512]{1,0:T(8,128)(2,1)} %get-tuple-element.95.grad_gate_ref, bf16[1024,1024]{1,0:T(8,128)(2,1)} %get-tuple-element.96.grad_ref, bf16[1024,1024]{1,0:T(8,128)(2,1)} %cot_ref.7, bf16[1024,1024]{1,0:T(8,128)(2,1)} %get-tuple-element.97.xbf_ref, ...), custom_call_target="tpu_custom_call" | custom-call | flops 3623878656 | bytes 14680064 | tf_op jit(solution)/shard_map/input_back/pallas_call | solution.py:817
  138.3 1.4 convert_reduce_fusion.early_ref
  139.7 5.8 %all-to-all-done.3.late_ref = bf16[64,8,1024]{2,1,0:T(8,128)(2,1)S(1)} async-done(((bf16[64,8,1024]{2,1,0:T(8,128)(2,1)}), bf16[64,8,1024]{2,1,0:T(8,128)(2,1)S(1)}, u32[]{:S(2)}, u32[]{:S(2)}) %all-to-all-start.3) | async-done | bytes 1048608 | tf_op jit(solution)/shard_map/all_to_all | solution.py:602
  145.5 0.9 final_sums.1
  (42 shorter events, 1.8 us)
Async XLA Ops:
  4.8 39.6 %all-to-all-start = ((bf16[32,128,256]{2,1,0:T(8,128)(2,1)}), bf16[32,128,256]{2,1,0:T(8,128)(2,1)}, u32[]{:S(2)}, u32[]{:S(2)}) async-start(bf16[32,128,256]{2,1,0:T(8,128)(2,1)} %bitcast.8), calls=%async_computation | async-start | bytes 4194304 | tf_op jit(solution)/shard_map/all_to_all | solution.py:585
  35.3 3.4 %collective-permute-start = (bf16[512,1024]{1,0:T(8,128)(2,1)}, bf16[512,1024]{1,0:T(8,128)(2,1)S(1)}, u32[]{:S(2)}, u32[]{:S(2)}) collective-permute-start(bf16[512,1024]{1,0:T(8,128)(2,1)} %get-tuple-element.59), channel_id=1, source_target_pairs={{0,32},{32,0},{64,96},{96,64},{1,33},{33,1},{65,97},{97,65},{2,34}... | collective-permute-start | bytes 3145736 | tf_op jit(solution)/shard_map/ppermute | solution.py:591
  44.4 9.1 %copy-start = (bf16[128,1024]{1,0:T(8,128)(2,1)S(1)}, bf16[128,1024]{1,0:T(8,128)(2,1)}, u32[]{:S(2)}) copy-start(bf16[128,1024]{1,0:T(8,128)(2,1)} %long_cot_ref.3) | copy-start | bytes 786436
  44.5 9.1 %copy-start.5 = (bf16[128,1024]{1,0:T(8,128)(2,1)S(1)}, bf16[128,1024]{1,0:T(8,128)(2,1)}, u32[]{:S(2)}) copy-start(bf16[128,1024]{1,0:T(8,128)(2,1)} %x_ref.5) | copy-start | bytes 786436
  44.5 9.1 %copy-start.11 = (bf16[128,512]{1,0:T(8,128)(2,1)S(1)}, bf16[128,512]{1,0:T(8,128)(2,1)}, u32[]{:S(2)}) copy-start(bf16[128,512]{1,0:T(8,128)(2,1)} %get-tuple-element.66.gate_ref) | copy-start | bytes 393220
  44.5 9.1 %copy-start.12 = (bf16[128,512]{1,0:T(8,128)(2,1)S(1)}, bf16[128,512]{1,0:T(8,128)(2,1)}, u32[]{:S(2)}) copy-start(bf16[128,512]{1,0:T(8,128)(2,1)} %get-tuple-element.67.slope_ref) | copy-start | bytes 393220
  47.5 4.2 %collective-permute-start.1 = (bf16[128,128]{1,0:T(8,128)(2,1)}, bf16[128,128]{1,0:T(8,128)(2,1)S(1)}, u32[]{:S(2)}, u32[]{:S(2)}) collective-permute-start(bf16[128,128]{1,0:T(8,128)(2,1)} %get-tuple-element.63), channel_id=1, source_target_pairs={{0,1},{1,0},{2,3},{3,2},{4,5},{5,4},{6,7},{7,6},{8,9},{9,8},{10,11... | collective-permute-start | bytes 98312 | tf_op jit(solution)/shard_map/ppermute | solution.py:578
  47.6 4.2 %collective-permute-start.2 = (bf16[128,128]{1,0:T(8,128)(2,1)}, bf16[128,128]{1,0:T(8,128)(2,1)S(1)}, u32[]{:S(2)}, u32[]{:S(2)}) collective-permute-start(bf16[128,128]{1,0:T(8,128)(2,1)} %get-tuple-element.64), channel_id=1, source_target_pairs={{0,2},{1,3},{2,0},{3,1},{4,6},{5,7},{6,4},{7,5},{8,10},{9,11},{10,... | collective-permute-start | bytes 98312 | tf_op jit(solution)/shard_map/ppermute | solution.py:578
  48.1 5.5 %collective-permute-start.3 = (bf16[128,128]{1,0:T(8,128)(2,1)}, bf16[128,128]{1,0:T(8,128)(2,1)S(1)}, u32[]{:S(2)}, u32[]{:S(2)}) collective-permute-start(bf16[128,128]{1,0:T(8,128)(2,1)} %get-tuple-element.65), channel_id=1, source_target_pairs={{0,3},{1,2},{2,1},{3,0},{4,7},{5,6},{6,5},{7,4},{8,11},{9,10},{10,... | collective-permute-start | bytes 98312 | tf_op jit(solution)/shard_map/ppermute | solution.py:578
  53.6 1.2 copy-start.8
  54.8 0.8 copy-start.14
  55.6 8.6 %copy-start.15 = (bf16[128,1024]{1,0:T(8,128)(2,1)S(1)}, bf16[128,1024]{1,0:T(8,128)(2,1)}, u32[]{:S(2)}) copy-start(bf16[128,1024]{1,0:T(8,128)(2,1)} %get-tuple-element.81) | copy-start | bytes 786436
  57.6 6.6 %copy-start.3 = (bf16[128,1024]{1,0:T(8,128)(2,1)S(1)}, bf16[128,1024]{1,0:T(8,128)(2,1)}, u32[]{:S(2)}) copy-start(bf16[128,1024]{1,0:T(8,128)(2,1)} %get-tuple-element.80.mid_ref.long_gate_ref) | copy-start | bytes 786436
  57.6 26.4 %all-to-all-start.1 = ((bf16[32,128,128]{2,1,0:T(8,128)(2,1)}), bf16[32,128,128]{2,1,0:T(8,128)(2,1)}, u32[]{:S(2)}, u32[]{:S(2)}) async-start(bf16[32,128,128]{2,1,0:T(8,128)(2,1)} %bitcast.9), calls=%async_computation.1 | async-start | bytes 2097152 | tf_op jit(solution)/shard_map/all_to_all | solution.py:585
  64.2 17.7 %collective-permute-start.6 = (bf16[128,1024]{1,0:T(8,128)(2,1)S(1)}, bf16[128,1024]{1,0:T(8,128)(2,1)S(1)}, u32[]{:S(2)}, u32[]{:S(2)}) collective-permute-start(bf16[128,1024]{1,0:T(8,128)(2,1)S(1)} %copy-done.15), channel_id=1, source_target_pairs={{0,32},{32,0},{64,96},{96,64},{1,33},{33,1},{65,97},{97,65},{2,34}... | collective-permute-start | bytes 786440 | tf_op jit(solution)/shard_map/ppermute | solution.py:591
  64.3 17.6 %collective-permute-start.5 = (bf16[128,1024]{1,0:T(8,128)(2,1)S(1)}, bf16[128,1024]{1,0:T(8,128)(2,1)S(1)}, u32[]{:S(2)}, u32[]{:S(2)}) collective-permute-start(bf16[128,1024]{1,0:T(8,128)(2,1)S(1)} %copy-done.3), channel_id=1, source_target_pairs={{0,32},{32,0},{64,96},{96,64},{1,33},{33,1},{65,97},{97,65},{2,34}... | collective-permute-start | bytes 786440 | tf_op jit(solution)/shard_map/ppermute | solution.py:591
  64.7 17.1 %copy-start.1 = (bf16[128,1024]{1,0:T(8,128)(2,1)S(1)}, bf16[128,1024]{1,0:T(8,128)(2,1)}, u32[]{:S(2)}) copy-start(bf16[128,1024]{1,0:T(8,128)(2,1)} %get-tuple-element.58.long_xbf_ref.xbf_ref) | copy-start | bytes 786436
  64.7 17.1 %copy-start.4 = (bf16[512,1024]{1,0:T(8,128)(2,1)S(1)}, bf16[512,1024]{1,0:T(8,128)(2,1)}, u32[]{:S(2)}) copy-start(bf16[512,1024]{1,0:T(8,128)(2,1)} %get-tuple-element.86.mine_ref) | copy-start | bytes 3145732
  78.1 35.9 %collective-permute-start.4 = (bf16[512,1024]{1,0:T(8,128)(2,1)}, bf16[512,1024]{1,0:T(8,128)(2,1)}, u32[]{:S(2)}, u32[]{:S(2)}) collective-permute-start(bf16[512,1024]{1,0:T(8,128)(2,1)} %get-tuple-element.79), channel_id=1, source_target_pairs={{0,32},{32,0},{64,96},{96,64},{1,33},{33,1},{65,97},{97,65},{2,34}... | collective-permute-start | bytes 3145736 | tf_op jit(solution)/shard_map/ppermute | solution.py:591
  83.4 0.7 copy-start.6
  84.1 33.7 %all-to-all-start.2 = ((bf16[64,8,1024]{2,1,0:T(8,128)(2,1)}), bf16[64,8,1024]{2,1,0:T(8,128)(2,1)}, u32[]{:S(2)}, u32[]{:S(2)}) async-start(bf16[64,8,1024]{2,1,0:T(8,128)(2,1)} %bitcast.6), calls=%async_computation.2 | async-start | bytes 2097152 | tf_op jit(solution)/shard_map/all_to_all | solution.py:602
  95.5 17.1 %copy-start.10 = (bf16[128,1024]{1,0:T(8,128)(2,1)S(1)}, bf16[128,1024]{1,0:T(8,128)(2,1)}, u32[]{:S(2)}) copy-start(bf16[128,1024]{1,0:T(8,128)(2,1)} %get-tuple-element.93.slope_ref) | copy-start | bytes 786436
  95.5 19.7 %copy-start.7 = (bf16[128,1024]{1,0:T(8,128)(2,1)S(1)}, bf16[128,1024]{1,0:T(8,128)(2,1)}, u32[]{:S(2)}) copy-start(bf16[128,1024]{1,0:T(8,128)(2,1)} %copy-done.6) | copy-start | bytes 786436
  95.5 19.7 %copy-start.9 = (bf16[512,1024]{1,0:T(8,128)(2,1)S(1)}, bf16[512,1024]{1,0:T(8,128)(2,1)}, u32[]{:S(2)}) copy-start(bf16[512,1024]{1,0:T(8,128)(2,1)} %get-tuple-element.78.mine_ref) | copy-start | bytes 3145732
  103.0 9.6 %collective-permute-start.7 = (bf16[128,256]{1,0:T(8,128)(2,1)}, bf16[128,256]{1,0:T(8,128)(2,1)S(1)}, u32[]{:S(2)}, u32[]{:S(2)}) collective-permute-start(bf16[128,256]{1,0:T(8,128)(2,1)} %get-tuple-element.90), channel_id=1, source_target_pairs={{0,1},{1,0},{2,3},{3,2},{4,5},{5,4},{6,7},{7,6},{8,9},{9,8},{10,11... | collective-permute-start | bytes 196616 | tf_op jit(solution)/shard_map/ppermute | solution.py:578
  104.5 8.1 %collective-permute-start.8 = (bf16[128,256]{1,0:T(8,128)(2,1)}, bf16[128,256]{1,0:T(8,128)(2,1)S(1)}, u32[]{:S(2)}, u32[]{:S(2)}) collective-permute-start(bf16[128,256]{1,0:T(8,128)(2,1)} %get-tuple-element.91), channel_id=1, source_target_pairs={{0,2},{1,3},{2,0},{3,1},{4,6},{5,7},{6,4},{7,5},{8,10},{9,11},{10,... | collective-permute-start | bytes 196616 | tf_op jit(solution)/shard_map/ppermute | solution.py:578
  105.9 6.7 %collective-permute-start.9 = (bf16[128,256]{1,0:T(8,128)(2,1)}, bf16[128,256]{1,0:T(8,128)(2,1)S(1)}, u32[]{:S(2)}, u32[]{:S(2)}) collective-permute-start(bf16[128,256]{1,0:T(8,128)(2,1)} %get-tuple-element.92), channel_id=1, source_target_pairs={{0,3},{1,2},{2,1},{3,0},{4,7},{5,6},{6,5},{7,4},{8,11},{9,10},{10,... | collective-permute-start | bytes 196616 | tf_op jit(solution)/shard_map/ppermute | solution.py:578
  112.6 0.8 copy-start.13
  113.6 4.2 %copy-start.2 = (bf16[128,1024]{1,0:T(8,128)(2,1)}, bf16[128,1024]{1,0:T(8,128)(2,1)S(1)}, u32[]{:S(2)}) copy-start(bf16[128,1024]{1,0:T(8,128)(2,1)S(1)} %long_slopes.1.grad_ref.long_grad_ref) | copy-start | bytes 786436
  113.6 1.6 %collective-permute-start.10 = (bf16[128,1024]{1,0:T(8,128)(2,1)S(1)}, bf16[128,1024]{1,0:T(8,128)(2,1)S(1)}, u32[]{:S(2)}, u32[]{:S(2)}) collective-permute-start(bf16[128,1024]{1,0:T(8,128)(2,1)S(1)} %long_slopes.1.grad_ref.long_grad_ref), channel_id=1, source_target_pairs={{0,32},{32,0},{64,96},{96,64},{1,33},{33,1},{65,97},{97,65},{2,34}... | collective-permute-start | bytes 786440 | tf_op jit(solution)/shard_map/ppermute | solution.py:591
  117.8 27.7 %all-to-all-start.3 = ((bf16[64,8,1024]{2,1,0:T(8,128)(2,1)}), bf16[64,8,1024]{2,1,0:T(8,128)(2,1)S(1)}, u32[]{:S(2)}, u32[]{:S(2)}) async-start(bf16[64,8,1024]{2,1,0:T(8,128)(2,1)} %bitcast.7), calls=%async_computation.3 | async-start | bytes 2097152 | tf_op jit(solution)/shard_map/all_to_all | solution.py:602

commit v6 on v5

--- a/solution.py
+++ b/solution.py
@@ -309,37 +309,18 @@
     return pl.ds(pl.multiple_of(index * BLOCK, BLOCK), BLOCK)
 
 
-def long_attend_kernel(blocks_smem, all_hbm, *refs):
-    mixed_refs, (acc_ref, all_ref, sems) = refs[:H], refs[H:]
+def long_attend_kernel(blocks_smem, all_ref, *refs):
+    mixed_refs, acc_ref = refs[:H], refs[H]
     mine, chunk, group = run_place()
     valid = blocks_smem[group]
-
-    def block_copy(index):
-        rows = rows_at(index)
-        return pltpu.make_async_copy(all_hbm.at[rows], all_ref.at[rows], sems.at[index])
-
-    block_copy(chunk).start()
-
-    @pl.loop(0, chunk)
-    def _(index):
-        block_copy(index).start()
-
     acc_ref[...] = jnp.zeros_like(acc_ref)
-    block_copy(chunk).wait()
-
-    @pl.when(chunk >= valid)
-    def _():
+
+    @pl.when(chunk < valid)
+    def _():
+        side = score_side(all_ref[rows_at(chunk), : 2 * KW])
+
         @pl.loop(0, chunk)
         def _(index):
-            block_copy(index).wait()
-
-    @pl.when(chunk < valid)
-    def _():
-        side = score_side(all_ref[rows_at(chunk), : 2 * KW])
-
-        @pl.loop(0, chunk)
-        def _(index):
-            block_copy(index).wait()
             scores = dot(side, all_ref[rows_at(index), : 2 * KW], 1, 1)
             acc_ref[...] += dot(
                 silu_half(scores).astype(BF16), all_ref[rows_at(index), 2 * KW :], 1, 0
@@ -708,13 +689,8 @@
         2 * 10**9,
         2 * 2**20,
         "long_attend",
-        vmem=62,
-        in_specs=[SMEM, pl.BlockSpec(memory_space=pl.ANY)],
-        scratch_shapes=[
-            pltpu.VMEM((BLOCK, VW), F32),
-            pltpu.VMEM((chunks * BLOCK, HW), BF16),
-            pltpu.SemaphoreType.DMA((chunks,)),
-        ],
+        in_specs=[SMEM, WHOLE],
+        scratch_shapes=[pltpu.VMEM((BLOCK, VW), F32)],
     )(long_blocks, whole)
     out_long, sent, mid = call(
         long_head_kernel,
@@ -776,7 +752,6 @@
         6 * 10**9,
         4 * 2**20,
         "long_back",
-        vmem=62,
         in_specs=[SMEM, WHOLE, WHOLE],
         scratch_shapes=[
             pltpu.VMEM((BLOCK, 2 * KW), F32),

time: 147 us -> 142 us (0.966)
  starting transfers between devices: 49.4 us -> 43.7 us
  Pallas kernels: 67.4 us -> 70.9 us
    ppermute x5, starting transfers between devices: 5.68 us -> 0.75 us  [swap_cores(): return lax.ppermute(half, 'dp', [(src, src ^ 1) for src in range(size)])]
    pallas_call x1, Pallas kernels: 13.4 us -> 16.9 us  [body(): call(short_back_kernel, (in_hbm((short_rows, rest)), in_hbm((half, rest))...]
    pallas_call x1, Pallas kernels: 3.07 us -> 1.17 us  [body(): call(long_attend_kernel, (shaped((long_rows, VW)),) * H, 2 * 10 ** 9, 2 *...]
    all_to_all x2, starting transfers between devices: 20.8 us -> 18.9 us  [scatter_pairs(): lax.all_to_all(sent, ('dp', 'sp'), 0, 0, tiled=True, axis_index_groups=gr...]
    ppermute x6, waiting for transfers between devices: 8.58 us -> 6.95 us  [swap_heads(): lax.ppermute(pieces[bits], 'sp', [(src, src ^ bits) for src in range(size)])]
    unnamed x32 -> x34, local copies, waits for them, and re-layouts: 3.56 us -> 2.83 us
  transfers between devices with their start and end apart: 15 -> 15, of which waited for: 8 -> 9; matrix products, arithmetic and copies ran while one was open for 1% -> 0% of each run, Pallas kernels for 39% -> 44%
where the time goes in v6:
time: 142 us
  Pallas kernels  70.9 us (50%)
  starting transfers between devices  43.7 us (31%)
  waiting for transfers between devices  23.2 us (16%)
  local copies, waits for them, and re-layouts  2.83 us (2%)
    pallas_call x1, Pallas kernels, body(): call(short_forward_kernel, (in_hbm((short_rows, width)), in_hbm((short_ro...  22.3 us
    all_to_all x2, starting transfers between devices, scatter_pairs(): lax.all_to_all(sent, ('dp', 'sp'), 0, 0, tiled=True, axis_index_groups=gr...  18.9 us
    pallas_call x1, Pallas kernels, body(): call(short_back_kernel, (in_hbm((short_rows, rest)), in_hbm((half, rest))...  16.9 us
    all_to_all x2, starting transfers between devices, spread_heads(): lax.all_to_all(sent.reshape(chunks * heads, rows, cols), 'sp', 0, 0, tile...  16.8 us
    pallas_call x1, Pallas kernels, body(): call(input_back_kernel, (in_hbm((short_rows, width)), in_hbm((long_rows,...  11.2 us
    pallas_call x1, Pallas kernels, body(): call(long_back_kernel, (shaped((long_rows, HW)),) * H, 6 * 10 ** 9, 4 * 2...  8.01 us
    ppermute x6, starting transfers between devices, swap_heads(): lax.ppermute(pieces[bits], 'sp', [(src, src ^ bits) for src in range(size)])  7.27 us
    ppermute x6, waiting for transfers between devices, swap_heads(): lax.ppermute(pieces[bits], 'sp', [(src, src ^ bits) for src in range(size)])  6.95 us
  transfers between devices with their start and end apart: 15, of which 9 were waited for; matrix products, arithmetic and copies ran while one was open for 0% of the time, Pallas kernels for 44%

profile of v6, /device:TPU:0, one launch (start us, length us, event | category | flops | bytes accessed | tf_op | source)
XLA Modules:
  0.0 141.7 jit_solution(15005791897892384552)
XLA Ops:
  0.6 4.2 %long_project.1 = (bf16[1024,1024]{1,0:T(8,128)(2,1)}, bf16[8,4,128,256]{3,2,1,0:T(8,128)(2,1)}, f32[128,1]{1,0:T(8,128)}, bf16[128,1024]{1,0:T(8,128)(2,1)}, bf16[128,1024]{1,0:T(8,128)(2,1)}) custom-call(bf16[128,1024]{1,0:T(8,128)(2,1)} %x_ref.5, bf16[1024,1536]{1,0:T(8,128)(2,1)} %pin_ref.3, bf16[1024,1536]{1,0:T(8,128)(2,1)} %pin_ref.3, ...), custom_call_target="tpu_custom_call" | custom-call | flops 268435456 | bytes 8388608 | tf_op jit(solution)/shard_map/long_project/pallas_call | solution.py:596
  4.8 9.3 %all-to-all-start = ((bf16[32,128,256]{2,1,0:T(8,128)(2,1)}), bf16[32,128,256]{2,1,0:T(8,128)(2,1)S(1)}, u32[]{:S(2)}, u32[]{:S(2)}) async-start(bf16[32,128,256]{2,1,0:T(8,128)(2,1)} %bitcast.11), calls=%async_computation | async-start | bytes 4194304 | tf_op jit(solution)/shard_map/all_to_all | solution.py:566
  14.1 22.3 %short_forward.1 = (bf16[1024,1024]{1,0:T(8,128)(2,1)}, bf16[1024,1024]{1,0:T(8,128)(2,1)}, bf16[1024,512]{1,0:T(8,128)(2,1)}, bf16[1024,512]{1,0:T(8,128)(2,1)}...) custom-call(s32[1,2]{1,0:T(1,128)} %user_ref.3, ...), custom_call_target="tpu_custom_call" | custom-call | flops 20000000000 | bytes 25165824 | tf_op jit(solution)/shard_map/short_forward/pallas_call | solution.py:625
  36.5 2.9 %collective-permute-done.got_ref = bf16[512,1024]{1,0:T(8,128)(2,1)S(1)} collective-permute-done((bf16[512,1024]{1,0:T(8,128)(2,1)}, bf16[512,1024]{1,0:T(8,128)(2,1)S(1)}, u32[]{:S(2)}, u32[]{:S(2)}) %collective-permute-start) | collective-permute-done | bytes 1048608 | tf_op jit(solution)/shard_map/ppermute | solution.py:572
  39.3 5.0 %all-to-all-done = bf16[32,128,256]{2,1,0:T(8,128)(2,1)S(1)} async-done(((bf16[32,128,256]{2,1,0:T(8,128)(2,1)}), bf16[32,128,256]{2,1,0:T(8,128)(2,1)S(1)}, u32[]{:S(2)}, u32[]{:S(2)}) %all-to-all-start) | async-done | bytes 2097184 | tf_op jit(solution)/shard_map/all_to_all | solution.py:566
  44.4 1.2 long_attend.1
  45.5 0.1 copy-done.3
  45.6 0.4 collective-permute-start.2
  46.1 3.0 %collective-permute-start.3 = (bf16[128,128]{1,0:T(8,128)(2,1)S(1)}, bf16[128,128]{1,0:T(8,128)(2,1)S(1)}, u32[]{:S(2)}, u32[]{:S(2)}) collective-permute-start(bf16[128,128]{1,0:T(8,128)(2,1)S(1)} %get-tuple-element.65), channel_id=1, source_target_pairs={{0,3},{1,2},{2,1},{3,0},{4,7},{5,6},{6,5},{7,4},{8,11},{9,10},{10,... | collective-permute-start | bytes 98312 | tf_op jit(solution)/shard_map/ppermute | solution.py:559
  49.1 0.4 collective-permute-done.1.got_1
  49.6 1.7 %collective-permute-done.3.got_3 = bf16[128,128]{1,0:T(8,128)(2,1)S(1)} collective-permute-done((bf16[128,128]{1,0:T(8,128)(2,1)S(1)}, bf16[128,128]{1,0:T(8,128)(2,1)S(1)}, u32[]{:S(2)}, u32[]{:S(2)}) %collective-permute-start.3) | collective-permute-done | bytes 32800 | tf_op jit(solution)/shard_map/ppermute | solution.py:559
  51.4 2.1 %long_head.1 = (bf16[128,1024]{1,0:T(8,128)(2,1)}, bf16[8,4,128,128]{3,2,1,0:T(8,128)(2,1)}, bf16[128,1024]{1,0:T(8,128)(2,1)}) custom-call(bf16[128,128]{1,0:T(8,128)(2,1)S(1)} %get-tuple-element.62.got_0, bf16[128,128]{1,0:T(8,128)(2,1)S(1)} %collective-permute-done.1.got_1, bf16[128,128]{1,0:T(8,128)(2,1)S(1)} %collective-permute-done.2.got_2, ...), custom_call_target="tpu_custom_call" | custom-call | flops 268435456 | bytes 3145728 | tf_op jit(solution)/shard_map/long_head/pallas_call | solution.py:695
  53.5 7.5 %all-to-all-start.1 = ((bf16[32,128,128]{2,1,0:T(8,128)(2,1)}), bf16[32,128,128]{2,1,0:T(8,128)(2,1)S(1)}, u32[]{:S(2)}, u32[]{:S(2)}) async-start(bf16[32,128,128]{2,1,0:T(8,128)(2,1)} %bitcast.12), calls=%async_computation.1 | async-start | bytes 2097152 | tf_op jit(solution)/shard_map/all_to_all | solution.py:566
  61.1 0.5 collective-permute-start.5
  61.6 16.9 %short_back.1 = (bf16[1024,1024]{1,0:T(8,128)(2,1)}, bf16[512,1024]{1,0:T(8,128)(2,1)}, bf16[512,1024]{1,0:T(8,128)(2,1)}) custom-call(s32[1,2]{1,0:T(1,128)} %user_ref.3, bf16[1024,1024]{1,0:T(8,128)(2,1)} %get-tuple-element.74.qkv_ref, bf16[1024,512]{1,0:T(8,128)(2,1)} %get-tuple-element.75.g_ref, bf16[1024,1024]{1,0:T(8,128)(2,1)} %get-tuple-element.76.slope_ref, ...), custom_call_target="tpu_custom_call" | custom-call | flops 16000000000 | bytes 13631488 | tf_op jit(solution)/shard_map/short_back/pallas_call | solution.py:712
  78.6 1.5 %early_sums.1 = bf16[512,1024]{1,0:T(8,128)(2,1)} custom-call(bf16[128,1024]{1,0:T(8,128)(2,1)S(1)} %copy-done.1, bf16[128,1024]{1,0:T(8,128)(2,1)S(1)} %copy-done, bf16[128,1024]{1,0:T(8,128)(2,1)S(1)} %copy-done.5, bf16[128,1024]{1,0:T(8,128)(2,1)S(1)} %collective-permute-done.6.half_ref, bf16[128,1024]{1,0:T(8,128)(2,1)S(1)} %collective-permute-done.5.mid_got, ...), custom_call_target="tpu_custom_call" | custom-call | flops 268435456 | bytes 5242880 | tf_op jit(solution)/shard_map/early_sums/pallas_call | solution.py:739
  80.1 10.4 %all-to-all-start.2 = ((bf16[64,8,1024]{2,1,0:T(8,128)(2,1)}), bf16[64,8,1024]{2,1,0:T(8,128)(2,1)S(1)}, u32[]{:S(2)}, u32[]{:S(2)}) async-start(bf16[64,8,1024]{2,1,0:T(8,128)(2,1)} %bitcast.9), calls=%async_computation.2 | async-start | bytes 2097152 | tf_op jit(solution)/shard_map/all_to_all | solution.py:583
  90.5 1.6 %copy-done.4 = bf16[32,128,256]{2,1,0:T(8,128)(2,1)S(1)} copy-done((bf16[32,128,256]{2,1,0:T(8,128)(2,1)S(1)}, bf16[32,128,256]{2,1,0:T(8,128)(2,1)}, u32[]{:S(2)}) %copy-start.4) | copy-done | bytes 2097176
  92.1 8.0 %long_back.1 = (bf16[128,256]{1,0:T(8,128)(2,1)S(1)}, bf16[128,256]{1,0:T(8,128)(2,1)S(1)}, bf16[128,256]{1,0:T(8,128)(2,1)S(1)}, bf16[128,256]{1,0:T(8,128)(2,1)S(1)}) custom-call(s32[4]{0:T(128)S(1)} %copy-done.13, bf16[4096,256]{1,0:T(8,128)(2,1)S(1)} %bitcast.7, bf16[4096,128]{1,0:T(8,128)(2,1)S(1)} %bitcast.8), custom_call_target="tpu_custom_call" | custom-call | flops 6000000000 | bytes 4194304 | tf_op jit(solution)/shard_map/long_back/pallas_call | solution.py:749
  100.1 1.9 %collective-permute-start.7 = (bf16[128,256]{1,0:T(8,128)(2,1)S(1)}, bf16[128,256]{1,0:T(8,128)(2,1)S(1)}, u32[]{:S(2)}, u32[]{:S(2)}) collective-permute-start(bf16[128,256]{1,0:T(8,128)(2,1)S(1)} %get-tuple-element.90), channel_id=1, source_target_pairs={{0,1},{1,0},{2,3},{3,2},{4,5},{5,4},{6,7},{7,6},{8,9},{9,8},{10,11... | collective-permute-start | bytes 196616 | tf_op jit(solution)/shard_map/ppermute | solution.py:559
  102.0 1.5 %collective-permute-start.8 = (bf16[128,256]{1,0:T(8,128)(2,1)S(1)}, bf16[128,256]{1,0:T(8,128)(2,1)S(1)}, u32[]{:S(2)}, u32[]{:S(2)}) collective-permute-start(bf16[128,256]{1,0:T(8,128)(2,1)S(1)} %get-tuple-element.91), channel_id=1, source_target_pairs={{0,2},{1,3},{2,0},{3,1},{4,6},{5,7},{6,4},{7,5},{8,10},{9,11},{10,... | collective-permute-start | bytes 196616 | tf_op jit(solution)/shard_map/ppermute | solution.py:559
  103.5 0.5 collective-permute-start.9
  103.9 2.9 %collective-permute-done.7.got_1 = bf16[128,256]{1,0:T(8,128)(2,1)S(1)} collective-permute-done((bf16[128,256]{1,0:T(8,128)(2,1)S(1)}, bf16[128,256]{1,0:T(8,128)(2,1)S(1)}, u32[]{:S(2)}, u32[]{:S(2)}) %collective-permute-start.7) | collective-permute-done | bytes 65568 | tf_op jit(solution)/shard_map/ppermute | solution.py:559
  106.8 1.8 %collective-permute-done.9.got_3 = bf16[128,256]{1,0:T(8,128)(2,1)S(1)} collective-permute-done((bf16[128,256]{1,0:T(8,128)(2,1)S(1)}, bf16[128,256]{1,0:T(8,128)(2,1)S(1)}, u32[]{:S(2)}, u32[]{:S(2)}) %collective-permute-start.9) | collective-permute-done | bytes 65568 | tf_op jit(solution)/shard_map/ppermute | solution.py:559
  108.8 1.5 %collective-permute-done.10.grad_got = bf16[128,1024]{1,0:T(8,128)(2,1)S(1)} collective-permute-done((bf16[128,1024]{1,0:T(8,128)(2,1)S(1)}, bf16[128,1024]{1,0:T(8,128)(2,1)S(1)}, u32[]{:S(2)}, u32[]{:S(2)}) %collective-permute-start.10) | collective-permute-done | bytes 262176 | tf_op jit(solution)/shard_map/ppermute | solution.py:572
  110.4 2.5 %late_sums.1 = bf16[512,1024]{1,0:T(8,128)(2,1)} custom-call(bf16[512,1024]{1,0:T(8,128)(2,1)S(1)} %copy-done.9, bf16[512,1024]{1,0:T(8,128)(2,1)} %collective-permute-done.4.got_ref, bf16[128,1024]{1,0:T(8,128)(2,1)S(1)} %copy-done.1, bf16[128,1024]{1,0:T(8,128)(2,1)S(1)} %collective-permute-done.6.half_ref, ...), custom_call_target="tpu_custom_call" | custom-call | flops 268435456 | bytes 5242880 | tf_op jit(solution)/shard_map/late_sums/pallas_call | solution.py:769
  112.9 1.1 copy-done.14
  114.0 8.5 %all-to-all-start.3 = ((bf16[64,8,1024]{2,1,0:T(8,128)(2,1)}), bf16[64,8,1024]{2,1,0:T(8,128)(2,1)S(1)}, u32[]{:S(2)}, u32[]{:S(2)}) async-start(bf16[64,8,1024]{2,1,0:T(8,128)(2,1)} %bitcast.10), calls=%async_computation.3 | async-start | bytes 2097152 | tf_op jit(solution)/shard_map/all_to_all | solution.py:583
  122.5 11.2 %input_back.1 = (bf16[1024,1024]{1,0:T(8,128)(2,1)}, bf16[128,1024]{1,0:T(8,128)(2,1)}) custom-call(bf16[1024,512]{1,0:T(8,128)(2,1)} %get-tuple-element.95.grad_gate_ref, bf16[1024,1024]{1,0:T(8,128)(2,1)} %get-tuple-element.96.grad_ref, bf16[1024,1024]{1,0:T(8,128)(2,1)} %cot_ref.7, bf16[1024,1024]{1,0:T(8,128)(2,1)} %get-tuple-element.97.xbf_ref, ...), custom_call_target="tpu_custom_call" | custom-call | flops 3623878656 | bytes 14680064 | tf_op jit(solution)/shard_map/input_back/pallas_call | solution.py:792
  133.7 0.2 convert_reduce_fusion.early_ref
  133.9 6.9 %all-to-all-done.3.late_ref = bf16[64,8,1024]{2,1,0:T(8,128)(2,1)S(1)} async-done(((bf16[64,8,1024]{2,1,0:T(8,128)(2,1)}), bf16[64,8,1024]{2,1,0:T(8,128)(2,1)S(1)}, u32[]{:S(2)}, u32[]{:S(2)}) %all-to-all-start.3) | async-done | bytes 1048608 | tf_op jit(solution)/shard_map/all_to_all | solution.py:583
  140.8 0.9 final_sums.1
  (44 shorter events, 0.5 us)
Async XLA Ops:
  4.8 39.5 %all-to-all-start = ((bf16[32,128,256]{2,1,0:T(8,128)(2,1)}), bf16[32,128,256]{2,1,0:T(8,128)(2,1)S(1)}, u32[]{:S(2)}, u32[]{:S(2)}) async-start(bf16[32,128,256]{2,1,0:T(8,128)(2,1)} %bitcast.11), calls=%async_computation | async-start | bytes 4194304 | tf_op jit(solution)/shard_map/all_to_all | solution.py:566
  14.1 30.2 %copy-start.13 = (s32[4]{0:T(128)S(1)}, s32[4]{0:T(128)}, u32[]{:S(2)}) copy-start(s32[4]{0:T(128)} %blocks_smem.3) | copy-start | bytes 52
  36.4 3.0 %collective-permute-start = (bf16[512,1024]{1,0:T(8,128)(2,1)}, bf16[512,1024]{1,0:T(8,128)(2,1)S(1)}, u32[]{:S(2)}, u32[]{:S(2)}) collective-permute-start(bf16[512,1024]{1,0:T(8,128)(2,1)} %get-tuple-element.59), channel_id=1, source_target_pairs={{0,32},{32,0},{64,96},{96,64},{1,33},{33,1},{65,97},{97,65},{2,34}... | collective-permute-start | bytes 3145736 | tf_op jit(solution)/shard_map/ppermute | solution.py:572
  44.3 1.3 copy-start.3
  44.3 7.0 %copy-start = (bf16[128,1024]{1,0:T(8,128)(2,1)S(1)}, bf16[128,1024]{1,0:T(8,128)(2,1)}, u32[]{:S(2)}) copy-start(bf16[128,1024]{1,0:T(8,128)(2,1)} %long_cot_ref.3) | copy-start | bytes 786436
  44.3 7.0 %copy-start.7 = (bf16[128,1024]{1,0:T(8,128)(2,1)S(1)}, bf16[128,1024]{1,0:T(8,128)(2,1)}, u32[]{:S(2)}) copy-start(bf16[128,1024]{1,0:T(8,128)(2,1)} %x_ref.5) | copy-start | bytes 786436
  44.3 7.0 %copy-start.8 = (bf16[512,1024]{1,0:T(8,128)(2,1)S(1)}, bf16[512,1024]{1,0:T(8,128)(2,1)}, u32[]{:S(2)}) copy-start(bf16[512,1024]{1,0:T(8,128)(2,1)} %pout_ref.3) | copy-start | bytes 3145732
  44.3 7.0 %copy-start.11 = (bf16[128,512]{1,0:T(8,128)(2,1)S(1)}, bf16[128,512]{1,0:T(8,128)(2,1)}, u32[]{:S(2)}) copy-start(bf16[128,512]{1,0:T(8,128)(2,1)} %get-tuple-element.66.gate_ref) | copy-start | bytes 393220
  44.4 7.0 %copy-start.12 = (bf16[128,512]{1,0:T(8,128)(2,1)S(1)}, bf16[128,512]{1,0:T(8,128)(2,1)}, u32[]{:S(2)}) copy-start(bf16[128,512]{1,0:T(8,128)(2,1)} %get-tuple-element.67.slope_ref) | copy-start | bytes 393220
  45.6 15.3 %copy-start.16 = (bf16[128,1024]{1,0:T(8,128)(2,1)S(1)}, bf16[128,1024]{1,0:T(8,128)(2,1)}, u32[]{:S(2)}) copy-start(bf16[128,1024]{1,0:T(8,128)(2,1)} %get-tuple-element.81) | copy-start | bytes 786436
  45.6 3.9 %collective-permute-start.1 = (bf16[128,128]{1,0:T(8,128)(2,1)S(1)}, bf16[128,128]{1,0:T(8,128)(2,1)S(1)}, u32[]{:S(2)}, u32[]{:S(2)}) collective-permute-start(bf16[128,128]{1,0:T(8,128)(2,1)S(1)} %get-tuple-element.63), channel_id=1, source_target_pairs={{0,1},{1,0},{2,3},{3,2},{4,5},{5,4},{6,7},{7,6},{8,9},{9,8},{10,11... | collective-permute-start | bytes 98312 | tf_op jit(solution)/shard_map/ppermute | solution.py:559
  45.6 4.0 %collective-permute-start.2 = (bf16[128,128]{1,0:T(8,128)(2,1)S(1)}, bf16[128,128]{1,0:T(8,128)(2,1)S(1)}, u32[]{:S(2)}, u32[]{:S(2)}) collective-permute-start(bf16[128,128]{1,0:T(8,128)(2,1)S(1)} %get-tuple-element.64), channel_id=1, source_target_pairs={{0,2},{1,3},{2,0},{3,1},{4,6},{5,7},{6,4},{7,5},{8,10},{9,11},{10,... | collective-permute-start | bytes 98312 | tf_op jit(solution)/shard_map/ppermute | solution.py:559
  46.1 5.3 %collective-permute-start.3 = (bf16[128,128]{1,0:T(8,128)(2,1)S(1)}, bf16[128,128]{1,0:T(8,128)(2,1)S(1)}, u32[]{:S(2)}, u32[]{:S(2)}) collective-permute-start(bf16[128,128]{1,0:T(8,128)(2,1)S(1)} %get-tuple-element.65), channel_id=1, source_target_pairs={{0,3},{1,2},{2,1},{3,0},{4,7},{5,6},{6,5},{7,4},{8,11},{9,10},{10,... | collective-permute-start | bytes 98312 | tf_op jit(solution)/shard_map/ppermute | solution.py:559
  53.5 7.6 %copy-start.5 = (bf16[128,1024]{1,0:T(8,128)(2,1)S(1)}, bf16[128,1024]{1,0:T(8,128)(2,1)}, u32[]{:S(2)}) copy-start(bf16[128,1024]{1,0:T(8,128)(2,1)} %get-tuple-element.80.mid_ref.long_gate_ref) | copy-start | bytes 786436
  53.5 26.6 %all-to-all-start.1 = ((bf16[32,128,128]{2,1,0:T(8,128)(2,1)}), bf16[32,128,128]{2,1,0:T(8,128)(2,1)S(1)}, u32[]{:S(2)}, u32[]{:S(2)}) async-start(bf16[32,128,128]{2,1,0:T(8,128)(2,1)} %bitcast.12), calls=%async_computation.1 | async-start | bytes 2097152 | tf_op jit(solution)/shard_map/all_to_all | solution.py:566
  61.0 17.5 %collective-permute-start.6 = (bf16[128,1024]{1,0:T(8,128)(2,1)S(1)}, bf16[128,1024]{1,0:T(8,128)(2,1)S(1)}, u32[]{:S(2)}, u32[]{:S(2)}) collective-permute-start(bf16[128,1024]{1,0:T(8,128)(2,1)S(1)} %copy-done.16), channel_id=1, source_target_pairs={{0,32},{32,0},{64,96},{96,64},{1,33},{33,1},{65,97},{97,65},{2,34}... | collective-permute-start | bytes 786440 | tf_op jit(solution)/shard_map/ppermute | solution.py:572
  61.1 17.4 %collective-permute-start.5 = (bf16[128,1024]{1,0:T(8,128)(2,1)S(1)}, bf16[128,1024]{1,0:T(8,128)(2,1)S(1)}, u32[]{:S(2)}, u32[]{:S(2)}) collective-permute-start(bf16[128,1024]{1,0:T(8,128)(2,1)S(1)} %copy-done.5), channel_id=1, source_target_pairs={{0,32},{32,0},{64,96},{96,64},{1,33},{33,1},{65,97},{97,65},{2,34}... | collective-permute-start | bytes 786440 | tf_op jit(solution)/shard_map/ppermute | solution.py:572
  61.6 17.0 %copy-start.1 = (bf16[128,1024]{1,0:T(8,128)(2,1)S(1)}, bf16[128,1024]{1,0:T(8,128)(2,1)}, u32[]{:S(2)}) copy-start(bf16[128,1024]{1,0:T(8,128)(2,1)} %get-tuple-element.58.long_xbf_ref.xbf_ref) | copy-start | bytes 786436
  61.6 17.0 %copy-start.6 = (bf16[512,1024]{1,0:T(8,128)(2,1)S(1)}, bf16[512,1024]{1,0:T(8,128)(2,1)}, u32[]{:S(2)}) copy-start(bf16[512,1024]{1,0:T(8,128)(2,1)} %get-tuple-element.86.mine_ref) | copy-start | bytes 3145732
  78.5 30.3 %collective-permute-start.4 = (bf16[512,1024]{1,0:T(8,128)(2,1)}, bf16[512,1024]{1,0:T(8,128)(2,1)}, u32[]{:S(2)}, u32[]{:S(2)}) collective-permute-start(bf16[512,1024]{1,0:T(8,128)(2,1)} %get-tuple-element.79), channel_id=1, source_target_pairs={{0,32},{32,0},{64,96},{96,64},{1,33},{33,1},{65,97},{97,65},{2,34}... | collective-permute-start | bytes 3145736 | tf_op jit(solution)/shard_map/ppermute | solution.py:572
  80.1 32.8 %all-to-all-start.2 = ((bf16[64,8,1024]{2,1,0:T(8,128)(2,1)}), bf16[64,8,1024]{2,1,0:T(8,128)(2,1)S(1)}, u32[]{:S(2)}, u32[]{:S(2)}) async-start(bf16[64,8,1024]{2,1,0:T(8,128)(2,1)} %bitcast.9), calls=%async_computation.2 | async-start | bytes 2097152 | tf_op jit(solution)/shard_map/all_to_all | solution.py:583
  90.5 1.6 %copy-start.4 = (bf16[32,128,256]{2,1,0:T(8,128)(2,1)S(1)}, bf16[32,128,256]{2,1,0:T(8,128)(2,1)}, u32[]{:S(2)}) copy-start(bf16[32,128,256]{2,1,0:T(8,128)(2,1)} %copy-done.3) | copy-start | bytes 6291460
  92.1 16.5 %copy-start.10 = (bf16[128,1024]{1,0:T(8,128)(2,1)S(1)}, bf16[128,1024]{1,0:T(8,128)(2,1)}, u32[]{:S(2)}) copy-start(bf16[128,1024]{1,0:T(8,128)(2,1)} %get-tuple-element.93.slope_ref) | copy-start | bytes 786436
  92.1 18.2 %copy-start.9 = (bf16[512,1024]{1,0:T(8,128)(2,1)S(1)}, bf16[512,1024]{1,0:T(8,128)(2,1)}, u32[]{:S(2)}) copy-start(bf16[512,1024]{1,0:T(8,128)(2,1)} %get-tuple-element.78.mine_ref) | copy-start | bytes 3145732
  100.1 6.7 %collective-permute-start.7 = (bf16[128,256]{1,0:T(8,128)(2,1)S(1)}, bf16[128,256]{1,0:T(8,128)(2,1)S(1)}, u32[]{:S(2)}, u32[]{:S(2)}) collective-permute-start(bf16[128,256]{1,0:T(8,128)(2,1)S(1)} %get-tuple-element.90), channel_id=1, source_target_pairs={{0,1},{1,0},{2,3},{3,2},{4,5},{5,4},{6,7},{7,6},{8,9},{9,8},{10,11... | collective-permute-start | bytes 196616 | tf_op jit(solution)/shard_map/ppermute | solution.py:559
  102.0 4.8 %collective-permute-start.8 = (bf16[128,256]{1,0:T(8,128)(2,1)S(1)}, bf16[128,256]{1,0:T(8,128)(2,1)S(1)}, u32[]{:S(2)}, u32[]{:S(2)}) collective-permute-start(bf16[128,256]{1,0:T(8,128)(2,1)S(1)} %get-tuple-element.91), channel_id=1, source_target_pairs={{0,2},{1,3},{2,0},{3,1},{4,6},{5,7},{6,4},{7,5},{8,10},{9,11},{10,... | collective-permute-start | bytes 196616 | tf_op jit(solution)/shard_map/ppermute | solution.py:559
  103.5 5.2 %collective-permute-start.9 = (bf16[128,256]{1,0:T(8,128)(2,1)S(1)}, bf16[128,256]{1,0:T(8,128)(2,1)S(1)}, u32[]{:S(2)}, u32[]{:S(2)}) collective-permute-start(bf16[128,256]{1,0:T(8,128)(2,1)S(1)} %get-tuple-element.92), channel_id=1, source_target_pairs={{0,3},{1,2},{2,1},{3,0},{4,7},{5,6},{6,5},{7,4},{8,11},{9,10},{10,... | collective-permute-start | bytes 196616 | tf_op jit(solution)/shard_map/ppermute | solution.py:559
  108.7 4.2 %copy-start.2 = (bf16[128,1024]{1,0:T(8,128)(2,1)}, bf16[128,1024]{1,0:T(8,128)(2,1)S(1)}, u32[]{:S(2)}) copy-start(bf16[128,1024]{1,0:T(8,128)(2,1)S(1)} %long_slopes.1.grad_ref.long_grad_ref) | copy-start | bytes 786436
  108.7 1.6 %collective-permute-start.10 = (bf16[128,1024]{1,0:T(8,128)(2,1)S(1)}, bf16[128,1024]{1,0:T(8,128)(2,1)S(1)}, u32[]{:S(2)}, u32[]{:S(2)}) collective-permute-start(bf16[128,1024]{1,0:T(8,128)(2,1)S(1)} %long_slopes.1.grad_ref.long_grad_ref), channel_id=1, source_target_pairs={{0,32},{32,0},{64,96},{96,64},{1,33},{33,1},{65,97},{97,65},{2,34}... | collective-permute-start | bytes 786440 | tf_op jit(solution)/shard_map/ppermute | solution.py:572
  112.9 1.1 copy-start.14
  114.0 26.8 %all-to-all-start.3 = ((bf16[64,8,1024]{2,1,0:T(8,128)(2,1)}), bf16[64,8,1024]{2,1,0:T(8,128)(2,1)S(1)}, u32[]{:S(2)}, u32[]{:S(2)}) async-start(bf16[64,8,1024]{2,1,0:T(8,128)(2,1)} %bitcast.10), calls=%async_computation.3 | async-start | bytes 2097152 | tf_op jit(solution)/shard_map/all_to_all | solution.py:583
  122.5 11.2 %copy-start.15 = (bf16[64,8,1024]{2,1,0:T(8,128)(2,1)S(1)}, bf16[64,8,1024]{2,1,0:T(8,128)(2,1)}, u32[]{:S(2)}) copy-start(bf16[64,8,1024]{2,1,0:T(8,128)(2,1)} %copy-done.14) | copy-start | bytes 3145732

commit v7 on v6

--- a/solution.py
+++ b/solution.py
@@ -752,6 +752,7 @@
         6 * 10**9,
         4 * 2**20,
         "long_back",
+        vmem=62,
         in_specs=[SMEM, WHOLE, WHOLE],
         scratch_shapes=[
             pltpu.VMEM((BLOCK, 2 * KW), F32),
@@ -795,7 +796,7 @@
         2 * (short_rows + long_rows) * width * cols,
         14 * 2**20,
         "input_back",
-        vmem=60,
+        vmem=59,
         grid=(short_rows // BLOCK + 1,),
         in_specs=[
             short_rows_spec(gates),

time: 142 us -> 146 us (1.028)
  local copies, waits for them, and re-layouts: 2.83 us -> 5.48 us
  Pallas kernels: 70.9 us -> 73 us
    unnamed x34 -> x38, local copies, waits for them, and re-layouts: 2.83 us -> 5.48 us
    pallas_call x1, Pallas kernels: 8.01 us -> 10.1 us  [body(): call(long_back_kernel, (shaped((long_rows, HW)),) * H, 6 * 10 ** 9, 4 * 2...]
  transfers between devices with their start and end apart: 15 -> 15, of which waited for: 9 -> 9; matrix products, arithmetic and copies ran while one was open for 0% -> 1% of each run, Pallas kernels for 44% -> 44%
where the time goes in v7:
time: 146 us; the launch traced here: 147 us
  Pallas kernels  73 us (50%)
  starting transfers between devices  43.7 us (30%)
  waiting for transfers between devices  22.2 us (15%)
  local copies, waits for them, and re-layouts  5.48 us (4%)
    pallas_call x1, Pallas kernels, body(): call(short_forward_kernel, (in_hbm((short_rows, width)), in_hbm((short_ro...  22.3 us
    all_to_all x2, starting transfers between devices, scatter_pairs(): lax.all_to_all(sent, ('dp', 'sp'), 0, 0, tiled=True, axis_index_groups=gr...  19.2 us
    pallas_call x1, Pallas kernels, body(): call(short_back_kernel, (in_hbm((short_rows, rest)), in_hbm((half, rest))...  17 us
    all_to_all x2, starting transfers between devices, spread_heads(): lax.all_to_all(sent.reshape(chunks * heads, rows, cols), 'sp', 0, 0, tile...  16.8 us
    pallas_call x1, Pallas kernels, body(): call(input_back_kernel, (in_hbm((short_rows, width)), in_hbm((long_rows,...  11.1 us
    pallas_call x1, Pallas kernels, body(): call(long_back_kernel, (shaped((long_rows, HW)),) * H, 6 * 10 ** 9, 4 * 2...  10.1 us
    ppermute x6, waiting for transfers between devices, swap_heads(): lax.ppermute(pieces[bits], 'sp', [(src, src ^ bits) for src in range(size)])  7.08 us
    ppermute x6, starting transfers between devices, swap_heads(): lax.ppermute(pieces[bits], 'sp', [(src, src ^ bits) for src in range(size)])  7.05 us
  transfers between devices with their start and end apart: 15, of which 9 were waited for; matrix products, arithmetic and copies ran while one was open for 1% of the time, Pallas kernels for 44%

profile of v7, /device:TPU:0, one launch (start us, length us, event | category | flops | bytes accessed | tf_op | source)
XLA Modules:
  0.0 146.7 jit_solution(14609089804038882761)
XLA Ops:
  0.6 4.2 %long_project.1 = (bf16[1024,1024]{1,0:T(8,128)(2,1)}, bf16[8,4,128,256]{3,2,1,0:T(8,128)(2,1)}, f32[128,1]{1,0:T(8,128)}, bf16[128,1024]{1,0:T(8,128)(2,1)}, bf16[128,1024]{1,0:T(8,128)(2,1)}) custom-call(bf16[128,1024]{1,0:T(8,128)(2,1)} %x_ref.5, bf16[1024,1536]{1,0:T(8,128)(2,1)} %pin_ref.3, bf16[1024,1536]{1,0:T(8,128)(2,1)} %pin_ref.3, ...), custom_call_target="tpu_custom_call" | custom-call | flops 268435456 | bytes 8388608 | tf_op jit(solution)/shard_map/long_project/pallas_call | solution.py:596
  4.8 9.3 %all-to-all-start = ((bf16[32,128,256]{2,1,0:T(8,128)(2,1)}), bf16[32,128,256]{2,1,0:T(8,128)(2,1)S(1)}, u32[]{:S(2)}, u32[]{:S(2)}) async-start(bf16[32,128,256]{2,1,0:T(8,128)(2,1)} %bitcast.10), calls=%async_computation | async-start | bytes 4194304 | tf_op jit(solution)/shard_map/all_to_all | solution.py:566
  14.1 22.3 %short_forward.1 = (bf16[1024,1024]{1,0:T(8,128)(2,1)}, bf16[1024,1024]{1,0:T(8,128)(2,1)}, bf16[1024,512]{1,0:T(8,128)(2,1)}, bf16[1024,512]{1,0:T(8,128)(2,1)}...) custom-call(s32[1,2]{1,0:T(1,128)} %user_ref.3, ...), custom_call_target="tpu_custom_call" | custom-call | flops 20000000000 | bytes 25165824 | tf_op jit(solution)/shard_map/short_forward/pallas_call | solution.py:625
  36.5 2.9 %collective-permute-done.got_ref = bf16[512,1024]{1,0:T(8,128)(2,1)S(1)} collective-permute-done((bf16[512,1024]{1,0:T(8,128)(2,1)}, bf16[512,1024]{1,0:T(8,128)(2,1)S(1)}, u32[]{:S(2)}, u32[]{:S(2)}) %collective-permute-start) | collective-permute-done | bytes 1048608 | tf_op jit(solution)/shard_map/ppermute | solution.py:572
  39.3 5.0 %all-to-all-done = bf16[32,128,256]{2,1,0:T(8,128)(2,1)S(1)} async-done(((bf16[32,128,256]{2,1,0:T(8,128)(2,1)}), bf16[32,128,256]{2,1,0:T(8,128)(2,1)S(1)}, u32[]{:S(2)}, u32[]{:S(2)}) %all-to-all-start) | async-done | bytes 2097184 | tf_op jit(solution)/shard_map/all_to_all | solution.py:566
  44.3 1.3 copy-done.3
  45.6 1.6 %copy-done.4 = bf16[32,128,256]{2,1,0:T(8,128)(2,1)S(1)} copy-done((bf16[32,128,256]{2,1,0:T(8,128)(2,1)S(1)}, bf16[32,128,256]{2,1,0:T(8,128)(2,1)}, u32[]{:S(2)}) %copy-start.4) | copy-done | bytes 2097176
  47.2 1.2 long_attend.1
  49.0 3.0 %collective-permute-start.3 = (bf16[128,128]{1,0:T(8,128)(2,1)S(1)}, bf16[128,128]{1,0:T(8,128)(2,1)S(1)}, u32[]{:S(2)}, u32[]{:S(2)}) collective-permute-start(bf16[128,128]{1,0:T(8,128)(2,1)S(1)} %get-tuple-element.65), channel_id=1, source_target_pairs={{0,3},{1,2},{2,1},{3,0},{4,7},{5,6},{6,5},{7,4},{8,11},{9,10},{10,... | collective-permute-start | bytes 98312 | tf_op jit(solution)/shard_map/ppermute | solution.py:559
  52.5 1.7 %collective-permute-done.3.got_3 = bf16[128,128]{1,0:T(8,128)(2,1)S(1)} collective-permute-done((bf16[128,128]{1,0:T(8,128)(2,1)S(1)}, bf16[128,128]{1,0:T(8,128)(2,1)S(1)}, u32[]{:S(2)}, u32[]{:S(2)}) %collective-permute-start.3) | collective-permute-done | bytes 32800 | tf_op jit(solution)/shard_map/ppermute | solution.py:559
  54.3 2.1 %long_head.1 = (bf16[128,1024]{1,0:T(8,128)(2,1)}, bf16[8,4,128,128]{3,2,1,0:T(8,128)(2,1)}, bf16[128,1024]{1,0:T(8,128)(2,1)}) custom-call(bf16[128,128]{1,0:T(8,128)(2,1)S(1)} %get-tuple-element.62.got_0, bf16[128,128]{1,0:T(8,128)(2,1)S(1)} %collective-permute-done.1.got_1, bf16[128,128]{1,0:T(8,128)(2,1)S(1)} %collective-permute-done.2.got_2, ...), custom_call_target="tpu_custom_call" | custom-call | flops 268435456 | bytes 3145728 | tf_op jit(solution)/shard_map/long_head/pallas_call | solution.py:695
  56.4 7.5 %all-to-all-start.1 = ((bf16[32,128,128]{2,1,0:T(8,128)(2,1)}), bf16[32,128,128]{2,1,0:T(8,128)(2,1)S(1)}, u32[]{:S(2)}, u32[]{:S(2)}) async-start(bf16[32,128,128]{2,1,0:T(8,128)(2,1)} %bitcast.12), calls=%async_computation.1 | async-start | bytes 2097152 | tf_op jit(solution)/shard_map/all_to_all | solution.py:566
  64.0 0.5 collective-permute-start.5
  64.5 17.0 %short_back.1 = (bf16[1024,1024]{1,0:T(8,128)(2,1)}, bf16[512,1024]{1,0:T(8,128)(2,1)}, bf16[512,1024]{1,0:T(8,128)(2,1)}) custom-call(s32[1,2]{1,0:T(1,128)} %user_ref.3, bf16[1024,1024]{1,0:T(8,128)(2,1)} %get-tuple-element.74.qkv_ref, bf16[1024,512]{1,0:T(8,128)(2,1)} %get-tuple-element.75.g_ref, bf16[1024,1024]{1,0:T(8,128)(2,1)} %get-tuple-element.76.slope_ref, ...), custom_call_target="tpu_custom_call" | custom-call | flops 16000000000 | bytes 13631488 | tf_op jit(solution)/shard_map/short_back/pallas_call | solution.py:712
  81.6 1.5 early_sums.1
  83.0 0.7 copy-done.8
  83.7 1.0 copy-done.17
  84.7 10.7 %all-to-all-start.2 = ((bf16[64,8,1024]{2,1,0:T(8,128)(2,1)}), bf16[64,8,1024]{2,1,0:T(8,128)(2,1)}, u32[]{:S(2)}, u32[]{:S(2)}) async-start(bf16[64,8,1024]{2,1,0:T(8,128)(2,1)} %bitcast.8), calls=%async_computation.2 | async-start | bytes 2097152 | tf_op jit(solution)/shard_map/all_to_all | solution.py:583
  95.4 10.1 %long_back.1 = (bf16[128,256]{1,0:T(8,128)(2,1)}, bf16[128,256]{1,0:T(8,128)(2,1)}, bf16[128,256]{1,0:T(8,128)(2,1)}, bf16[128,256]{1,0:T(8,128)(2,1)}) custom-call(s32[4]{0:T(128)} %blocks_smem.3, bf16[4096,256]{1,0:T(8,128)(2,1)} %bitcast.6, bf16[4096,128]{1,0:T(8,128)(2,1)} %bitcast.11), custom_call_target="tpu_custom_call" | custom-call | flops 6000000000 | bytes 4194304 | tf_op jit(solution)/shard_map/long_back/pallas_call | solution.py:749
  105.5 1.5 %collective-permute-start.7 = (bf16[128,256]{1,0:T(8,128)(2,1)}, bf16[128,256]{1,0:T(8,128)(2,1)S(1)}, u32[]{:S(2)}, u32[]{:S(2)}) collective-permute-start(bf16[128,256]{1,0:T(8,128)(2,1)} %get-tuple-element.90), channel_id=1, source_target_pairs={{0,1},{1,0},{2,3},{3,2},{4,5},{5,4},{6,7},{7,6},{8,9},{9,8},{10,11... | collective-permute-start | bytes 196616 | tf_op jit(solution)/shard_map/ppermute | solution.py:559
  107.0 1.5 collective-permute-start.8
  108.5 0.5 collective-permute-start.9
  109.0 2.8 %collective-permute-done.7.got_1 = bf16[128,256]{1,0:T(8,128)(2,1)S(1)} collective-permute-done((bf16[128,256]{1,0:T(8,128)(2,1)}, bf16[128,256]{1,0:T(8,128)(2,1)S(1)}, u32[]{:S(2)}, u32[]{:S(2)}) %collective-permute-start.7) | collective-permute-done | bytes 65568 | tf_op jit(solution)/shard_map/ppermute | solution.py:559
  111.8 2.0 %collective-permute-done.9.got_3 = bf16[128,256]{1,0:T(8,128)(2,1)S(1)} collective-permute-done((bf16[128,256]{1,0:T(8,128)(2,1)}, bf16[128,256]{1,0:T(8,128)(2,1)S(1)}, u32[]{:S(2)}, u32[]{:S(2)}) %collective-permute-start.9) | collective-permute-done | bytes 65568 | tf_op jit(solution)/shard_map/ppermute | solution.py:559
  113.9 0.8 copy-done.15
  114.9 1.5 %collective-permute-done.10.grad_got = bf16[128,1024]{1,0:T(8,128)(2,1)S(1)} collective-permute-done((bf16[128,1024]{1,0:T(8,128)(2,1)S(1)}, bf16[128,1024]{1,0:T(8,128)(2,1)S(1)}, u32[]{:S(2)}, u32[]{:S(2)}) %collective-permute-start.10) | collective-permute-done | bytes 262176 | tf_op jit(solution)/shard_map/ppermute | solution.py:572
  116.4 2.6 %late_sums.1 = bf16[512,1024]{1,0:T(8,128)(2,1)} custom-call(bf16[512,1024]{1,0:T(8,128)(2,1)S(1)} %copy-done.11, bf16[512,1024]{1,0:T(8,128)(2,1)} %collective-permute-done.4.got_ref, bf16[128,1024]{1,0:T(8,128)(2,1)S(1)} %copy-done.1, bf16[128,1024]{1,0:T(8,128)(2,1)S(1)} %copy-done.9, bf16[128,1024]{1,0:T(8,128)(2,1)S(1)} %long_slopes.1.grad_ref.long_grad_ref, ...), custom_call_target="tpu_custom_call" | custom-call | flops 268435456 | bytes 5242880 | tf_op jit(solution)/shard_map/late_sums/pallas_call | solution.py:770
  119.0 8.5 %all-to-all-start.3 = ((bf16[64,8,1024]{2,1,0:T(8,128)(2,1)}), bf16[64,8,1024]{2,1,0:T(8,128)(2,1)S(1)}, u32[]{:S(2)}, u32[]{:S(2)}) async-start(bf16[64,8,1024]{2,1,0:T(8,128)(2,1)} %bitcast.9), calls=%async_computation.3 | async-start | bytes 2097152 | tf_op jit(solution)/shard_map/all_to_all | solution.py:583
  127.5 11.1 %input_back.1 = (bf16[1024,1024]{1,0:T(8,128)(2,1)}, bf16[128,1024]{1,0:T(8,128)(2,1)}) custom-call(bf16[1024,512]{1,0:T(8,128)(2,1)} %get-tuple-element.95.grad_gate_ref, bf16[1024,1024]{1,0:T(8,128)(2,1)} %get-tuple-element.96.grad_ref, bf16[1024,1024]{1,0:T(8,128)(2,1)} %cot_ref.7, bf16[1024,1024]{1,0:T(8,128)(2,1)} %get-tuple-element.97.xbf_ref, ...), custom_call_target="tpu_custom_call" | custom-call | flops 3623878656 | bytes 14680064 | tf_op jit(solution)/shard_map/input_back/pallas_call | solution.py:793
  138.6 1.4 convert_reduce_fusion.early_ref
  140.0 5.8 %all-to-all-done.3.late_ref = bf16[64,8,1024]{2,1,0:T(8,128)(2,1)S(1)} async-done(((bf16[64,8,1024]{2,1,0:T(8,128)(2,1)}), bf16[64,8,1024]{2,1,0:T(8,128)(2,1)S(1)}, u32[]{:S(2)}, u32[]{:S(2)}) %all-to-all-start.3) | async-done | bytes 1048608 | tf_op jit(solution)/shard_map/all_to_all | solution.py:583
  145.8 0.9 final_sums.1
  (48 shorter events, 1.5 us)
Async XLA Ops:
  4.8 39.5 %all-to-all-start = ((bf16[32,128,256]{2,1,0:T(8,128)(2,1)}), bf16[32,128,256]{2,1,0:T(8,128)(2,1)S(1)}, u32[]{:S(2)}, u32[]{:S(2)}) async-start(bf16[32,128,256]{2,1,0:T(8,128)(2,1)} %bitcast.10), calls=%async_computation | async-start | bytes 4194304 | tf_op jit(solution)/shard_map/all_to_all | solution.py:566
  14.1 31.5 %copy-start.16 = (s32[4]{0:T(128)S(1)}, s32[4]{0:T(128)}, u32[]{:S(2)}) copy-start(s32[4]{0:T(128)} %blocks_smem.3) | copy-start | bytes 52
  36.4 3.0 %collective-permute-start = (bf16[512,1024]{1,0:T(8,128)(2,1)}, bf16[512,1024]{1,0:T(8,128)(2,1)S(1)}, u32[]{:S(2)}, u32[]{:S(2)}) collective-permute-start(bf16[512,1024]{1,0:T(8,128)(2,1)} %get-tuple-element.59), channel_id=1, source_target_pairs={{0,32},{32,0},{64,96},{96,64},{1,33},{33,1},{65,97},{97,65},{2,34}... | collective-permute-start | bytes 3145736 | tf_op jit(solution)/shard_map/ppermute | solution.py:572
  44.3 1.3 copy-start.3
  45.6 1.6 %copy-start.4 = (bf16[32,128,256]{2,1,0:T(8,128)(2,1)S(1)}, bf16[32,128,256]{2,1,0:T(8,128)(2,1)}, u32[]{:S(2)}) copy-start(bf16[32,128,256]{2,1,0:T(8,128)(2,1)} %copy-done.3) | copy-start | bytes 6291460
  47.2 7.0 %copy-start = (bf16[128,1024]{1,0:T(8,128)(2,1)S(1)}, bf16[128,1024]{1,0:T(8,128)(2,1)}, u32[]{:S(2)}) copy-start(bf16[128,1024]{1,0:T(8,128)(2,1)} %long_cot_ref.3) | copy-start | bytes 786436
  47.2 7.0 %copy-start.7 = (bf16[128,1024]{1,0:T(8,128)(2,1)S(1)}, bf16[128,1024]{1,0:T(8,128)(2,1)}, u32[]{:S(2)}) copy-start(bf16[128,1024]{1,0:T(8,128)(2,1)} %x_ref.5) | copy-start | bytes 786436
  47.2 7.0 %copy-start.10 = (bf16[512,1024]{1,0:T(8,128)(2,1)S(1)}, bf16[512,1024]{1,0:T(8,128)(2,1)}, u32[]{:S(2)}) copy-start(bf16[512,1024]{1,0:T(8,128)(2,1)} %pout_ref.3) | copy-start | bytes 3145732
  47.2 7.0 %copy-start.13 = (bf16[128,512]{1,0:T(8,128)(2,1)S(1)}, bf16[128,512]{1,0:T(8,128)(2,1)}, u32[]{:S(2)}) copy-start(bf16[128,512]{1,0:T(8,128)(2,1)} %get-tuple-element.66.gate_ref) | copy-start | bytes 393220
  47.2 7.0 %copy-start.14 = (bf16[128,512]{1,0:T(8,128)(2,1)S(1)}, bf16[128,512]{1,0:T(8,128)(2,1)}, u32[]{:S(2)}) copy-start(bf16[128,512]{1,0:T(8,128)(2,1)} %get-tuple-element.67.slope_ref) | copy-start | bytes 393220
  48.4 15.4 %copy-start.18 = (bf16[128,1024]{1,0:T(8,128)(2,1)S(1)}, bf16[128,1024]{1,0:T(8,128)(2,1)}, u32[]{:S(2)}) copy-start(bf16[128,1024]{1,0:T(8,128)(2,1)} %get-tuple-element.81) | copy-start | bytes 786436
  48.4 4.0 %collective-permute-start.1 = (bf16[128,128]{1,0:T(8,128)(2,1)S(1)}, bf16[128,128]{1,0:T(8,128)(2,1)S(1)}, u32[]{:S(2)}, u32[]{:S(2)}) collective-permute-start(bf16[128,128]{1,0:T(8,128)(2,1)S(1)} %get-tuple-element.63), channel_id=1, source_target_pairs={{0,1},{1,0},{2,3},{3,2},{4,5},{5,4},{6,7},{7,6},{8,9},{9,8},{10,11... | collective-permute-start | bytes 98312 | tf_op jit(solution)/shard_map/ppermute | solution.py:559
  48.5 4.0 %collective-permute-start.2 = (bf16[128,128]{1,0:T(8,128)(2,1)S(1)}, bf16[128,128]{1,0:T(8,128)(2,1)S(1)}, u32[]{:S(2)}, u32[]{:S(2)}) collective-permute-start(bf16[128,128]{1,0:T(8,128)(2,1)S(1)} %get-tuple-element.64), channel_id=1, source_target_pairs={{0,2},{1,3},{2,0},{3,1},{4,6},{5,7},{6,4},{7,5},{8,10},{9,11},{10,... | collective-permute-start | bytes 98312 | tf_op jit(solution)/shard_map/ppermute | solution.py:559
  49.0 5.3 %collective-permute-start.3 = (bf16[128,128]{1,0:T(8,128)(2,1)S(1)}, bf16[128,128]{1,0:T(8,128)(2,1)S(1)}, u32[]{:S(2)}, u32[]{:S(2)}) collective-permute-start(bf16[128,128]{1,0:T(8,128)(2,1)S(1)} %get-tuple-element.65), channel_id=1, source_target_pairs={{0,3},{1,2},{2,1},{3,0},{4,7},{5,6},{6,5},{7,4},{8,11},{9,10},{10,... | collective-permute-start | bytes 98312 | tf_op jit(solution)/shard_map/ppermute | solution.py:559
  56.4 7.6 %copy-start.5 = (bf16[128,1024]{1,0:T(8,128)(2,1)S(1)}, bf16[128,1024]{1,0:T(8,128)(2,1)}, u32[]{:S(2)}) copy-start(bf16[128,1024]{1,0:T(8,128)(2,1)} %get-tuple-element.80.mid_ref.long_gate_ref) | copy-start | bytes 786436
  56.4 27.3 %all-to-all-start.1 = ((bf16[32,128,128]{2,1,0:T(8,128)(2,1)}), bf16[32,128,128]{2,1,0:T(8,128)(2,1)S(1)}, u32[]{:S(2)}, u32[]{:S(2)}) async-start(bf16[32,128,128]{2,1,0:T(8,128)(2,1)} %bitcast.12), calls=%async_computation.1 | async-start | bytes 2097152 | tf_op jit(solution)/shard_map/all_to_all | solution.py:566
  63.9 17.6 %collective-permute-start.6 = (bf16[128,1024]{1,0:T(8,128)(2,1)S(1)}, bf16[128,1024]{1,0:T(8,128)(2,1)S(1)}, u32[]{:S(2)}, u32[]{:S(2)}) collective-permute-start(bf16[128,1024]{1,0:T(8,128)(2,1)S(1)} %copy-done.18), channel_id=1, source_target_pairs={{0,32},{32,0},{64,96},{96,64},{1,33},{33,1},{65,97},{97,65},{2,34}... | collective-permute-start | bytes 786440 | tf_op jit(solution)/shard_map/ppermute | solution.py:572
  64.0 17.5 %collective-permute-start.5 = (bf16[128,1024]{1,0:T(8,128)(2,1)S(1)}, bf16[128,1024]{1,0:T(8,128)(2,1)S(1)}, u32[]{:S(2)}, u32[]{:S(2)}) collective-permute-start(bf16[128,1024]{1,0:T(8,128)(2,1)S(1)} %copy-done.5), channel_id=1, source_target_pairs={{0,32},{32,0},{64,96},{96,64},{1,33},{33,1},{65,97},{97,65},{2,34}... | collective-permute-start | bytes 786440 | tf_op jit(solution)/shard_map/ppermute | solution.py:572
  64.5 17.1 %copy-start.1 = (bf16[128,1024]{1,0:T(8,128)(2,1)S(1)}, bf16[128,1024]{1,0:T(8,128)(2,1)}, u32[]{:S(2)}) copy-start(bf16[128,1024]{1,0:T(8,128)(2,1)} %get-tuple-element.58.long_xbf_ref.xbf_ref) | copy-start | bytes 786436
  64.5 17.1 %copy-start.6 = (bf16[512,1024]{1,0:T(8,128)(2,1)S(1)}, bf16[512,1024]{1,0:T(8,128)(2,1)}, u32[]{:S(2)}) copy-start(bf16[512,1024]{1,0:T(8,128)(2,1)} %get-tuple-element.86.mine_ref) | copy-start | bytes 3145732
  81.5 33.4 %collective-permute-start.4 = (bf16[512,1024]{1,0:T(8,128)(2,1)}, bf16[512,1024]{1,0:T(8,128)(2,1)}, u32[]{:S(2)}, u32[]{:S(2)}) collective-permute-start(bf16[512,1024]{1,0:T(8,128)(2,1)} %get-tuple-element.79), channel_id=1, source_target_pairs={{0,32},{32,0},{64,96},{96,64},{1,33},{33,1},{65,97},{97,65},{2,34}... | collective-permute-start | bytes 3145736 | tf_op jit(solution)/shard_map/ppermute | solution.py:572
  83.7 1.0 copy-start.17
  84.7 34.3 %all-to-all-start.2 = ((bf16[64,8,1024]{2,1,0:T(8,128)(2,1)}), bf16[64,8,1024]{2,1,0:T(8,128)(2,1)}, u32[]{:S(2)}, u32[]{:S(2)}) async-start(bf16[64,8,1024]{2,1,0:T(8,128)(2,1)} %bitcast.8), calls=%async_computation.2 | async-start | bytes 2097152 | tf_op jit(solution)/shard_map/all_to_all | solution.py:583
  95.4 18.5 %copy-start.12 = (bf16[128,1024]{1,0:T(8,128)(2,1)S(1)}, bf16[128,1024]{1,0:T(8,128)(2,1)}, u32[]{:S(2)}) copy-start(bf16[128,1024]{1,0:T(8,128)(2,1)} %get-tuple-element.93.slope_ref) | copy-start | bytes 786436
  95.4 21.0 %copy-start.9 = (bf16[128,1024]{1,0:T(8,128)(2,1)S(1)}, bf16[128,1024]{1,0:T(8,128)(2,1)}, u32[]{:S(2)}) copy-start(bf16[128,1024]{1,0:T(8,128)(2,1)} %copy-done.8) | copy-start | bytes 786436
  95.4 21.0 %copy-start.11 = (bf16[512,1024]{1,0:T(8,128)(2,1)S(1)}, bf16[512,1024]{1,0:T(8,128)(2,1)}, u32[]{:S(2)}) copy-start(bf16[512,1024]{1,0:T(8,128)(2,1)} %get-tuple-element.78.mine_ref) | copy-start | bytes 3145732
  105.5 6.3 %collective-permute-start.7 = (bf16[128,256]{1,0:T(8,128)(2,1)}, bf16[128,256]{1,0:T(8,128)(2,1)S(1)}, u32[]{:S(2)}, u32[]{:S(2)}) collective-permute-start(bf16[128,256]{1,0:T(8,128)(2,1)} %get-tuple-element.90), channel_id=1, source_target_pairs={{0,1},{1,0},{2,3},{3,2},{4,5},{5,4},{6,7},{7,6},{8,9},{9,8},{10,11... | collective-permute-start | bytes 196616 | tf_op jit(solution)/shard_map/ppermute | solution.py:559
  107.0 4.8 %collective-permute-start.8 = (bf16[128,256]{1,0:T(8,128)(2,1)}, bf16[128,256]{1,0:T(8,128)(2,1)S(1)}, u32[]{:S(2)}, u32[]{:S(2)}) collective-permute-start(bf16[128,256]{1,0:T(8,128)(2,1)} %get-tuple-element.91), channel_id=1, source_target_pairs={{0,2},{1,3},{2,0},{3,1},{4,6},{5,7},{6,4},{7,5},{8,10},{9,11},{10,... | collective-permute-start | bytes 196616 | tf_op jit(solution)/shard_map/ppermute | solution.py:559
  108.5 5.4 %collective-permute-start.9 = (bf16[128,256]{1,0:T(8,128)(2,1)}, bf16[128,256]{1,0:T(8,128)(2,1)S(1)}, u32[]{:S(2)}, u32[]{:S(2)}) collective-permute-start(bf16[128,256]{1,0:T(8,128)(2,1)} %get-tuple-element.92), channel_id=1, source_target_pairs={{0,3},{1,2},{2,1},{3,0},{4,7},{5,6},{6,5},{7,4},{8,11},{9,10},{10,... | collective-permute-start | bytes 196616 | tf_op jit(solution)/shard_map/ppermute | solution.py:559
  114.8 4.2 %copy-start.2 = (bf16[128,1024]{1,0:T(8,128)(2,1)}, bf16[128,1024]{1,0:T(8,128)(2,1)S(1)}, u32[]{:S(2)}) copy-start(bf16[128,1024]{1,0:T(8,128)(2,1)S(1)} %long_slopes.1.grad_ref.long_grad_ref) | copy-start | bytes 786436
  114.8 1.6 %collective-permute-start.10 = (bf16[128,1024]{1,0:T(8,128)(2,1)S(1)}, bf16[128,1024]{1,0:T(8,128)(2,1)S(1)}, u32[]{:S(2)}, u32[]{:S(2)}) collective-permute-start(bf16[128,1024]{1,0:T(8,128)(2,1)S(1)} %long_slopes.1.grad_ref.long_grad_ref), channel_id=1, source_target_pairs={{0,32},{32,0},{64,96},{96,64},{1,33},{33,1},{65,97},{97,65},{2,34}... | collective-permute-start | bytes 786440 | tf_op jit(solution)/shard_map/ppermute | solution.py:572
  119.0 26.8 %all-to-all-start.3 = ((bf16[64,8,1024]{2,1,0:T(8,128)(2,1)}), bf16[64,8,1024]{2,1,0:T(8,128)(2,1)S(1)}, u32[]{:S(2)}, u32[]{:S(2)}) async-start(bf16[64,8,1024]{2,1,0:T(8,128)(2,1)} %bitcast.9), calls=%async_computation.3 | async-start | bytes 2097152 | tf_op jit(solution)/shard_map/all_to_all | solution.py:583
  (2 other events, 1.5 us)
